TPU v7x, 128 devices: a whole 4x4x4 slice. The times are simulated.
128 devices in a mesh: dp: 32 (over z, x, y_hi), mp: 4 (over y_lo, core).
Axes of the slice: x: 4, y: 4 (y_hi: 2, y_lo: 2; y = y_hi * 2 + y_lo), z: 4, core: 2. Of those that a mesh axis runs over, the one named last changes fastest.
Arguments:
- block_input: bfloat16 [12288, 1024], P('dp', 'mp'), may hold values from -6 to 6
- cotangent: bfloat16 [12288, 1024], P('dp', 'mp'), may hold values from -6 to 6
- norm_gain: bfloat16 [1, 2, 1024], P(None, None, 'dp'), may hold values from 0.25 to 1.75
- w_qkv: bfloat16 [1, 1024, 3, 1024], P(None, 'dp', None, 'mp'), may hold values from -0.1875 to 0.1875
- w_out: bfloat16 [1, 1024, 1024], P(None, 'mp', 'dp'), may hold values from -0.75 to 0.75
- w_in: bfloat16 [1, 1024, 2, 2624], P(None, 'dp', None, 'mp'), may hold values from -0.1875 to 0.1875
- w_down: bfloat16 [1, 2624, 1024], P(None, 'mp', 'dp'), may hold values from -0.125 to 0.125
Outputs:
- block_output: bfloat16 [12288, 1024], P('dp', 'mp')
- input_grad: bfloat16 [12288, 1024], P('dp', 'mp')
- gain_grad: float32 [1, 2, 1024], P(None, None, 'dp')
- qkv_grad: float32 [1, 1024, 3, 1024], P(None, 'dp', None, 'mp')
- out_grad: float32 [1, 1024, 1024], P(None, 'mp', 'dp')
- in_grad: float32 [1, 1024, 2, 2624], P(None, 'dp', None, 'mp')
- down_grad: float32 [1, 2624, 1024], P(None, 'mp', 'dp')
All inputs are finite; a program needn't handle non-finite values.
Results may differ from a plain program's by a relative error of at most 0.03.
Values may be sent and summed in bfloat16 or wider, within the bound.
No kernel may reach another device: no remote copies, remote signals or barrier semaphores. Data moves between devices by JAX's collectives and lax.ppermute only.
A program may use at most 128 MiB of HBM per device.

v0:
```python
import functools

import jax
import jax.numpy as jnp
from jax import lax
from jax.experimental import pallas as pl
from jax.experimental.pallas import tpu as pltpu
from jax.sharding import Mesh
from jax.sharding import PartitionSpec as P

HEAD_DIM = 64
REACH = 64
LEN = 2048
EPS = 1e-05
NEG = -1e30
BF = jnp.bfloat16
F32 = jnp.float32
DP = ("z", "x", "yh")

D = 1024
FF = 656
MAIN = 640
TAIL = 16
FFP = 768
VMEM_MB = 56
PACK = 1024 + 384
ROWS = (128, 128, 64, 64)
OWN_AT = (0, 128, 256, 320)
EXT_AT = (0, 256, 512, 704)
OWN = 384
EXT = 896
HALO = 256
NT = (((1,), (1,)), ((), ()))
TN = (((0,), (0,)), ((), ()))


def turn_by(x, axis, by):
    n = lax.axis_size(axis)
    return lax.ppermute(x, axis, [((i + by) % n, i) for i in range(n)])


def sum_of(got, n):
    return jnp.sum(got.reshape(n, got.shape[0] // n, -1).astype(F32), axis=0)


def scatter_sum(x, axis):
    return lax.psum_scatter(x, axis, scatter_dimension=0, tiled=True)


def columns(full, at, width):
    return full, pl.BlockSpec((full.shape[0], width), lambda i: (0, at))


def call(us, body, outs, scratch, *args):
    specs = []
    for a in args:
        if isinstance(a, tuple):
            specs.append(a[1])
        else:
            where = pltpu.SMEM if a.dtype == jnp.int32 else pltpu.VMEM
            specs.append(pl.BlockSpec(memory_space=where))
    return pl.pallas_call(
        body,
        grid=(1,),
        out_shape=[jax.ShapeDtypeStruct(s, t) for s, t in outs],
        in_specs=specs,
        out_specs=[pl.BlockSpec(memory_space=pltpu.VMEM)] * len(outs),
        scratch_shapes=[pltpu.VMEM(s, t) for s, t in scratch],
        cost_estimate=pl.CostEstimate(flops=us * 10**9, bytes_accessed=0, transcendentals=0),
        compiler_params=pltpu.CompilerParams(vmem_limit_bytes=VMEM_MB * 1024 * 1024),
    )(*[a[0] if isinstance(a, tuple) else a for a in args])


def mm(a, b):
    return jnp.dot(a, b, preferred_element_type=F32)


def nt(a, b):
    return lax.dot_general(a, b, NT, preferred_element_type=F32)


def tn(a, b):
    return lax.dot_general(a, b, TN, preferred_element_type=F32)


def block(place, s):
    return pl.ds(pl.multiple_of((place[0] ^ s) * 256, 256), 256)


def enter_kernel(place, x0, x1, x2, x3, xr, own, stats):
    for s in range(4):
        at, x = block(place, s), (x0, x1, x2, x3)[s]
        own[:, at] = x[0:OWN, :]
        for b in range(4):
            e, o, r = EXT_AT[b], OWN_AT[b], ROWS[b]
            xr[e : e + 64, at] = x[OWN + b * 64 : OWN + b * 64 + 64, :]
            xr[e + 64 : e + 64 + r, at] = x[o : o + r, :]
            k = OWN + HALO + b * 64
            xr[e + 64 + r : e + 128 + r, at] = x[k : k + 64, :]

    @pl.loop(0, EXT // 128)
    def _(i):
        rows = pl.ds(pl.multiple_of(i * 128, 128), 128)
        v = xr[rows, :].astype(F32)
        m = jnp.mean(v, axis=1, keepdims=True)
        v = v - m
        r = lax.rsqrt(jnp.mean(v * v, axis=1, keepdims=True) + EPS)
        lane = lax.broadcasted_iota(jnp.int32, (128, 128), 1)
        stats[rows, :] = jnp.where(lane == 0, m, r)


def normalized(x, stats):
    return (x.astype(F32) - stats[:, 0:1]) * stats[:, 1:2]


def own_rows(ref):
    return jnp.concatenate(
        [ref[EXT_AT[b] + REACH : EXT_AT[b] + REACH + ROWS[b], :] for b in range(4)], axis=0
    )


def load_sum(place, half, far, half_c, far_c, full):
    for s in range(4):
        a, b = ((half, far), (half_c, far_c))[s & 1]
        full[:, block(place, s)] = a[s >> 1].astype(F32) + b[1 - (s >> 1)].astype(F32)


def half_turn(v):
    low = (lax.broadcasted_iota(jnp.int32, v.shape, 1) & 63) < 32
    return jnp.where(low, pltpu.roll(v, 96, axis=1), pltpu.roll(v, 32, axis=1))


def window(place, b):
    r = ROWS[b]
    i = lax.broadcasted_iota(jnp.int32, (r, r + 128), 0)
    j = lax.broadcasted_iota(jnp.int32, (r, r + 128), 1)
    begin = (place[1] * r) & (LEN - 1)
    at = j + (begin - REACH)
    return (j >= i) & (j <= i + 128) & (at >= 0) & (at < LEN)


def head_lanes(shape, h):
    return (lax.broadcasted_iota(jnp.int32, shape, 1) >> 6) == h


def only(v, h):
    return jnp.where(head_lanes(v.shape, h), v, jnp.zeros_like(v))


def attend_kernel(
    place, xr, stat, w, cos, sin,
    gains, normed, qo, kx, vx, att, lse, even, odd, wide, nb, raw,
):
    gains[...] = w[:, 1024:1152].astype(F32).T[0:8]
    g = gains[0:1]

    @pl.loop(0, EXT // 128)
    def _(i):
        rows = pl.ds(pl.multiple_of(i * 128, 128), 128)
        nb[rows, :] = (normalized(xr[rows, :], stat[rows, :]) * g).astype(BF)

    for b in range(4):
        e, o, r = EXT_AT[b] + REACH, OWN_AT[b], ROWS[b]
        normed[o : o + r, :] = nb[e : e + r, :]
    for t in range(3):
        into = (wide, kx, vx)[t]
        raw[...] = mm(nb[...], w[:, t * 256 : t * 256 + 256])
        for h in range(2):
            lanes = slice(h * 128, h * 128 + 128)
            v = raw[:, lanes]
            if t < 2:
                v = v * cos[...] + half_turn(v) * sin[...]
            into[:, lanes] = v.astype(BF)
    for b in range(4):
        e, o, r = EXT_AT[b] + REACH, OWN_AT[b], ROWS[b]
        qo[o : o + r, :] = wide[e : e + r, :]
    for b in range(4):
        allowed = window(place, b)
        e, at, r = EXT_AT[b], OWN_AT[b], ROWS[b]
        lane = lax.broadcasted_iota(jnp.int32, (r, 128), 1)
        kept = jnp.zeros((r, 128), F32)
        for t in range(2):
            lanes = slice(t * 128, t * 128 + 128)
            q, k, v = qo[at : at + r, lanes], kx[e : e + r + 128, lanes], vx[e : e + r + 128, lanes]
            o = []
            for h in range(2):
                x = jnp.where(allowed, nt(only(q, h), k) * 0.125, NEG)
                most = jnp.max(x, axis=1, keepdims=True)
                x = jnp.exp(x - most)
                total = jnp.sum(x, axis=1, keepdims=True)
                o.append(mm((x * (1.0 / total)).astype(BF), v))
                kept = jnp.where(lane == t * 2 + h, most + jnp.log(total), kept)
            att[at : at + r, lanes] = jnp.where(head_lanes(o[0].shape, 0), o[0], o[1]).astype(BF)
        lse[at : at + r, :] = kept
    for s in range(4):
        y = nt(att[...], w[block(place, s), 768:1024])
        (even, odd)[s & 1][s >> 1] = y.astype(BF)


def tail_of(tail, k):
    v = tail.astype(F32)
    v = v if k == 0 else pltpu.roll(v, 128 - k * TAIL, axis=1)
    lane = lax.broadcasted_iota(jnp.int32, v.shape, 1)
    return jnp.where(lane < TAIL, v, 0.0).astype(BF)


def mlp_kernel(
    place, xo, half, far, half_c, far_c, gains, w, c0, c1, c2, c3,
    ct, own, xhat, rinv, normed, act, de0, de1, even, odd, gpart,
    w0, w1, wd, stream,
):
    for s in range(4):
        ct[:, block(place, s)] = (c0, c1, c2, c3)[s][...]
    tail = w[:, 3 * MAIN :]
    for k, full in enumerate((w0, w1, wd)):
        full[:, 0:MAIN] = w[:, k * MAIN : k * MAIN + MAIN]
        full[:, MAIN:] = tail_of(tail, k)

    gain = gains[1:2]
    load_sum(place, half, far, half_c, far_c, stream)
    stream[...] += xo[...].astype(F32)
    own[...] = stream[:, block(place, 0)]

    @pl.loop(0, OWN // 128)
    def _(i):
        rows = pl.ds(pl.multiple_of(i * 128, 128), 128)
        v = stream[rows, :]
        v = v - jnp.mean(v, axis=1, keepdims=True)
        r = lax.rsqrt(jnp.mean(v * v, axis=1, keepdims=True) + EPS)
        v = v * r
        xhat[rows, :] = v
        rinv[rows, :] = jnp.broadcast_to(r, (128, 128))
        normed[rows, :] = (v * gain).astype(BF)

    @pl.loop(0, FFP // 256)
    def _(n):
        at = pl.ds(pl.multiple_of(n * 256, 256), 256)
        e0 = mm(normed[...], w0[:, at])
        e1 = mm(normed[...], w1[:, at])
        da = mm(ct[...], wd[:, at])
        cdf = 0.5 * (1.0 + lax.erf(e0 * 0.7071067811865476))
        pdf = jnp.exp(-0.5 * e0 * e0) * 0.3989422804014327
        ge = e0 * cdf
        act[:, at] = (ge * e1).astype(BF)
        de0[:, at] = (da * e1 * (cdf + e0 * pdf)).astype(BF)
        de1[:, at] = (da * ge).astype(BF)

    for s in range(4):
        at = block(place, s)
        y = nt(de0[...], w0[at, :]) + nt(de1[...], w1[at, :])
        (even, odd)[s & 1][s >> 1] = y.astype(BF)
        gpart[:, at] = jnp.sum(y * xhat[:, at], axis=0, keepdims=True)


def mlp_grads_kernel(place, normed, act, de0, de1, ct, wm, wt, down, g, wd):
    wd[:, 0:MAIN] = wm[...]
    wd[:, MAIN:] = tail_of(wt[...], 2)
    for s in range(4):
        down[s] = nt(act[...], wd[block(place, s), :]).astype(BF)
    lane = lax.broadcasted_iota(jnp.int32, (256, 128), 1)
    for k in range(4):
        at = slice(k * 256, k * 256 + 256)
        n, c = normed[:, at], ct[:, at]
        y0, y1, y2 = tn(n, de0[...]), tn(n, de1[...]), tn(c, act[...])
        tail = jnp.zeros((256, 128), F32)
        for t, y in enumerate((y0, y1, y2)):
            end = jnp.where(lane < TAIL, y[:, MAIN:], 0.0)
            tail = tail + (end if t == 0 else pltpu.roll(end, t * TAIL, axis=1))
        for t, y in enumerate((y0, y1, y2)):
            g[at, t * MAIN : t * MAIN + MAIN] = y[:, 0:MAIN].astype(BF)
        g[at, 3 * MAIN :] = tail.astype(BF)


def attend_back_kernel(
    place, half, far, half_c, far_c, ct, xhat, rinv, gains, w, att, qo, kx, vx, lse,
    own, go, dq, dk, dv, below, above,
    grad, gb, da, dk_ext, dv_ext,
):
    gain = gains[1:2]
    load_sum(place, half, far, half_c, far_c, grad)

    @pl.loop(0, OWN // 128)
    def _(i):
        rows = pl.ds(pl.multiple_of(i * 128, 128), 128)
        e = grad[rows, :] * gain
        x = xhat[rows, :]
        m1 = jnp.mean(e, axis=1, keepdims=True)
        m2 = jnp.mean(e * x, axis=1, keepdims=True)
        r = rinv[rows, 0:1]
        g = ct[rows, :].astype(F32) + r * (e - m1 - x * m2)
        grad[rows, :] = g
        gb[rows, :] = g.astype(BF)

    own[...] = grad[:, block(place, 0)]
    da[...] = mm(gb[...], w[...]).astype(BF)
    dk_ext[...] = jnp.zeros_like(dk_ext)
    dv_ext[...] = jnp.zeros_like(dv_ext)
    for b in range(4):
        allowed = window(place, b)
        e, o, r = EXT_AT[b], OWN_AT[b], ROWS[b]
        for t in range(2):
            lanes = slice(t * 128, t * 128 + 128)
            q, k, v = qo[o : o + r, lanes], kx[e : e + r + 128, lanes], vx[e : e + r + 128, lanes]
            d = da[o : o + r, lanes]
            dqs, dks, dvs = [], [], []
            for h in range(2):
                qh, dh = only(q, h), only(d, h)
                total = lse[o : o + r, t * 2 + h : t * 2 + h + 1]
                p = jnp.exp(jnp.where(allowed, nt(qh, k) * 0.125 - total, NEG))
                dp = nt(dh, v)
                ds = (p * (dp - jnp.sum(p * dp, axis=1, keepdims=True))).astype(BF)
                dqs.append(mm(ds, k))
                dks.append(tn(ds, qh))
                dvs.append(tn(p.astype(BF), dh))
            dq[o : o + r, lanes] = jnp.where(head_lanes(dqs[0].shape, 0), dqs[0], dqs[1]) * 0.125
            dk_ext[e : e + r + 128, lanes] = (dks[0] + dks[1]) * 0.125
            dv_ext[e : e + r + 128, lanes] = dvs[0] + dvs[1]
    for b in range(4):
        e, o, r = EXT_AT[b], OWN_AT[b], ROWS[b]
        dk[o : o + r, :] = dk_ext[e + 64 : e + 64 + r, :]
        dv[o : o + r, :] = dv_ext[e + 64 : e + 64 + r, :]
        at = slice(b * 64, b * 64 + 64)
        below[at, 0:256] = dk_ext[e : e + 64, :].astype(BF)
        below[at, 256:512] = dv_ext[e : e + 64, :].astype(BF)
        above[at, 0:256] = dk_ext[e + 64 + r : e + 128 + r, :].astype(BF)
        above[at, 256:512] = dv_ext[e + 64 + r : e + 128 + r, :].astype(BF)
    for k in range(4):
        go[k * 256 : k * 256 + 256, :] = tn(gb[:, k * 256 : k * 256 + 256], att[...]).astype(BF)


def qkv_back_kernel(
    place, dq, dk, dv, low, high, cos, sin, xo, stat, gains, gain2, w,
    dn, pack, xq, raw, gsum,
):
    for b in range(4):
        o, r = OWN_AT[b], ROWS[b]
        at = slice(b * 64, b * 64 + 64)
        dk[o : o + 64, :] += low[at, 0:256].astype(F32)
        dv[o : o + 64, :] += low[at, 256:512].astype(F32)
        dk[o + r - 64 : o + r, :] += high[at, 0:256].astype(F32)
        dv[o + r - 64 : o + r, :] += high[at, 256:512].astype(F32)
    for b in range(4):
        e, o, r = EXT_AT[b] + REACH, OWN_AT[b], ROWS[b]
        c, s = cos[e : e + r, :], sin[e : e + r, :]
        for t in range(2):
            lanes = slice(t * 128, t * 128 + 128)
            v = dq[o : o + r, lanes]
            raw[o : o + r, lanes] = (v * c - half_turn(v) * s).astype(BF)
            v = dk[o : o + r, lanes]
            lanes = slice(256 + t * 128, 256 + t * 128 + 128)
            raw[o : o + r, lanes] = (v * c - half_turn(v) * s).astype(BF)
    raw[:, 512:768] = dv[...].astype(BF)
    st = own_rows(stat)
    m1 = jnp.zeros((OWN, 1), F32)
    m2 = jnp.zeros((OWN, 1), F32)
    for s in range(4):
        at = block(place, s)
        y = nt(raw[...], w[at, :])
        dn[s] = y.astype(BF)
        x = normalized(xo[:, at], st)
        if s == 0:
            xq[...] = x
        e = y * gains[0:1, at]
        m1 = m1 + jnp.sum(e, axis=1, keepdims=True)
        m2 = m2 + jnp.sum(e * x, axis=1, keepdims=True)
        gsum[:, at] = jnp.sum(y * x, axis=0, keepdims=True)
    lane = lax.broadcasted_iota(jnp.int32, (OWN, 128), 1)
    sums = jnp.where(lane == 0, m1, jnp.where(lane == 1, m2, 0.0)) * (1.0 / D)
    pack[:, D:] = sums.T[0:8]
    pack[0:1, 0:D] = gsum[...]
    pack[1:2, 0:D] = gain2[...]


def qkv_grads_kernel(normed, raw, go, p0, p1, p2, p3, g):
    for k in range(4):
        at = slice(k * 256, k * 256 + 256)
        g[at, 0:768] = tn(normed[:, at], raw[...]).astype(BF)
    g[:, 768:1024] = go[...]
    row = lax.broadcasted_iota(jnp.int32, (8, D), 0)
    both = jnp.where(row < 2, p0[:, :D] + p1[:, :D] + p2[:, :D] + p3[:, :D], 0.0)
    g[:, 1024:1152] = jnp.concatenate([both, jnp.zeros((120, D), F32)], axis=0).T.astype(BF)


def leave_kernel(place, grad, own, a, b, c, p0, p1, p2, p3, xq, stat, gains, out):
    sums = p0[:, D:] + p1[:, D:] + p2[:, D:] + p3[:, D:]
    sums = jnp.concatenate([sums, jnp.zeros((120, OWN), F32)], axis=0).T
    m1, m2 = sums[:, 0:1], sums[:, 1:2]
    e = own[0].astype(F32) + a[...].astype(F32) + b[...].astype(F32) + c[...].astype(F32)
    e = e * gains[0:1, block(place, 0)]
    y = grad[...] + own_rows(stat)[:, 1:2] * (e - m1 - xq[...] * m2)
    out[...] = y.astype(BF)


def output_kernel(stream, own, a, b, c, out):
    y = stream[...] + own[0].astype(F32) + a[...].astype(F32)
    out[...] = (y + b[...].astype(F32) + c[...].astype(F32)).astype(BF)


def mp_gather(x):
    far = turn_by(x, "yl", 1)
    return x, turn_by(x, "c", 1), far, turn_by(far, "c", 1)


def mp_turn(x, slot):
    return lax.ppermute(x, ("yl", "c"), [(i, i ^ slot) for i in range(4)])


def mp_terms(slots):
    return [slots, *(mp_turn(slots[s], s) for s in (1, 2, 3))]


def mp_reduce(even, odd):
    return (even.astype(F32) + turn_by(odd, "c", 1).astype(F32)).astype(BF)


def mp_sum(even, odd):
    half = mp_reduce(even, odd)
    far = turn_by(half, "yl", 1)
    return half, far, turn_by(half, "c", 1), turn_by(far, "c", 1)


def dp_turn(x, by):
    pairs = [(i, i + by) for i in range(32) if 0 <= i + by < 32]
    return lax.ppermute(x, ("z", "x", "yh"), pairs)


def rope_tables(place):
    rows = []
    for b in range(4):
        r = ROWS[b]
        rows.append((place * r + jnp.arange(r + 128, dtype=jnp.int32) - REACH) % LEN)
    position = jnp.concatenate(rows).astype(F32)
    frequency = 1.0 / 10000.0 ** (jnp.arange(0, HEAD_DIM, 2, dtype=F32) / HEAD_DIM)
    angles = position[:, None] * frequency[None, :]
    c, s = jnp.cos(angles), jnp.sin(angles)
    return jnp.concatenate([c, c, c, c], axis=1), jnp.concatenate([-s, s, -s, s], axis=1)


def body(block_input, cotangent, norm_gain, w_qkv, w_out, w_in, w_down):
    mp = lax.axis_index("yl") * 2 + lax.axis_index("c")
    dp = (lax.axis_index("z") * 4 + lax.axis_index("x")) * 2 + lax.axis_index("yh")
    place = jnp.stack([mp, dp]).astype(jnp.int32)

    gain_t = jnp.pad(norm_gain[0].T, ((0, 0), (0, 126)))
    shard0 = jnp.concatenate([w_qkv[0].reshape(32, 768), w_out[0].T, gain_t], axis=1)
    in0, in1, down_t = w_in[0, :, 0], w_in[0, :, 1], w_down[0].T
    shard1 = jnp.concatenate(
        [in0[:, :MAIN], in1[:, :MAIN], down_t[:, :MAIN]]
        + [in0[:, MAIN:], in1[:, MAIN:], down_t[:, MAIN:], jnp.zeros((32, 128 - 3 * TAIL), BF)],
        axis=1,
    )
    shard = jnp.concatenate([shard0, shard1], axis=1)
    lows = jnp.concatenate([block_input[o + r - 64 : o + r] for o, r in zip(OWN_AT, ROWS)], axis=0)
    highs = jnp.concatenate([block_input[o : o + 64] for o in OWN_AT], axis=0)
    low, high = dp_turn(lows, 1), dp_turn(highs, -1)
    shard, low, high = lax.optimization_barrier((shard, low, high))
    pair = turn_by(shard, "yh", 1)
    first = lax.axis_index("yh") == 0
    pair = [jnp.where(first, shard, pair), jnp.where(first, pair, shard)]
    pair = jnp.concatenate(pair, axis=0)
    spread = jnp.broadcast_to(pair[None, :, :1152], (16, 64, 1152)).reshape(D, 1152)
    w0 = lax.all_to_all(spread, ("z", "x"), 0, 0, tiled=True)
    w1 = lax.all_gather(pair[:, 1152:], ("z", "x"), axis=0, tiled=True)
    x_slots = mp_gather(jnp.concatenate([block_input, low, high], axis=0))
    cos, sin = rope_tables(dp)

    xr, xo, stat1 = call(
        5, enter_kernel, [((EXT, D), BF), ((OWN, D), BF), ((EXT, 128), F32)], [], place, *x_slots
    )
    xr, cotangent = lax.optimization_barrier((xr, cotangent))
    xr, *c_slots = lax.optimization_barrier((xr, *mp_gather(cotangent)))
    slots = [((2, OWN, 256), BF)] * 2
    gains, normed1, qo, kx, vx, att, lse, *parts = call(
        10,
        attend_kernel,
        [((8, D), F32), ((OWN, D), BF), ((OWN, 256), BF), ((EXT, 256), BF), ((EXT, 256), BF)]
        + [((OWN, 256), BF), ((OWN, 128), F32)] + slots,
        [((EXT, 256), BF), ((EXT, D), BF), ((EXT, 256), F32)],
        place, xr, stat1, w0, cos, sin,
    )
    ct, stream, xhat2, rinv2, normed2, act, de0, de1, even, odd, gain2 = call(
        10,
        mlp_kernel,
        [
            ((OWN, D), BF), ((OWN, 256), F32), ((OWN, D), F32), ((OWN, 128), F32), ((OWN, D), BF),
            ((OWN, FFP), BF), ((OWN, FFP), BF), ((OWN, FFP), BF),
            *slots, ((1, D), F32),
        ],
        [((D, FFP), BF), ((D, FFP), BF), ((D, FFP), BF), ((OWN, D), F32)],
        place, xo, *mp_sum(*parts), gains, w1, *c_slots,
    )
    half = mp_reduce(even, odd)
    far = turn_by(half, "yl", 1)
    half_c = turn_by(half, "c", 1)
    down, g1 = call(
        9,
        mlp_grads_kernel,
        [((4, OWN, 256), BF), ((D, 2048), BF)],
        [((D, FFP), BF)],
        place, normed2, act, de0, de1, ct, columns(w1, 2, MAIN), columns(w1, 15, 128),
    )
    far, down, g1 = lax.optimization_barrier((far, down, g1))
    far_c = turn_by(far, "c", 1)
    g1 = scatter_sum(g1, "z")
    down = mp_terms(down)

    grad, go, dq, dk, dv, below, above = call(
        11,
        attend_back_kernel,
        [((OWN, 256), F32), ((D, 256), BF)] + [((OWN, 256), F32)] * 3 + [((HALO, 512), BF)] * 2,
        [((OWN, D), F32), ((OWN, D), BF), ((OWN, 256), BF), ((EXT, 256), F32), ((EXT, 256), F32)],
        place, half, far, half_c, far_c, ct, xhat2, rinv2, gains, columns(w0, 3, 256),
        att, qo, kx, vx, lse,
    )
    below, above, *down = lax.optimization_barrier((below, above, *down))
    low = dp_turn(above, 1)
    high = dp_turn(below, -1)
    (block_output,) = call(2, output_kernel, [((OWN, 256), BF)], [], stream, *down)
    dn, pack, xq, raw = call(
        7,
        functools.partial(qkv_in_place, qkv_back_kernel),
        [((4, OWN, 256), BF), ((8, PACK), F32), ((OWN, 256), F32), ((OWN, 768), BF)],
        [((OWN, 256), F32), ((OWN, 256), F32), ((1, D), F32)],
        place, dq, dk, dv, low, high, cos, sin, xo, stat1, gains, gain2, columns(w0, 0, 768),
    )
    dn = mp_terms(dn)
    packs = [pack, *(mp_turn(pack, s) for s in (1, 2, 3))]
    raw, g1, *rest = lax.optimization_barrier((raw, g1, *dn, *packs))
    dn, packs = rest[:4], rest[4:]
    g1 = scatter_sum(g1, "x")
    (g0,) = call(4, qkv_grads_kernel, [((D, 1152), BF)], [], normed1, raw, go, *packs)
    g0 = sum_of(lax.all_to_all(g0, DP, 0, 0, tiled=True), 32)
    (input_grad,) = call(
        2, leave_kernel, [((OWN, 256), BF)], [],
        place, grad, *dn, *packs, xq, stat1, gains,
    )
    g1 = jnp.where(first, g1[:32], g1[32:]).astype(F32) + turn_by(
        jnp.where(first, g1[32:], g1[:32]), "yh", 1
    ).astype(F32)
    in0, in1, down_t = [
        jnp.concatenate(
            [g1[:, k * MAIN : k * MAIN + MAIN], g1[:, 3 * MAIN + k * TAIL : 3 * MAIN + k * TAIL + TAIL]],
            axis=1,
        )
        for k in range(3)
    ]
    return (
        block_output, input_grad, g0[:, 1024:1026].T[None], g0[:, :768].reshape(1, 32, 3, 256),
        g0[:, 768:1024].T[None], jnp.stack([in0, in1], axis=1)[None], down_t.T[None],
    )


def qkv_in_place(inner, place, dq, dk, dv, *refs):
    *refs, dks, dvs, gsum = refs
    dks[...] = dk[...]
    dvs[...] = dv[...]
    inner(place, dq, dks, dvs, *refs, gsum)


def solution(mesh):
    fine = Mesh(mesh.devices.reshape(4, 4, 2, 2, 2), ("z", "x", "yh", "yl", "c"))
    dp, mp = ("z", "x", "yh"), ("yl", "c")
    return jax.shard_map(
        body,
        mesh=fine,
        in_specs=(
            P(dp, mp),
            P(dp, mp),
            P(None, None, dp),
            P(None, dp, None, mp),
            P(None, mp, dp),
            P(None, dp, None, mp),
            P(None, mp, dp),
        ),
        out_specs=(
            P(dp, mp),
            P(dp, mp),
            P(None, None, dp),
            P(None, dp, None, mp),
            P(None, mp, dp),
            P(None, dp, None, mp),
            P(None, mp, dp),
        ),
        check_vma=False,
    )
```

profile of v0, /device:TPU:1, one launch (start us, length us, event | category | flops | bytes accessed | tf_op | source)
XLA Modules:
  0.0 250.4 jit_solution(11289550973960418552)
XLA Ops:
  8.9 1.3 collective-permute-start.1
  11.1 6.3 %collective-permute-start = (bf16[256,256]{1,0:T(8,128)(2,1)S(1)}, bf16[256,256]{1,0:T(8,128)(2,1)S(1)}, u32[]{:S(2)}, u32[]{:S(2)}) collective-permute-start(bf16[256,256]{1,0:T(8,128)(2,1)S(1)} %pad_maximum_fusion.4), channel_id=1, source_target_pairs={{0,4},{4,8},{8,12},{12,16},{16,20},{20,24},{24,28},{28,32},{32,36}... | collective-permute-start | bytes 393224 | tf_op jit(solution)/shard_map/ppermute | solution.py:424
  17.4 1.1 fusion.6
  22.6 3.9 %collective-permute-start.8 = (bf16[32,3200]{1,0:T(8,128)(2,1)S(1)}, bf16[32,3200]{1,0:T(8,128)(2,1)S(1)}, u32[]{:S(2)}, u32[]{:S(2)}) collective-permute-start(bf16[32,3200]{1,0:T(8,128)(2,1)S(1)} %concatenate.39), channel_id=1, source_target_pairs={{4,0},{0,4},{5,1},{1,5},{6,2},{2,6},{7,3},{3,7},{12,8},{8,12},{13,... | collective-permute-start | bytes 614408 | tf_op jit(solution)/shard_map/ppermute | solution.py:39
  26.5 7.4 %collective-permute-done.8 = bf16[32,3200]{1,0:T(8,128)(2,1)S(1)} collective-permute-done((bf16[32,3200]{1,0:T(8,128)(2,1)S(1)}, bf16[32,3200]{1,0:T(8,128)(2,1)S(1)}, u32[]{:S(2)}, u32[]{:S(2)}) %collective-permute-start.8) | collective-permute-done | bytes 204832 | tf_op jit(solution)/shard_map/ppermute | solution.py:39
  34.8 1.7 broadcast_in_dim.24
  36.5 6.1 %all-to-all-start = ((bf16[16,64,1152]{2,1,0:T(8,128)(2,1)}), bf16[16,64,1152]{2,1,0:T(8,128)(2,1)S(1)}, u32[]{:S(2)}, u32[]{:S(2)}) async-start(bf16[16,64,1152]{2,1,0:T(8,128)(2,1)} %broadcast_in_dim.24), calls=%async_computation | async-start | bytes 4718592 | tf_op jit(solution)/shard_map/all_to_all | solution.py:462
  43.1 2.9 %collective-permute-start.2 = (bf16[896,256]{1,0:T(8,128)(2,1)S(1)}, bf16[896,256]{1,0:T(8,128)(2,1)}, u32[]{:S(2)}, u32[]{:S(2)}) collective-permute-start(bf16[896,256]{1,0:T(8,128)(2,1)S(1)} %constant_dynamic-update-slice_fusion.x0), channel_id=1, source_target_pairs={{1,0},{0,1},{3,2},{2,3},{5,4},{4,5},{7,6},{6,7},{9,8},{8,9},{11,10... | collective-permute-start | bytes 1376264 | tf_op jit(solution)/shard_map/ppermute | solution.py:39
  46.0 6.3 %collective-permute-done.3.x2 = bf16[896,256]{1,0:T(8,128)(2,1)S(1)} collective-permute-done((bf16[896,256]{1,0:T(8,128)(2,1)S(1)}, bf16[896,256]{1,0:T(8,128)(2,1)S(1)}, u32[]{:S(2)}, u32[]{:S(2)}) %collective-permute-start.3) | collective-permute-done | bytes 458784 | tf_op jit(solution)/shard_map/ppermute | solution.py:39
  52.3 3.4 %collective-permute-start.4 = (bf16[896,256]{1,0:T(8,128)(2,1)S(1)}, bf16[896,256]{1,0:T(8,128)(2,1)}, u32[]{:S(2)}, u32[]{:S(2)}) collective-permute-start(bf16[896,256]{1,0:T(8,128)(2,1)S(1)} %collective-permute-done.3.x2), channel_id=1, source_target_pairs={{1,0},{0,1},{3,2},{2,3},{5,4},{4,5},{7,6},{6,7},{9,8},{8,9},{11,10... | collective-permute-start | bytes 1376264 | tf_op jit(solution)/shard_map/ppermute | solution.py:39
  57.3 4.9 %shard_map.126 = (bf16[896,1024]{1,0:T(8,128)(2,1)}, bf16[384,1024]{1,0:T(8,128)(2,1)}, f32[896,128]{1,0:T(8,128)}) custom-call(s32[2]{0:T(128)} %pad_add_fusion.place, bf16[896,256]{1,0:T(8,128)(2,1)} %copy-done.6, bf16[896,256]{1,0:T(8,128)(2,1)} %collective-permute-done.2.x1, bf16[896,256]{1,0:T(8,128)(2,1)} %copy-done.7, ...), custom_call_target="tpu_custom_call" | custom-call | flops 5000000000 | tf_op jit(solution)/shard_map/pallas_call | solution.py:62
  63.3 5.1 %collective-permute-done.6.c2 = bf16[384,256]{1,0:T(8,128)(2,1)S(1)} collective-permute-done((bf16[384,256]{1,0:T(8,128)(2,1)S(1)}, bf16[384,256]{1,0:T(8,128)(2,1)S(1)}, u32[]{:S(2)}, u32[]{:S(2)}) %collective-permute-start.6) | collective-permute-done | bytes 196640 | tf_op jit(solution)/shard_map/ppermute | solution.py:39
  69.5 1.7 fusion
  71.2 1.7 pad_maximum_fusion
  72.9 2.9 %all-to-all-done = bf16[16,64,1152]{2,1,0:T(8,128)(2,1)S(1)} async-done(((bf16[16,64,1152]{2,1,0:T(8,128)(2,1)}), bf16[16,64,1152]{2,1,0:T(8,128)(2,1)S(1)}, u32[]{:S(2)}, u32[]{:S(2)}) %all-to-all-start) | async-done | bytes 2359328 | tf_op jit(solution)/shard_map/all_to_all | solution.py:462
  75.8 1.4 copy-done
  77.2 12.4 %shard_map.127 = (f32[8,1024]{1,0:T(8,128)}, bf16[384,1024]{1,0:T(8,128)(2,1)}, bf16[384,256]{1,0:T(8,128)(2,1)}, bf16[896,256]{1,0:T(8,128)(2,1)}, bf16[896,256...) custom-call(s32[2]{0:T(128)} %pad_add_fusion.place, ...), custom_call_target="tpu_custom_call" | custom-call | flops 10000000000 | tf_op jit(solution)/shard_map/pallas_call | solution.py:62
  89.6 5.7 %collective-permute-start.9 = (bf16[2,384,256]{2,1,0:T(8,128)(2,1)}, bf16[2,384,256]{2,1,0:T(8,128)(2,1)S(1)}, u32[]{:S(2)}, u32[]{:S(2)}) collective-permute-start(bf16[2,384,256]{2,1,0:T(8,128)(2,1)} %get-tuple-element.82), channel_id=1, source_target_pairs={{1,0},{0,1},{3,2},{2,3},{5,4},{4,5},{7,6},{6,7},{9,8},{8,9},{11,10... | collective-permute-start | bytes 1179656 | tf_op jit(solution)/shard_map/ppermute | solution.py:39
  95.3 1.6 collective-permute-done.9
  96.8 1.1 add_convert_fusion.1.half
  99.1 9.3 %collective-permute-done.10.far = bf16[2,384,256]{2,1,0:T(8,128)(2,1)S(1)} collective-permute-done((bf16[2,384,256]{2,1,0:T(8,128)(2,1)S(1)}, bf16[2,384,256]{2,1,0:T(8,128)(2,1)S(1)}, u32[]{:S(2)}, u32[]{:S(2)}) %collective-permute-start.10) | collective-permute-done | bytes 393248 | tf_op jit(solution)/shard_map/ppermute | solution.py:39
  108.4 1.2 collective-permute-start.12
  109.6 1.3 collective-permute-done.12.far_c
  111.7 10.6 %shard_map.128 = (bf16[384,1024]{1,0:T(8,128)(2,1)}, f32[384,256]{1,0:T(8,128)}, f32[384,1024]{1,0:T(8,128)}, f32[384,128]{1,0:T(8,128)}, bf16[384,1024]{1,0:T(8...) custom-call(s32[2]{0:T(128)} %pad_add_fusion.place, ...), custom_call_target="tpu_custom_call" | custom-call | flops 10000000000 | tf_op jit(solution)/shard_map/pallas_call | solution.py:62
  122.7 1.6 collective-permute-done.13
  124.2 1.1 add_convert_fusion.half
  125.9 8.1 %shard_map.129 = (bf16[4,384,256]{2,1,0:T(8,128)(2,1)}, bf16[1024,2048]{1,0:T(8,128)(2,1)}) custom-call(s32[2]{0:T(128)} %pad_add_fusion.place, bf16[384,1024]{1,0:T(8,128)(2,1)} %get-tuple-element.91.normed, bf16[384,768]{1,0:T(8,128)(2,1)} %get-tuple-element.92.act, bf16[384,768]{1,0:T(8,128)(2,1)} %get-tuple-element.93.de0, ...), custom_call_target="tpu_custom_call" | custom-call | flops 8999999488 | tf_op jit(solution)/shard_map/pallas_call | solution.py:62
  133.9 1.8 collective-permute-done.14.far
  135.9 1.3 collective-permute-start.15
  138.2 1.3 collective-permute-start.19
  140.4 11.6 %shard_map.130 = (f32[384,256]{1,0:T(8,128)}, bf16[1024,256]{1,0:T(8,128)(2,1)}, f32[384,256]{1,0:T(8,128)}, f32[384,256]{1,0:T(8,128)}, f32[384,256]{1,0:T(8,12...) custom-call(s32[2]{0:T(128)} %pad_add_fusion.place, bf16[2,384,256]{2,1,0:T(8,128)(2,1)} %copy-done.4, ...), custom_call_target="tpu_custom_call" | custom-call | flops 11000000512 | tf_op jit(solution)/shard_map/pallas_call | solution.py:62
  152.1 4.8 %collective-permute-start.20 = (bf16[256,512]{1,0:T(8,128)(2,1)}, bf16[256,512]{1,0:T(8,128)(2,1)S(1)}, u32[]{:S(2)}, u32[]{:S(2)}) collective-permute-start(bf16[256,512]{1,0:T(8,128)(2,1)} %get-tuple-element.117), channel_id=1, source_target_pairs={{0,4},{4,8},{8,12},{12,16},{16,20},{20,24},{24,28},{28,32},{32,36}... | collective-permute-start | bytes 786440 | tf_op jit(solution)/shard_map/ppermute | solution.py:424
  156.9 1.3 collective-permute-start.21
  158.2 10.3 %collective-permute-done.20.refs_0_ = bf16[256,512]{1,0:T(8,128)(2,1)S(1)} collective-permute-done((bf16[256,512]{1,0:T(8,128)(2,1)}, bf16[256,512]{1,0:T(8,128)(2,1)S(1)}, u32[]{:S(2)}, u32[]{:S(2)}) %collective-permute-start.20) | collective-permute-done | bytes 262176 | tf_op jit(solution)/shard_map/ppermute | solution.py:424
  168.6 1.5 collective-permute-done.21.refs_1_
  170.8 5.1 %shard_map.132 = (bf16[4,384,256]{2,1,0:T(8,128)(2,1)}, f32[8,1408]{1,0:T(8,128)}, f32[384,256]{1,0:T(8,128)}, bf16[384,768]{1,0:T(8,128)(2,1)}) custom-call(s32[2]{0:T(128)} %pad_add_fusion.place, f32[384,256]{1,0:T(8,128)} %get-tuple-element.114.dq, f32[384,256]{1,0:T(8,128)} %get-tuple-element.115.dk, f32[384,256]{1,0:T(8,128)} %get-tuple-element.116.dv, ...), custom_call_target="tpu_custom_call" | custom-call | flops 7000000000 | tf_op jit(solution)/shard_map/pallas_call | solution.py:62
  175.9 1.2 slice_bitcast_fusion
  178.0 1.5 collective-permute-start.24
  181.6 7.8 %collective-permute-done.26.p2 = f32[8,1408]{1,0:T(8,128)S(1)} collective-permute-done((f32[8,1408]{1,0:T(8,128)}, f32[8,1408]{1,0:T(8,128)S(1)}, u32[]{:S(2)}, u32[]{:S(2)}) %collective-permute-start.26) | collective-permute-done | bytes 45088 | tf_op jit(solution)/shard_map/ppermute | solution.py:405
  189.3 1.1 collective-permute-done.27.p3
  191.1 3.9 %shard_map.134 = bf16[1024,1152]{1,0:T(8,128)(2,1)} custom-call(bf16[384,1024]{1,0:T(8,128)(2,1)} %get-tuple-element.133.normed, bf16[384,768]{1,0:T(8,128)(2,1)} %get-tuple-element.134.raw, bf16[1024,256]{1,0:T(8,128)(2,1)} %get-tuple-element.135.go, f32[8,1408]{1,0:T(8,128)} %get-tuple-element.128.p0, f32[8,1408]{1,0:T(8,128)} %copy-done.26, ...), custom_call_target="tpu_custom_call" | custom-call | flops 4000000000 | tf_op jit(solution)/shard_map/pallas_call | solution.py:62
  195.0 6.6 %all-to-all-start.1 = ((bf16[32,32,1152]{2,1,0:T(8,128)(2,1)}), bf16[32,32,1152]{2,1,0:T(8,128)(2,1)S(1)}, u32[]{:S(2)}, u32[]{:S(2)}) async-start(bf16[32,32,1152]{2,1,0:T(8,128)(2,1)} %bitcast.51), calls=%async_computation.2 | async-start | bytes 4718592 | tf_op jit(solution)/shard_map/all_to_all | solution.py:532
  201.6 2.2 shard_map.131
  203.8 11.5 %reduce-scatter.5.cloned.1.call-done = bf16[64,2048]{1,0:T(8,128)(2,1)} async-done(((bf16[256,2048]{1,0:T(8,128)(2,1)}), bf16[64,2048]{1,0:T(8,128)(2,1)}) %reduce-scatter.5.cloned.1.call-update) | async-done | bytes 262160 | tf_op jit(solution)/shard_map/reduce_scatter | solution.py:47
  216.2 5.3 %collective-permute-start.28 = (bf16[32,2048]{1,0:T(8,128)(2,1)S(1)}, bf16[32,2048]{1,0:T(8,128)(2,1)S(1)}, u32[]{:S(2)}, u32[]{:S(2)}) collective-permute-start(bf16[32,2048]{1,0:T(8,128)(2,1)S(1)} %broadcast_select_fusion.2), channel_id=1, source_target_pairs={{4,0},{0,4},{5,1},{1,5},{6,2},{2,6},{7,3},{3,7},{12,8},{8,12},{13,... | collective-permute-start | bytes 393224 | tf_op jit(solution)/shard_map/ppermute | solution.py:39
  221.5 2.8 %shard_map.133 = bf16[384,256]{1,0:T(8,128)(2,1)} custom-call(s32[2]{0:T(128)} %pad_add_fusion.place, f32[384,256]{1,0:T(8,128)} %get-tuple-element.113.grad, bf16[4,384,256]{2,1,0:T(8,128)(2,1)} %get-tuple-element.124.own, bf16[384,256]{1,0:T(8,128)(2,1)} %copy-done.22, bf16[384,256]{1,0:T(8,128)(2,1)} %copy-done.24, bf16[384,256]{1,0:T(8,128)(2,1)} %copy-done.25, ...), custom_call_target="tpu_custom_call" | custom-call | flops 2000000000 | tf_op jit(solution)/shard_map/pallas_call | solution.py:62
  224.4 1.6 collective-permute-done.28
  227.7 13.9 %all-to-all-done.1 = bf16[32,32,1152]{2,1,0:T(8,128)(2,1)S(1)} async-done(((bf16[32,32,1152]{2,1,0:T(8,128)(2,1)}), bf16[32,32,1152]{2,1,0:T(8,128)(2,1)S(1)}, u32[]{:S(2)}, u32[]{:S(2)}) %all-to-all-start.1) | async-done | bytes 2359328 | tf_op jit(solution)/shard_map/all_to_all | solution.py:532
  (143 shorter events, 25.8 us)
Async XLA Ops:
  7.2 27.5 %copy-start.1 = (bf16[384,256]{1,0:T(8,128)(2,1)S(1)}, bf16[384,256]{1,0:T(8,128)(2,1)}, u32[]{:S(2)}) copy-start(bf16[384,256]{1,0:T(8,128)(2,1)} %param.7) | copy-start | bytes 589828
  7.2 103.7 %all-gather.2.cloned.1.call-start = ((), (), s32[]{:S(2)}) async-start(), calls=%async_computation.4 | async-start | bytes 4456448 | tf_op jit(solution)/shard_map/all_gather | solution.py:463
  8.9 13.7 %collective-permute-start.1 = (bf16[256,256]{1,0:T(8,128)(2,1)S(1)}, bf16[256,256]{1,0:T(8,128)(2,1)S(1)}, u32[]{:S(2)}, u32[]{:S(2)}) collective-permute-start(bf16[256,256]{1,0:T(8,128)(2,1)S(1)} %pad_maximum_fusion.5), channel_id=1, source_target_pairs={{4,0},{8,4},{12,8},{16,12},{20,16},{24,20},{28,24},{32,28},{36,32}... | collective-permute-start | bytes 393224 | tf_op jit(solution)/shard_map/ppermute | solution.py:424
  11.1 11.4 %collective-permute-start = (bf16[256,256]{1,0:T(8,128)(2,1)S(1)}, bf16[256,256]{1,0:T(8,128)(2,1)S(1)}, u32[]{:S(2)}, u32[]{:S(2)}) collective-permute-start(bf16[256,256]{1,0:T(8,128)(2,1)S(1)} %pad_maximum_fusion.4), channel_id=1, source_target_pairs={{0,4},{4,8},{8,12},{12,16},{16,20},{20,24},{24,28},{28,32},{32,36}... | collective-permute-start | bytes 393224 | tf_op jit(solution)/shard_map/ppermute | solution.py:424
  22.6 11.3 %collective-permute-start.8 = (bf16[32,3200]{1,0:T(8,128)(2,1)S(1)}, bf16[32,3200]{1,0:T(8,128)(2,1)S(1)}, u32[]{:S(2)}, u32[]{:S(2)}) collective-permute-start(bf16[32,3200]{1,0:T(8,128)(2,1)S(1)} %concatenate.39), channel_id=1, source_target_pairs={{4,0},{0,4},{5,1},{1,5},{6,2},{2,6},{7,3},{3,7},{12,8},{8,12},{13,... | collective-permute-start | bytes 614408 | tf_op jit(solution)/shard_map/ppermute | solution.py:39
  36.5 39.3 %all-to-all-start = ((bf16[16,64,1152]{2,1,0:T(8,128)(2,1)}), bf16[16,64,1152]{2,1,0:T(8,128)(2,1)S(1)}, u32[]{:S(2)}, u32[]{:S(2)}) async-start(bf16[16,64,1152]{2,1,0:T(8,128)(2,1)} %broadcast_in_dim.24), calls=%async_computation | async-start | bytes 4718592 | tf_op jit(solution)/shard_map/all_to_all | solution.py:462
  42.6 148.0 %reduce-scatter.3.cloned.1.call-start = ((), (), s32[]{:S(2)}) async-start(), calls=%async_computation.5 | async-start | bytes 5242880 | tf_op jit(solution)/shard_map/reduce_scatter | solution.py:47
  42.7 14.6 %copy-start.6 = (bf16[896,256]{1,0:T(8,128)(2,1)}, bf16[896,256]{1,0:T(8,128)(2,1)S(1)}, u32[]{:S(2)}) copy-start(bf16[896,256]{1,0:T(8,128)(2,1)S(1)} %constant_dynamic-update-slice_fusion.x0) | copy-start | bytes 1376260
  42.7 9.6 %collective-permute-start.3 = (bf16[896,256]{1,0:T(8,128)(2,1)S(1)}, bf16[896,256]{1,0:T(8,128)(2,1)S(1)}, u32[]{:S(2)}, u32[]{:S(2)}) collective-permute-start(bf16[896,256]{1,0:T(8,128)(2,1)S(1)} %constant_dynamic-update-slice_fusion.x0), channel_id=1, source_target_pairs={{2,0},{0,2},{3,1},{1,3},{6,4},{4,6},{7,5},{5,7},{10,8},{8,10},{11,... | collective-permute-start | bytes 1376264 | tf_op jit(solution)/shard_map/ppermute | solution.py:39
  43.1 13.2 %collective-permute-start.2 = (bf16[896,256]{1,0:T(8,128)(2,1)S(1)}, bf16[896,256]{1,0:T(8,128)(2,1)}, u32[]{:S(2)}, u32[]{:S(2)}) collective-permute-start(bf16[896,256]{1,0:T(8,128)(2,1)S(1)} %constant_dynamic-update-slice_fusion.x0), channel_id=1, source_target_pairs={{1,0},{0,1},{3,2},{2,3},{5,4},{4,5},{7,6},{6,7},{9,8},{8,9},{11,10... | collective-permute-start | bytes 1376264 | tf_op jit(solution)/shard_map/ppermute | solution.py:39
  52.3 5.0 %copy-start.7 = (bf16[896,256]{1,0:T(8,128)(2,1)}, bf16[896,256]{1,0:T(8,128)(2,1)S(1)}, u32[]{:S(2)}) copy-start(bf16[896,256]{1,0:T(8,128)(2,1)S(1)} %collective-permute-done.3.x2) | copy-start | bytes 1376260
  52.3 5.0 %collective-permute-start.4 = (bf16[896,256]{1,0:T(8,128)(2,1)S(1)}, bf16[896,256]{1,0:T(8,128)(2,1)}, u32[]{:S(2)}, u32[]{:S(2)}) collective-permute-start(bf16[896,256]{1,0:T(8,128)(2,1)S(1)} %collective-permute-done.3.x2), channel_id=1, source_target_pairs={{1,0},{0,1},{3,2},{2,3},{5,4},{4,5},{7,6},{6,7},{9,8},{8,9},{11,10... | collective-permute-start | bytes 1376264 | tf_op jit(solution)/shard_map/ppermute | solution.py:39
  56.3 5.9 %copy-start.16 = (bf16[384,256]{1,0:T(8,128)(2,1)S(1)}, bf16[384,256]{1,0:T(8,128)(2,1)}, u32[]{:S(2)}) copy-start(bf16[384,256]{1,0:T(8,128)(2,1)} %c0) | copy-start | bytes 589828
  62.2 6.2 %collective-permute-start.6 = (bf16[384,256]{1,0:T(8,128)(2,1)S(1)}, bf16[384,256]{1,0:T(8,128)(2,1)S(1)}, u32[]{:S(2)}, u32[]{:S(2)}) collective-permute-start(bf16[384,256]{1,0:T(8,128)(2,1)S(1)} %copy-done.16), channel_id=1, source_target_pairs={{2,0},{0,2},{3,1},{1,3},{6,4},{4,6},{7,5},{5,7},{10,8},{8,10},{11,... | collective-permute-start | bytes 589832 | tf_op jit(solution)/shard_map/ppermute | solution.py:39
  62.7 10.2 %collective-permute-start.5 = (bf16[384,256]{1,0:T(8,128)(2,1)S(1)}, bf16[384,256]{1,0:T(8,128)(2,1)S(1)}, u32[]{:S(2)}, u32[]{:S(2)}) collective-permute-start(bf16[384,256]{1,0:T(8,128)(2,1)S(1)} %copy-done.16), channel_id=1, source_target_pairs={{1,0},{0,1},{3,2},{2,3},{5,4},{4,5},{7,6},{6,7},{9,8},{8,9},{11,10... | collective-permute-start | bytes 589832 | tf_op jit(solution)/shard_map/ppermute | solution.py:39
  68.4 21.2 %copy-start.20 = (bf16[384,256]{1,0:T(8,128)(2,1)}, bf16[384,256]{1,0:T(8,128)(2,1)S(1)}, u32[]{:S(2)}) copy-start(bf16[384,256]{1,0:T(8,128)(2,1)S(1)} %collective-permute-done.6.c2) | copy-start | bytes 589828
  68.4 4.5 %collective-permute-start.7 = (bf16[384,256]{1,0:T(8,128)(2,1)S(1)}, bf16[384,256]{1,0:T(8,128)(2,1)S(1)}, u32[]{:S(2)}, u32[]{:S(2)}) collective-permute-start(bf16[384,256]{1,0:T(8,128)(2,1)S(1)} %collective-permute-done.6.c2), channel_id=1, source_target_pairs={{1,0},{0,1},{3,2},{2,3},{5,4},{4,5},{7,6},{6,7},{9,8},{8,9},{11,10... | collective-permute-start | bytes 589832 | tf_op jit(solution)/shard_map/ppermute | solution.py:39
  72.9 16.7 %copy-start.21 = (bf16[384,256]{1,0:T(8,128)(2,1)}, bf16[384,256]{1,0:T(8,128)(2,1)S(1)}, u32[]{:S(2)}) copy-start(bf16[384,256]{1,0:T(8,128)(2,1)S(1)} %collective-permute-done.5.c1) | copy-start | bytes 589828
  72.9 16.7 %copy-start.23 = (bf16[384,256]{1,0:T(8,128)(2,1)}, bf16[384,256]{1,0:T(8,128)(2,1)S(1)}, u32[]{:S(2)}) copy-start(bf16[384,256]{1,0:T(8,128)(2,1)S(1)} %collective-permute-done.7.c3) | copy-start | bytes 589828
  89.6 7.2 %collective-permute-start.9 = (bf16[2,384,256]{2,1,0:T(8,128)(2,1)}, bf16[2,384,256]{2,1,0:T(8,128)(2,1)S(1)}, u32[]{:S(2)}, u32[]{:S(2)}) collective-permute-start(bf16[2,384,256]{2,1,0:T(8,128)(2,1)} %get-tuple-element.82), channel_id=1, source_target_pairs={{1,0},{0,1},{3,2},{2,3},{5,4},{4,5},{7,6},{6,7},{9,8},{8,9},{11,10... | collective-permute-start | bytes 1179656 | tf_op jit(solution)/shard_map/ppermute | solution.py:39
  97.9 13.0 %copy-start.5 = (bf16[2,384,256]{2,1,0:T(8,128)(2,1)}, bf16[2,384,256]{2,1,0:T(8,128)(2,1)S(1)}, u32[]{:S(2)}) copy-start(bf16[2,384,256]{2,1,0:T(8,128)(2,1)S(1)} %add_convert_fusion.1.half) | copy-start | bytes 1179652
  98.0 10.4 %collective-permute-start.10 = (bf16[2,384,256]{2,1,0:T(8,128)(2,1)S(1)}, bf16[2,384,256]{2,1,0:T(8,128)(2,1)S(1)}, u32[]{:S(2)}, u32[]{:S(2)}) collective-permute-start(bf16[2,384,256]{2,1,0:T(8,128)(2,1)S(1)} %add_convert_fusion.1.half), channel_id=1, source_target_pairs={{2,0},{0,2},{3,1},{1,3},{6,4},{4,6},{7,5},{5,7},{10,8},{8,10},{11,... | collective-permute-start | bytes 1179656 | tf_op jit(solution)/shard_map/ppermute | solution.py:39
  98.4 11.1 %collective-permute-start.11 = (bf16[2,384,256]{2,1,0:T(8,128)(2,1)S(1)}, bf16[2,384,256]{2,1,0:T(8,128)(2,1)S(1)}, u32[]{:S(2)}, u32[]{:S(2)}) collective-permute-start(bf16[2,384,256]{2,1,0:T(8,128)(2,1)S(1)} %add_convert_fusion.1.half), channel_id=1, source_target_pairs={{1,0},{0,1},{3,2},{2,3},{5,4},{4,5},{7,6},{6,7},{9,8},{8,9},{11,10... | collective-permute-start | bytes 1179656 | tf_op jit(solution)/shard_map/ppermute | solution.py:39
  108.4 2.6 %collective-permute-start.12 = (bf16[2,384,256]{2,1,0:T(8,128)(2,1)S(1)}, bf16[2,384,256]{2,1,0:T(8,128)(2,1)S(1)}, u32[]{:S(2)}, u32[]{:S(2)}) collective-permute-start(bf16[2,384,256]{2,1,0:T(8,128)(2,1)S(1)} %collective-permute-done.10.far), channel_id=1, source_target_pairs={{1,0},{0,1},{3,2},{2,3},{5,4},{4,5},{7,6},{6,7},{9,8},{8,9},{11,10... | collective-permute-start | bytes 1179656 | tf_op jit(solution)/shard_map/ppermute | solution.py:39
  122.3 1.9 collective-permute-start.13
  125.4 10.5 %copy-start.4 = (bf16[2,384,256]{2,1,0:T(8,128)(2,1)}, bf16[2,384,256]{2,1,0:T(8,128)(2,1)S(1)}, u32[]{:S(2)}) copy-start(bf16[2,384,256]{2,1,0:T(8,128)(2,1)S(1)} %add_convert_fusion.half) | copy-start | bytes 1179652
  125.4 10.4 %collective-permute-start.14 = (bf16[2,384,256]{2,1,0:T(8,128)(2,1)S(1)}, bf16[2,384,256]{2,1,0:T(8,128)(2,1)S(1)}, u32[]{:S(2)}, u32[]{:S(2)}) collective-permute-start(bf16[2,384,256]{2,1,0:T(8,128)(2,1)S(1)} %add_convert_fusion.half), channel_id=1, source_target_pairs={{2,0},{0,2},{3,1},{1,3},{6,4},{4,6},{7,5},{5,7},{10,8},{8,10},{11,... | collective-permute-start | bytes 1179656 | tf_op jit(solution)/shard_map/ppermute | solution.py:39
  135.8 79.5 %reduce-scatter.5.cloned.1.call-start = ((), (), s32[]{:S(2)}) async-start(), calls=%async_computation.6 | async-start | bytes 1310720 | tf_op jit(solution)/shard_map/reduce_scatter | solution.py:47
  135.9 3.7 %collective-permute-start.15 = (bf16[2,384,256]{2,1,0:T(8,128)(2,1)S(1)}, bf16[2,384,256]{2,1,0:T(8,128)(2,1)S(1)}, u32[]{:S(2)}, u32[]{:S(2)}) collective-permute-start(bf16[2,384,256]{2,1,0:T(8,128)(2,1)S(1)} %add_convert_fusion.half), channel_id=1, source_target_pairs={{1,0},{0,1},{3,2},{2,3},{5,4},{4,5},{7,6},{6,7},{9,8},{8,9},{11,10... | collective-permute-start | bytes 1179656 | tf_op jit(solution)/shard_map/ppermute | solution.py:39
  137.1 2.4 collective-permute-start.16
  137.3 14.7 %collective-permute-start.17 = (bf16[384,256]{1,0:T(8,128)(2,1)S(1)}, bf16[384,256]{1,0:T(8,128)(2,1)S(1)}, u32[]{:S(2)}, u32[]{:S(2)}) collective-permute-start(bf16[384,256]{1,0:T(8,128)(2,1)S(1)} %get-tuple-element.163), channel_id=1, source_target_pairs={{0,1},{1,0},{2,3},{3,2},{4,5},{5,4},{6,7},{7,6},{8,9},{9,8},{10,11... | collective-permute-start | bytes 589832 | tf_op jit(solution)/shard_map/ppermute | solution.py:405
  137.8 14.3 %collective-permute-start.18 = (bf16[384,256]{1,0:T(8,128)(2,1)S(1)}, bf16[384,256]{1,0:T(8,128)(2,1)S(1)}, u32[]{:S(2)}, u32[]{:S(2)}) collective-permute-start(bf16[384,256]{1,0:T(8,128)(2,1)S(1)} %get-tuple-element.162), channel_id=1, source_target_pairs={{0,2},{1,3},{2,0},{3,1},{4,6},{5,7},{6,4},{7,5},{8,10},{9,11},{10,... | collective-permute-start | bytes 589832 | tf_op jit(solution)/shard_map/ppermute | solution.py:405
  138.2 13.9 %collective-permute-start.19 = (bf16[384,256]{1,0:T(8,128)(2,1)S(1)}, bf16[384,256]{1,0:T(8,128)(2,1)S(1)}, u32[]{:S(2)}, u32[]{:S(2)}) collective-permute-start(bf16[384,256]{1,0:T(8,128)(2,1)S(1)} %get-tuple-element.161), channel_id=1, source_target_pairs={{0,3},{1,2},{2,1},{3,0},{4,7},{5,6},{6,5},{7,4},{8,11},{9,10},{10,... | collective-permute-start | bytes 589832 | tf_op jit(solution)/shard_map/ppermute | solution.py:405
  152.0 23.8 %copy-start.17 = (bf16[384,256]{1,0:T(8,128)(2,1)}, bf16[384,256]{1,0:T(8,128)(2,1)S(1)}, u32[]{:S(2)}) copy-start(bf16[384,256]{1,0:T(8,128)(2,1)S(1)} %collective-permute-done.17.a) | copy-start | bytes 589828
  152.1 23.8 %copy-start.18 = (bf16[384,256]{1,0:T(8,128)(2,1)}, bf16[384,256]{1,0:T(8,128)(2,1)S(1)}, u32[]{:S(2)}) copy-start(bf16[384,256]{1,0:T(8,128)(2,1)S(1)} %collective-permute-done.18.b) | copy-start | bytes 589828
  152.1 23.8 %copy-start.19 = (bf16[384,256]{1,0:T(8,128)(2,1)}, bf16[384,256]{1,0:T(8,128)(2,1)S(1)}, u32[]{:S(2)}) copy-start(bf16[384,256]{1,0:T(8,128)(2,1)S(1)} %collective-permute-done.19.c) | copy-start | bytes 589828
  152.1 16.5 %collective-permute-start.20 = (bf16[256,512]{1,0:T(8,128)(2,1)}, bf16[256,512]{1,0:T(8,128)(2,1)S(1)}, u32[]{:S(2)}, u32[]{:S(2)}) collective-permute-start(bf16[256,512]{1,0:T(8,128)(2,1)} %get-tuple-element.117), channel_id=1, source_target_pairs={{0,4},{4,8},{8,12},{12,16},{16,20},{20,24},{24,28},{28,32},{32,36}... | collective-permute-start | bytes 786440 | tf_op jit(solution)/shard_map/ppermute | solution.py:424
  156.9 13.1 %collective-permute-start.21 = (bf16[256,512]{1,0:T(8,128)(2,1)}, bf16[256,512]{1,0:T(8,128)(2,1)S(1)}, u32[]{:S(2)}, u32[]{:S(2)}) collective-permute-start(bf16[256,512]{1,0:T(8,128)(2,1)} %get-tuple-element.118), channel_id=1, source_target_pairs={{4,0},{8,4},{12,8},{16,12},{20,16},{24,20},{28,24},{32,28},{36,32}... | collective-permute-start | bytes 786440 | tf_op jit(solution)/shard_map/ppermute | solution.py:424
  177.1 13.4 %collective-permute-start.22 = (bf16[384,256]{1,0:T(8,128)(2,1)S(1)}, bf16[384,256]{1,0:T(8,128)(2,1)S(1)}, u32[]{:S(2)}, u32[]{:S(2)}) collective-permute-start(bf16[384,256]{1,0:T(8,128)(2,1)S(1)} %get-tuple-element.160), channel_id=1, source_target_pairs={{0,1},{1,0},{2,3},{3,2},{4,5},{5,4},{6,7},{7,6},{8,9},{9,8},{10,11... | collective-permute-start | bytes 589832 | tf_op jit(solution)/shard_map/ppermute | solution.py:405
  177.7 12.8 %collective-permute-start.23 = (bf16[384,256]{1,0:T(8,128)(2,1)S(1)}, bf16[384,256]{1,0:T(8,128)(2,1)S(1)}, u32[]{:S(2)}, u32[]{:S(2)}) collective-permute-start(bf16[384,256]{1,0:T(8,128)(2,1)S(1)} %get-tuple-element.159), channel_id=1, source_target_pairs={{0,2},{1,3},{2,0},{3,1},{4,6},{5,7},{6,4},{7,5},{8,10},{9,11},{10,... | collective-permute-start | bytes 589832 | tf_op jit(solution)/shard_map/ppermute | solution.py:405
  178.0 12.5 %collective-permute-start.24 = (bf16[384,256]{1,0:T(8,128)(2,1)S(1)}, bf16[384,256]{1,0:T(8,128)(2,1)S(1)}, u32[]{:S(2)}, u32[]{:S(2)}) collective-permute-start(bf16[384,256]{1,0:T(8,128)(2,1)S(1)} %get-tuple-element.158), channel_id=1, source_target_pairs={{0,3},{1,2},{2,1},{3,0},{4,7},{5,6},{6,5},{7,4},{8,11},{9,10},{10,... | collective-permute-start | bytes 589832 | tf_op jit(solution)/shard_map/ppermute | solution.py:405
  179.4 1.4 collective-permute-start.25
  179.6 9.8 %collective-permute-start.26 = (f32[8,1408]{1,0:T(8,128)}, f32[8,1408]{1,0:T(8,128)S(1)}, u32[]{:S(2)}, u32[]{:S(2)}) collective-permute-start(f32[8,1408]{1,0:T(8,128)} %get-tuple-element.128.p0), channel_id=1, source_target_pairs={{0,2},{1,3},{2,0},{3,1},{4,6},{5,7},{6,4},{7,5},{8,10},{9,11},{10,... | collective-permute-start | bytes 135176 | tf_op jit(solution)/shard_map/ppermute | solution.py:405
  180.9 9.7 %copy-start.26 = (f32[8,1408]{1,0:T(8,128)}, f32[8,1408]{1,0:T(8,128)S(1)}, u32[]{:S(2)}) copy-start(f32[8,1408]{1,0:T(8,128)S(1)} %collective-permute-done.25.p1) | copy-start | bytes 135172
  180.9 9.6 %collective-permute-start.27 = (f32[8,1408]{1,0:T(8,128)}, f32[8,1408]{1,0:T(8,128)S(1)}, u32[]{:S(2)}, u32[]{:S(2)}) collective-permute-start(f32[8,1408]{1,0:T(8,128)} %get-tuple-element.128.p0), channel_id=1, source_target_pairs={{0,3},{1,2},{2,1},{3,0},{4,7},{5,6},{6,5},{7,4},{8,11},{9,10},{10,... | collective-permute-start | bytes 135176 | tf_op jit(solution)/shard_map/ppermute | solution.py:405
  190.5 4.5 %copy-start.22 = (bf16[384,256]{1,0:T(8,128)(2,1)}, bf16[384,256]{1,0:T(8,128)(2,1)S(1)}, u32[]{:S(2)}) copy-start(bf16[384,256]{1,0:T(8,128)(2,1)S(1)} %collective-permute-done.22.a) | copy-start | bytes 589828
  195.0 46.6 %all-to-all-start.1 = ((bf16[32,32,1152]{2,1,0:T(8,128)(2,1)}), bf16[32,32,1152]{2,1,0:T(8,128)(2,1)S(1)}, u32[]{:S(2)}, u32[]{:S(2)}) async-start(bf16[32,32,1152]{2,1,0:T(8,128)(2,1)} %bitcast.51), calls=%async_computation.2 | async-start | bytes 4718592 | tf_op jit(solution)/shard_map/all_to_all | solution.py:532
  216.2 9.8 %collective-permute-start.28 = (bf16[32,2048]{1,0:T(8,128)(2,1)S(1)}, bf16[32,2048]{1,0:T(8,128)(2,1)S(1)}, u32[]{:S(2)}, u32[]{:S(2)}) collective-permute-start(bf16[32,2048]{1,0:T(8,128)(2,1)S(1)} %broadcast_select_fusion.2), channel_id=1, source_target_pairs={{4,0},{0,4},{5,1},{1,5},{6,2},{2,6},{7,3},{3,7},{12,8},{8,12},{13,... | collective-permute-start | bytes 393224 | tf_op jit(solution)/shard_map/ppermute | solution.py:39
  (15 other events, 30.1 us)
Sparse Core Ops, SparseCore 0:
  34.8 70.5 all-gather.1
  135.9 46.4 reduce-scatter.2
  190.7 24.5 reduce-scatter.4
where the time goes:
time: 251 us; the launch traced here: 250 us
  waiting for transfers between devices  87 us (35%)
  Pallas kernels  61.7 us (25%)
  starting transfers between devices  60.5 us (24%)
  local copies, waits for them, and re-layouts  17.9 us (7%)
  between operations  14.3 us (6%)
  other arithmetic  9.15 us (4%)
    pallas_call x9, Pallas kernels, call(): pl.pallas_call(body, grid=(1,), out_shape=[jax.ShapeDtypeStruct(s, t) for...  61.7 us
    ppermute x16, waiting for transfers between devices, turn_by(): return lax.ppermute(x, axis, [((i + by) % n, i) for i in range(n)])  36.9 us
    ppermute x16, starting transfers between devices, turn_by(): return lax.ppermute(x, axis, [((i + by) % n, i) for i in range(n)])  28.3 us
    all_to_all x1, waiting for transfers between devices, body(): g0 = sum_of(lax.all_to_all(g0, DP, 0, 0, tiled=True), 32)  13.9 us
    ppermute x4, starting transfers between devices, dp_turn(): return lax.ppermute(x, ('z', 'x', 'yh'), pairs)  13.7 us
    ppermute x4, waiting for transfers between devices, dp_turn(): return lax.ppermute(x, ('z', 'x', 'yh'), pairs)  11.8 us
    reduce_scatter x2, waiting for transfers between devices, scatter_sum(): return lax.psum_scatter(x, axis, scatter_dimension=0, tiled=True)  11.5 us
    ppermute x9, waiting for transfers between devices, mp_turn(): return lax.ppermute(x, ('yl', 'c'), [(i, i ^ slot) for i in range(4)])  9.95 us
  transfers between devices with their start and end apart: 34, of which 18 were waited for; matrix products, arithmetic and copies ran while one was open for 7% of the time, Pallas kernels for 20%

commit v1 on v0

--- a/solution.py
+++ b/solution.py
@@ -22,7 +22,7 @@
 MAIN = 640
 TAIL = 16
 FFP = 768
-VMEM_MB = 56
+VMEM_MB = 62
 PACK = 1024 + 384
 ROWS = (128, 128, 64, 64)
 OWN_AT = (0, 128, 256, 320)
@@ -130,10 +130,10 @@
     return jnp.where(low, pltpu.roll(v, 96, axis=1), pltpu.roll(v, 32, axis=1))
 
 
-def window(place, b):
+def window(place, b, times):
     r = ROWS[b]
-    i = lax.broadcasted_iota(jnp.int32, (r, r + 128), 0)
-    j = lax.broadcasted_iota(jnp.int32, (r, r + 128), 1)
+    i = lax.broadcasted_iota(jnp.int32, (times * r, r + 128), 0) & (r - 1)
+    j = lax.broadcasted_iota(jnp.int32, (times * r, r + 128), 1)
     begin = (place[1] * r) & (LEN - 1)
     at = j + (begin - REACH)
     return (j >= i) & (j <= i + 128) & (at >= 0) & (at < LEN)
@@ -147,9 +147,24 @@
     return jnp.where(head_lanes(v.shape, h), v, jnp.zeros_like(v))
 
 
+def by_head(v):
+    return jnp.concatenate([only(v, h) for h in range(4)], axis=0)
+
+
+def join_heads(v, r):
+    out = v[0:r]
+    for h in range(1, 4):
+        out = jnp.where(head_lanes(out.shape, h), v[h * r : h * r + r], out)
+    return out
+
+
+def columns_of(v, first, r):
+    return jnp.concatenate([v[:, first + h : first + h + 1] for h in range(4)], axis=0)
+
+
 def attend_kernel(
     place, xr, stat, w, cos, sin,
-    gains, normed, qo, kx, vx, att, lse, even, odd, wide, nb, raw,
+    gains, normed, qx, kx, vx, att, lse, even, odd, nb, raw,
 ):
     gains[...] = w[:, 1024:1152].astype(F32).T[0:8]
     g = gains[0:1]
@@ -163,7 +178,7 @@
         e, o, r = EXT_AT[b] + REACH, OWN_AT[b], ROWS[b]
         normed[o : o + r, :] = nb[e : e + r, :]
     for t in range(3):
-        into = (wide, kx, vx)[t]
+        into = (qx, kx, vx)[t]
         raw[...] = mm(nb[...], w[:, t * 256 : t * 256 + 256])
         for h in range(2):
             lanes = slice(h * 128, h * 128 + 128)
@@ -172,25 +187,20 @@
                 v = v * cos[...] + half_turn(v) * sin[...]
             into[:, lanes] = v.astype(BF)
     for b in range(4):
-        e, o, r = EXT_AT[b] + REACH, OWN_AT[b], ROWS[b]
-        qo[o : o + r, :] = wide[e : e + r, :]
-    for b in range(4):
-        allowed = window(place, b)
         e, at, r = EXT_AT[b], OWN_AT[b], ROWS[b]
+        allowed = window(place, b, 4)
+        x = nt(by_head(qx[e + 64 : e + 64 + r, :]), kx[e : e + r + 128, :]) * 0.125
+        x = jnp.where(allowed, x, NEG)
+        most = jnp.max(x, axis=1, keepdims=True)
+        x = jnp.exp(x - most)
+        total = jnp.sum(x, axis=1, keepdims=True)
+        y = mm((x * (1.0 / total)).astype(BF), vx[e : e + r + 128, :])
+        att[at : at + r, :] = join_heads(y, r).astype(BF)
+        total = most + jnp.log(total)
         lane = lax.broadcasted_iota(jnp.int32, (r, 128), 1)
         kept = jnp.zeros((r, 128), F32)
-        for t in range(2):
-            lanes = slice(t * 128, t * 128 + 128)
-            q, k, v = qo[at : at + r, lanes], kx[e : e + r + 128, lanes], vx[e : e + r + 128, lanes]
-            o = []
-            for h in range(2):
-                x = jnp.where(allowed, nt(only(q, h), k) * 0.125, NEG)
-                most = jnp.max(x, axis=1, keepdims=True)
-                x = jnp.exp(x - most)
-                total = jnp.sum(x, axis=1, keepdims=True)
-                o.append(mm((x * (1.0 / total)).astype(BF), v))
-                kept = jnp.where(lane == t * 2 + h, most + jnp.log(total), kept)
-            att[at : at + r, lanes] = jnp.where(head_lanes(o[0].shape, 0), o[0], o[1]).astype(BF)
+        for h in range(4):
+            kept = jnp.where(lane == h, total[h * r : h * r + r], kept)
         lse[at : at + r, :] = kept
     for s in range(4):
         y = nt(att[...], w[block(place, s), 768:1024])
@@ -271,10 +281,15 @@
         g[at, 3 * MAIN :] = tail.astype(BF)
 
 
-def attend_back_kernel(
-    place, half, far, half_c, far_c, ct, xhat, rinv, gains, w, att, qo, kx, vx, lse,
-    own, go, dq, dk, dv, below, above,
-    grad, gb, da, dk_ext, dv_ext,
+def edges(ref, last):
+    at = [OWN_AT[b] + (ROWS[b] - 64 if last else 0) for b in range(4)]
+    return jnp.concatenate([ref[k : k + 64, :] for k in at], axis=0)
+
+
+def norm_back_kernel(
+    place, half, far, half_c, far_c, ct, xhat, rinv, gains, w, att, lse,
+    own, gb, da, da_first, da_last,
+    grad, stat,
 ):
     gain = gains[1:2]
     load_sum(place, half, far, half_c, far_c, grad)
@@ -293,52 +308,64 @@
 
     own[...] = grad[:, block(place, 0)]
     da[...] = mm(gb[...], w[...]).astype(BF)
-    dk_ext[...] = jnp.zeros_like(dk_ext)
-    dv_ext[...] = jnp.zeros_like(dv_ext)
-    for b in range(4):
-        allowed = window(place, b)
-        e, o, r = EXT_AT[b], OWN_AT[b], ROWS[b]
-        for t in range(2):
-            lanes = slice(t * 128, t * 128 + 128)
-            q, k, v = qo[o : o + r, lanes], kx[e : e + r + 128, lanes], vx[e : e + r + 128, lanes]
-            d = da[o : o + r, lanes]
-            dqs, dks, dvs = [], [], []
-            for h in range(2):
-                qh, dh = only(q, h), only(d, h)
-                total = lse[o : o + r, t * 2 + h : t * 2 + h + 1]
-                p = jnp.exp(jnp.where(allowed, nt(qh, k) * 0.125 - total, NEG))
-                dp = nt(dh, v)
-                ds = (p * (dp - jnp.sum(p * dp, axis=1, keepdims=True))).astype(BF)
-                dqs.append(mm(ds, k))
-                dks.append(tn(ds, qh))
-                dvs.append(tn(p.astype(BF), dh))
-            dq[o : o + r, lanes] = jnp.where(head_lanes(dqs[0].shape, 0), dqs[0], dqs[1]) * 0.125
-            dk_ext[e : e + r + 128, lanes] = (dks[0] + dks[1]) * 0.125
-            dv_ext[e : e + r + 128, lanes] = dvs[0] + dvs[1]
+    prod = da[...].astype(F32) * att[...].astype(F32)
+    lane = lax.broadcasted_iota(jnp.int32, (OWN, 128), 1)
+    kept = lse[...]
+    for h in range(4):
+        centre = jnp.sum(only(prod, h), axis=1, keepdims=True)
+        kept = jnp.where(lane == 4 + h, centre, kept)
+    stat[...] = kept
+    for out, last in ((da_first, False), (da_last, True)):
+        out[0:HALO, :] = edges(da, last)
+        st = edges(stat, last).T[0:8]
+        high = st.astype(BF)
+        rest = (st - high.astype(F32)).astype(BF)
+        out[HALO : HALO + 16, :] = jnp.concatenate([high.astype(F32), rest.astype(F32)], axis=0).astype(BF)
+
+
+def attend_back_kernel(place, da, lse, gb, att, qx, kx, vx, go, dq, dk, dv):
     for b in range(4):
         e, o, r = EXT_AT[b], OWN_AT[b], ROWS[b]
-        dk[o : o + r, :] = dk_ext[e + 64 : e + 64 + r, :]
-        dv[o : o + r, :] = dv_ext[e + 64 : e + 64 + r, :]
-        at = slice(b * 64, b * 64 + 64)
-        below[at, 0:256] = dk_ext[e : e + 64, :].astype(BF)
-        below[at, 256:512] = dv_ext[e : e + 64, :].astype(BF)
-        above[at, 0:256] = dk_ext[e + 64 + r : e + 128 + r, :].astype(BF)
-        above[at, 256:512] = dv_ext[e + 64 + r : e + 128 + r, :].astype(BF)
+        q, d = by_head(qx[e + 64 : e + 64 + r, :]), by_head(da[o : o + r, :])
+        k, v = kx[e : e + r + 128, :], vx[e : e + r + 128, :]
+        total = columns_of(lse[o : o + r, :], 0, r)
+        p = jnp.exp(jnp.where(window(place, b, 4), nt(q, k) * 0.125 - total, NEG))
+        dp = nt(d, v)
+        ds = (p * (dp - jnp.sum(p * dp, axis=1, keepdims=True))).astype(BF)
+        dq[o : o + r, :] = join_heads(mm(ds, k), r) * 0.125
+        dk[o : o + r, :] = tn(ds, q)[64 : 64 + r] * 0.125
+        dv[o : o + r, :] = tn(p.astype(BF), d)[64 : 64 + r]
     for k in range(4):
         go[k * 256 : k * 256 + 256, :] = tn(gb[:, k * 256 : k * 256 + 256], att[...]).astype(BF)
 
 
 def qkv_back_kernel(
-    place, dq, dk, dv, low, high, cos, sin, xo, stat, gains, gain2, w,
+    place, dq, dk, dv, da_lo, da_hi, qx, kx, vx, cos, sin, xo, stat, gains, gain2, w,
     dn, pack, xq, raw, gsum,
 ):
+    i = lax.broadcasted_iota(jnp.int32, (256, 64), 0) & 63
+    j = lax.broadcasted_iota(jnp.int32, (256, 64), 1)
+    pad = jnp.zeros((120, HALO), F32)
+    known = []
+    for ref in (da_lo, da_hi):
+        st = ref[HALO : HALO + 16, :].astype(F32)
+        known.append(jnp.concatenate([st[0:8] + st[8:16], pad], axis=0).T)
     for b in range(4):
-        o, r = OWN_AT[b], ROWS[b]
+        e, o, r = EXT_AT[b], OWN_AT[b], ROWS[b]
+        begin = (place[1] * r) & (LEN - 1)
         at = slice(b * 64, b * 64 + 64)
-        dk[o : o + 64, :] += low[at, 0:256].astype(F32)
-        dv[o : o + 64, :] += low[at, 256:512].astype(F32)
-        dk[o + r - 64 : o + r, :] += high[at, 0:256].astype(F32)
-        dv[o + r - 64 : o + r, :] += high[at, 256:512].astype(F32)
+        for side in range(2):
+            of = e if side == 0 else e + 64 + r
+            keys = e + 64 if side == 0 else e + r
+            to = slice(o, o + 64) if side == 0 else slice(o + r - 64, o + r)
+            allowed = (j <= i) & (begin != 0) if side == 0 else (j >= i) & (begin + r != LEN)
+            q, d = by_head(qx[of : of + 64, :]), by_head((da_lo, da_hi)[side][at, :])
+            k, v = kx[keys : keys + 64, :], vx[keys : keys + 64, :]
+            st = known[side][at]
+            p = jnp.exp(jnp.where(allowed, nt(q, k) * 0.125 - columns_of(st, 0, 64), NEG))
+            ds = (p * (nt(d, v) - columns_of(st, 4, 64))).astype(BF)
+            dk[to, :] += tn(ds, q) * 0.125
+            dv[to, :] += tn(p.astype(BF), d)
     for b in range(4):
         e, o, r = EXT_AT[b] + REACH, OWN_AT[b], ROWS[b]
         c, s = cos[e : e + r, :], sin[e : e + r, :]
@@ -452,9 +479,10 @@
     shard = jnp.concatenate([shard0, shard1], axis=1)
     lows = jnp.concatenate([block_input[o + r - 64 : o + r] for o, r in zip(OWN_AT, ROWS)], axis=0)
     highs = jnp.concatenate([block_input[o : o + 64] for o in OWN_AT], axis=0)
+    lows, highs, shard = lax.optimization_barrier((lows, highs, shard))
     low, high = dp_turn(lows, 1), dp_turn(highs, -1)
-    shard, low, high = lax.optimization_barrier((shard, low, high))
     pair = turn_by(shard, "yh", 1)
+    low, high, pair = lax.optimization_barrier((low, high, pair))
     first = lax.axis_index("yh") == 0
     pair = [jnp.where(first, shard, pair), jnp.where(first, pair, shard)]
     pair = jnp.concatenate(pair, axis=0)
@@ -470,12 +498,12 @@
     xr, cotangent = lax.optimization_barrier((xr, cotangent))
     xr, *c_slots = lax.optimization_barrier((xr, *mp_gather(cotangent)))
     slots = [((2, OWN, 256), BF)] * 2
-    gains, normed1, qo, kx, vx, att, lse, *parts = call(
+    gains, normed1, qx, kx, vx, att, lse, *parts = call(
         10,
         attend_kernel,
-        [((8, D), F32), ((OWN, D), BF), ((OWN, 256), BF), ((EXT, 256), BF), ((EXT, 256), BF)]
+        [((8, D), F32), ((OWN, D), BF), ((EXT, 256), BF), ((EXT, 256), BF), ((EXT, 256), BF)]
         + [((OWN, 256), BF), ((OWN, 128), F32)] + slots,
-        [((EXT, 256), BF), ((EXT, D), BF), ((EXT, 256), F32)],
+        [((EXT, D), BF), ((EXT, 256), F32)],
         place, xr, stat1, w0, cos, sin,
     )
     ct, stream, xhat2, rinv2, normed2, act, de0, de1, even, odd, gain2 = call(
@@ -504,24 +532,30 @@
     g1 = scatter_sum(g1, "z")
     down = mp_terms(down)
 
-    grad, go, dq, dk, dv, below, above = call(
-        11,
+    grad, gb, da, da_first, da_last = call(
+        6,
+        norm_back_kernel,
+        [((OWN, 256), F32), ((OWN, D), BF), ((OWN, 256), BF)]
+        + [((HALO + 16, 256), BF)] * 2,
+        [((OWN, D), F32), ((OWN, 128), F32)],
+        place, half, far, half_c, far_c, ct, xhat2, rinv2, gains, columns(w0, 3, 256), att, lse,
+    )
+    gb, *down = lax.optimization_barrier((gb, *down))
+    da_lo, da_hi = dp_turn(da_last, 1), dp_turn(da_first, -1)
+    go, dq, dk, dv = call(
+        8,
         attend_back_kernel,
-        [((OWN, 256), F32), ((D, 256), BF)] + [((OWN, 256), F32)] * 3 + [((HALO, 512), BF)] * 2,
-        [((OWN, D), F32), ((OWN, D), BF), ((OWN, 256), BF), ((EXT, 256), F32), ((EXT, 256), F32)],
-        place, half, far, half_c, far_c, ct, xhat2, rinv2, gains, columns(w0, 3, 256),
-        att, qo, kx, vx, lse,
-    )
-    below, above, *down = lax.optimization_barrier((below, above, *down))
-    low = dp_turn(above, 1)
-    high = dp_turn(below, -1)
+        [((D, 256), BF)] + [((OWN, 256), F32)] * 3,
+        [],
+        place, da, lse, gb, att, qx, kx, vx,
+    )
     (block_output,) = call(2, output_kernel, [((OWN, 256), BF)], [], stream, *down)
     dn, pack, xq, raw = call(
         7,
         functools.partial(qkv_in_place, qkv_back_kernel),
         [((4, OWN, 256), BF), ((8, PACK), F32), ((OWN, 256), F32), ((OWN, 768), BF)],
         [((OWN, 256), F32), ((OWN, 256), F32), ((1, D), F32)],
-        place, dq, dk, dv, low, high, cos, sin, xo, stat1, gains, gain2, columns(w0, 0, 768),
+        place, dq, dk, dv, da_lo, da_hi, qx, kx, vx, cos, sin, xo, stat1, gains, gain2, columns(w0, 0, 768),
     )
     dn = mp_terms(dn)
     packs = [pack, *(mp_turn(pack, s) for s in (1, 2, 3))]

time: 251 us -> 246 us (0.980)
  starting transfers between devices: 60.5 us -> 48.2 us
  waiting for transfers between devices: 87 us -> 92.6 us
    ppermute x16, starting transfers between devices: 28.3 us -> 19.6 us  [turn_by(): return lax.ppermute(x, axis, [((i + by) % n, i) for i in range(n)])]
    ppermute x4, starting transfers between devices: 13.7 us -> 8.2 us  [dp_turn(): return lax.ppermute(x, ('z', 'x', 'yh'), pairs)]
    all_to_all x1, waiting for transfers between devices: 2.9 us -> 7.54 us  [body(): w0 = lax.all_to_all(spread, ('z', 'x'), 0, 0, tiled=True)]
    ppermute x9, waiting for transfers between devices: 9.95 us -> 12.6 us  [mp_turn(): return lax.ppermute(x, ('yl', 'c'), [(i, i ^ slot) for i in range(4)])]
    pallas_call x9 -> x10, Pallas kernels: 61.7 us -> 61.7 us  [call(): pl.pallas_call(body, grid=(1,), out_shape=[jax.ShapeDtypeStruct(s, t) for...]
    unnamed x64 -> x60, local copies, waits for them, and re-layouts: 6.67 us -> 6.65 us
  transfers between devices with their start and end apart: 34 -> 34, of which waited for: 18 -> 19; matrix products, arithmetic and copies ran while one was open for 7% -> 4% of each run, Pallas kernels for 20% -> 21%
where the time goes in v1:
time: 246 us; the launch traced here: 245 us
  waiting for transfers between devices  92.6 us (38%)
  Pallas kernels  61.7 us (25%)
  starting transfers between devices  48.2 us (20%)
  local copies, waits for them, and re-layouts  17.8 us (7%)
  between operations  14.2 us (6%)
  other arithmetic  10.9 us (4%)
    pallas_call x10, Pallas kernels, call(): pl.pallas_call(body, grid=(1,), out_shape=[jax.ShapeDtypeStruct(s, t) for...  61.7 us
    ppermute x16, waiting for transfers between devices, turn_by(): return lax.ppermute(x, axis, [((i + by) % n, i) for i in range(n)])  34.5 us
    ppermute x16, starting transfers between devices, turn_by(): return lax.ppermute(x, axis, [((i + by) % n, i) for i in range(n)])  19.6 us
    all_to_all x1, waiting for transfers between devices, body(): g0 = sum_of(lax.all_to_all(g0, DP, 0, 0, tiled=True), 32)  13.9 us
    ppermute x4, waiting for transfers between devices, dp_turn(): return lax.ppermute(x, ('z', 'x', 'yh'), pairs)  12.6 us
    ppermute x9, waiting for transfers between devices, mp_turn(): return lax.ppermute(x, ('yl', 'c'), [(i, i ^ slot) for i in range(4)])  12.6 us
    reduce_scatter x2, waiting for transfers between devices, scatter_sum(): return lax.psum_scatter(x, axis, scatter_dimension=0, tiled=True)  11.5 us
    all_to_all x1, starting transfers between devices, body(): g0 = sum_of(lax.all_to_all(g0, DP, 0, 0, tiled=True), 32)  8.75 us
  transfers between devices with their start and end apart: 34, of which 19 were waited for; matrix products, arithmetic and copies ran while one was open for 4% of the time, Pallas kernels for 21%

profile of v1, /device:TPU:1, one launch (start us, length us, event | category | flops | bytes accessed | tf_op | source)
XLA Modules:
  0.0 245.4 jit_solution(17414137881514790257)
XLA Ops:
  7.2 1.1 fusion.6
  14.9 3.8 %collective-permute-start.2 = (bf16[32,3200]{1,0:T(8,128)(2,1)S(1)}, bf16[32,3200]{1,0:T(8,128)(2,1)S(1)}, u32[]{:S(2)}, u32[]{:S(2)}) collective-permute-start(bf16[32,3200]{1,0:T(8,128)(2,1)S(1)} %concatenate.41), channel_id=1, source_target_pairs={{4,0},{0,4},{5,1},{1,5},{6,2},{2,6},{7,3},{3,7},{12,8},{8,12},{13,... | collective-permute-start | bytes 614408 | tf_op jit(solution)/shard_map/ppermute | solution.py:39
  18.8 1.9 collective-permute-start
  20.7 1.3 collective-permute-start.1
  22.0 3.3 %collective-permute-done = bf16[256,256]{1,0:T(8,128)(2,1)S(1)} collective-permute-done((bf16[256,256]{1,0:T(8,128)(2,1)S(1)}, bf16[256,256]{1,0:T(8,128)(2,1)S(1)}, u32[]{:S(2)}, u32[]{:S(2)}) %collective-permute-start) | collective-permute-done | bytes 131104 | tf_op jit(solution)/shard_map/ppermute | solution.py:451
  25.3 7.3 %collective-permute-done.1 = bf16[256,256]{1,0:T(8,128)(2,1)S(1)} collective-permute-done((bf16[256,256]{1,0:T(8,128)(2,1)S(1)}, bf16[256,256]{1,0:T(8,128)(2,1)S(1)}, u32[]{:S(2)}, u32[]{:S(2)}) %collective-permute-start.1) | collective-permute-done | bytes 131104 | tf_op jit(solution)/shard_map/ppermute | solution.py:451
  33.4 1.7 broadcast_in_dim.24
  35.1 6.2 %all-to-all-start = ((bf16[16,64,1152]{2,1,0:T(8,128)(2,1)}), bf16[16,64,1152]{2,1,0:T(8,128)(2,1)}, u32[]{:S(2)}, u32[]{:S(2)}) async-start(bf16[16,64,1152]{2,1,0:T(8,128)(2,1)} %broadcast_in_dim.24), calls=%async_computation | async-start | bytes 4718592 | tf_op jit(solution)/shard_map/all_to_all | solution.py:490
  41.5 1.6 collective-permute-start.3
  43.1 9.6 %collective-permute-done.4.x2 = bf16[896,256]{1,0:T(8,128)(2,1)S(1)} collective-permute-done((bf16[896,256]{1,0:T(8,128)(2,1)S(1)}, bf16[896,256]{1,0:T(8,128)(2,1)S(1)}, u32[]{:S(2)}, u32[]{:S(2)}) %collective-permute-start.4) | collective-permute-done | bytes 458784 | tf_op jit(solution)/shard_map/ppermute | solution.py:39
  52.7 1.7 collective-permute-start.5
  56.7 4.9 %shard_map.126 = (bf16[896,1024]{1,0:T(8,128)(2,1)}, bf16[384,1024]{1,0:T(8,128)(2,1)}, f32[896,128]{1,0:T(8,128)}) custom-call(s32[2]{0:T(128)} %pad_add_fusion.place, bf16[896,256]{1,0:T(8,128)(2,1)} %copy-done.5, bf16[896,256]{1,0:T(8,128)(2,1)} %copy-done.7, bf16[896,256]{1,0:T(8,128)(2,1)} %copy-done.6, bf16[896,256]{1,0:T(8,128)(2,1)} %copy-done.8), custom_call_target="tpu_custom_call" | custom-call | flops 5000000000 | tf_op jit(solution)/shard_map/pallas_call | solution.py:62
  62.3 5.7 %collective-permute-done.7.c2 = bf16[384,256]{1,0:T(8,128)(2,1)S(1)} collective-permute-done((bf16[384,256]{1,0:T(8,128)(2,1)}, bf16[384,256]{1,0:T(8,128)(2,1)S(1)}, u32[]{:S(2)}, u32[]{:S(2)}) %collective-permute-start.7) | collective-permute-done | bytes 196640 | tf_op jit(solution)/shard_map/ppermute | solution.py:39
  69.1 1.7 fusion
  70.8 1.7 pad_maximum_fusion
  72.5 7.5 %all-to-all-done = bf16[16,64,1152]{2,1,0:T(8,128)(2,1)} async-done(((bf16[16,64,1152]{2,1,0:T(8,128)(2,1)}), bf16[16,64,1152]{2,1,0:T(8,128)(2,1)}, u32[]{:S(2)}, u32[]{:S(2)}) %all-to-all-start) | async-done | bytes 2359328 | tf_op jit(solution)/shard_map/all_to_all | solution.py:490
  80.1 9.2 %shard_map.127 = (f32[8,1024]{1,0:T(8,128)}, bf16[384,1024]{1,0:T(8,128)(2,1)}, bf16[896,256]{1,0:T(8,128)(2,1)}, bf16[896,256]{1,0:T(8,128)(2,1)}, bf16[896,256...) custom-call(s32[2]{0:T(128)} %pad_add_fusion.place, ...), custom_call_target="tpu_custom_call" | custom-call | flops 10000000000 | tf_op jit(solution)/shard_map/pallas_call | solution.py:62
  89.3 1.9 collective-permute-start.9
  91.1 1.6 collective-permute-done.9
  94.4 9.9 %collective-permute-done.10.far = bf16[2,384,256]{2,1,0:T(8,128)(2,1)S(1)} collective-permute-done((bf16[2,384,256]{2,1,0:T(8,128)(2,1)S(1)}, bf16[2,384,256]{2,1,0:T(8,128)(2,1)S(1)}, u32[]{:S(2)}, u32[]{:S(2)}) %collective-permute-start.10) | collective-permute-done | bytes 393248 | tf_op jit(solution)/shard_map/ppermute | solution.py:39
  105.4 1.3 collective-permute-done.12.far_c
  107.5 10.6 %shard_map.128 = (bf16[384,1024]{1,0:T(8,128)(2,1)}, f32[384,256]{1,0:T(8,128)}, f32[384,1024]{1,0:T(8,128)}, f32[384,128]{1,0:T(8,128)}, bf16[384,1024]{1,0:T(8...) custom-call(s32[2]{0:T(128)} %pad_add_fusion.place, ...), custom_call_target="tpu_custom_call" | custom-call | flops 10000000000 | tf_op jit(solution)/shard_map/pallas_call | solution.py:62
  118.6 1.6 collective-permute-done.13
  121.3 8.1 %shard_map.129 = (bf16[4,384,256]{2,1,0:T(8,128)(2,1)}, bf16[1024,2048]{1,0:T(8,128)(2,1)}) custom-call(s32[2]{0:T(128)} %pad_add_fusion.place, bf16[384,1024]{1,0:T(8,128)(2,1)} %get-tuple-element.98.normed, bf16[384,768]{1,0:T(8,128)(2,1)} %get-tuple-element.99.act, bf16[384,768]{1,0:T(8,128)(2,1)} %get-tuple-element.100.de0, ...), custom_call_target="tpu_custom_call" | custom-call | flops 8999999488 | tf_op jit(solution)/shard_map/pallas_call | solution.py:62
  129.5 2.3 collective-permute-done.14.far
  131.8 1.3 collective-permute-start.15
  133.8 1.7 collective-permute-start.19
  137.0 5.5 %shard_map.130 = (f32[384,256]{1,0:T(8,128)}, bf16[384,1024]{1,0:T(8,128)(2,1)}, bf16[384,256]{1,0:T(8,128)(2,1)}, bf16[272,256]{1,0:T(8,128)(2,1)}, bf16[272,256]{1,0:T(8,128)(2,1)}) custom-call(s32[2]{0:T(128)} %pad_add_fusion.place, bf16[2,384,256]{2,1,0:T(8,128)(2,1)} %copy-done.3, bf16[2,384,256]{2,1,0:T(8,128)(2,1)} %collective-permute-done.14.far, ...), custom_call_target="tpu_custom_call" | custom-call | flops 6000000000 | tf_op jit(solution)/shard_map/pallas_call | solution.py:62
  142.6 2.4 collective-permute-done.19.c
  145.0 3.5 %collective-permute-start.20 = (bf16[272,256]{1,0:T(8,128)(2,1)}, bf16[272,256]{1,0:T(8,128)(2,1)S(1)}, u32[]{:S(2)}, u32[]{:S(2)}) collective-permute-start(bf16[272,256]{1,0:T(8,128)(2,1)} %get-tuple-element.125), channel_id=1, source_target_pairs={{0,4},{4,8},{8,12},{12,16},{16,20},{20,24},{24,28},{28,32},{32,36}... | collective-permute-start | bytes 417800 | tf_op jit(solution)/shard_map/ppermute | solution.py:451
  148.5 1.5 collective-permute-start.21
  150.0 6.9 %shard_map.132 = (bf16[1024,256]{1,0:T(8,128)(2,1)}, f32[384,256]{1,0:T(8,128)}, f32[384,256]{1,0:T(8,128)}, f32[384,256]{1,0:T(8,128)}) custom-call(s32[2]{0:T(128)} %pad_add_fusion.place, bf16[384,256]{1,0:T(8,128)(2,1)} %get-tuple-element.117.da, f32[384,128]{1,0:T(8,128)} %get-tuple-element.109.lse, bf16[384,1024]{1,0:T(8,128)(2,1)} %get-tuple-element.118.gb, ...), custom_call_target="tpu_custom_call" | custom-call | flops 8000000000 | tf_op jit(solution)/shard_map/pallas_call | solution.py:62
  156.9 2.0 collective-permute-done.21.refs_1_
  159.6 7.6 %shard_map.133 = (bf16[4,384,256]{2,1,0:T(8,128)(2,1)}, f32[8,1408]{1,0:T(8,128)}, f32[384,256]{1,0:T(8,128)}, bf16[384,768]{1,0:T(8,128)(2,1)}) custom-call(s32[2]{0:T(128)} %pad_add_fusion.place, f32[384,256]{1,0:T(8,128)} %get-tuple-element.122.dq, f32[384,256]{1,0:T(8,128)} %get-tuple-element.123.dk, f32[384,256]{1,0:T(8,128)} %get-tuple-element.124.dv, ...), custom_call_target="tpu_custom_call" | custom-call | flops 7000000000 | tf_op jit(solution)/shard_map/pallas_call | solution.py:62
  167.2 1.2 slice_bitcast_fusion
  168.9 1.7 collective-permute-start.24
  170.8 1.3 collective-permute-done.25.p1
  172.8 7.3 %collective-permute-done.26.p2 = f32[8,1408]{1,0:T(8,128)S(1)} collective-permute-done((f32[8,1408]{1,0:T(8,128)}, f32[8,1408]{1,0:T(8,128)S(1)}, u32[]{:S(2)}, u32[]{:S(2)}) %collective-permute-start.26) | collective-permute-done | bytes 45088 | tf_op jit(solution)/shard_map/ppermute | solution.py:432
  180.1 1.5 collective-permute-done.27.p3
  182.2 3.9 %shard_map.135 = bf16[1024,1152]{1,0:T(8,128)(2,1)} custom-call(bf16[384,1024]{1,0:T(8,128)(2,1)} %get-tuple-element.141.normed, bf16[384,768]{1,0:T(8,128)(2,1)} %get-tuple-element.142.raw, bf16[1024,256]{1,0:T(8,128)(2,1)} %get-tuple-element.143.go, f32[8,1408]{1,0:T(8,128)} %get-tuple-element.136.p0, f32[8,1408]{1,0:T(8,128)} %copy-done.24, ...), custom_call_target="tpu_custom_call" | custom-call | flops 4000000000 | tf_op jit(solution)/shard_map/pallas_call | solution.py:62
  186.1 8.7 %all-to-all-start.1 = ((bf16[32,32,1152]{2,1,0:T(8,128)(2,1)}), bf16[32,32,1152]{2,1,0:T(8,128)(2,1)}, u32[]{:S(2)}, u32[]{:S(2)}) async-start(bf16[32,32,1152]{2,1,0:T(8,128)(2,1)} %bitcast.48), calls=%async_computation.2 | async-start | bytes 4718592 | tf_op jit(solution)/shard_map/all_to_all | solution.py:566
  194.9 2.2 shard_map.131
  197.1 11.4 %reduce-scatter.5.cloned.1.call-done = bf16[64,2048]{1,0:T(8,128)(2,1)} async-done(((bf16[256,2048]{1,0:T(8,128)(2,1)}), bf16[64,2048]{1,0:T(8,128)(2,1)}) %reduce-scatter.5.cloned.1.call-update) | async-done | bytes 262160 | tf_op jit(solution)/shard_map/reduce_scatter | solution.py:47
  209.5 5.2 %collective-permute-start.28 = (bf16[32,2048]{1,0:T(8,128)(2,1)S(1)}, bf16[32,2048]{1,0:T(8,128)(2,1)S(1)}, u32[]{:S(2)}, u32[]{:S(2)}) collective-permute-start(bf16[32,2048]{1,0:T(8,128)(2,1)S(1)} %broadcast_select_fusion.2), channel_id=1, source_target_pairs={{4,0},{0,4},{5,1},{1,5},{6,2},{2,6},{7,3},{3,7},{12,8},{8,12},{13,... | collective-permute-start | bytes 393224 | tf_op jit(solution)/shard_map/ppermute | solution.py:39
  214.7 2.8 %shard_map.134 = bf16[384,256]{1,0:T(8,128)(2,1)} custom-call(s32[2]{0:T(128)} %pad_add_fusion.place, f32[384,256]{1,0:T(8,128)} %get-tuple-element.116.grad, bf16[4,384,256]{2,1,0:T(8,128)(2,1)} %get-tuple-element.132.own, bf16[384,256]{1,0:T(8,128)(2,1)} %copy-done.19, bf16[384,256]{1,0:T(8,128)(2,1)} %copy-done.20, bf16[384,256]{1,0:T(8,128)(2,1)} %copy-done.21, ...), custom_call_target="tpu_custom_call" | custom-call | flops 2000000000 | tf_op jit(solution)/shard_map/pallas_call | solution.py:62
  217.6 1.7 collective-permute-done.28
  220.9 13.9 %all-to-all-done.1 = bf16[32,32,1152]{2,1,0:T(8,128)(2,1)} async-done(((bf16[32,32,1152]{2,1,0:T(8,128)(2,1)}), bf16[32,32,1152]{2,1,0:T(8,128)(2,1)}, u32[]{:S(2)}, u32[]{:S(2)}) %all-to-all-start.1) | async-done | bytes 2359328 | tf_op jit(solution)/shard_map/all_to_all | solution.py:566
  234.8 2.0 convert_reduce_fusion
  (139 shorter events, 26.1 us)
Async XLA Ops:
  7.2 26.2 %copy-start = (bf16[384,256]{1,0:T(8,128)(2,1)S(1)}, bf16[384,256]{1,0:T(8,128)(2,1)}, u32[]{:S(2)}) copy-start(bf16[384,256]{1,0:T(8,128)(2,1)} %param.7) | copy-start | bytes 589828
  7.2 99.6 %all-gather.2.cloned.1.call-start = ((), (), s32[]{:S(2)}) async-start(), calls=%async_computation.4 | async-start | bytes 4456448 | tf_op jit(solution)/shard_map/all_gather | solution.py:491
  14.9 17.6 %collective-permute-start.2 = (bf16[32,3200]{1,0:T(8,128)(2,1)S(1)}, bf16[32,3200]{1,0:T(8,128)(2,1)S(1)}, u32[]{:S(2)}, u32[]{:S(2)}) collective-permute-start(bf16[32,3200]{1,0:T(8,128)(2,1)S(1)} %concatenate.41), channel_id=1, source_target_pairs={{4,0},{0,4},{5,1},{1,5},{6,2},{2,6},{7,3},{3,7},{12,8},{8,12},{13,... | collective-permute-start | bytes 614408 | tf_op jit(solution)/shard_map/ppermute | solution.py:39
  18.8 6.6 %collective-permute-start = (bf16[256,256]{1,0:T(8,128)(2,1)S(1)}, bf16[256,256]{1,0:T(8,128)(2,1)S(1)}, u32[]{:S(2)}, u32[]{:S(2)}) collective-permute-start(bf16[256,256]{1,0:T(8,128)(2,1)S(1)} %get-tuple-element.76), channel_id=1, source_target_pairs={{0,4},{4,8},{8,12},{12,16},{16,20},{20,24},{24,28},{28,32},{32,36}... | collective-permute-start | bytes 393224 | tf_op jit(solution)/shard_map/ppermute | solution.py:451
  20.7 11.9 %collective-permute-start.1 = (bf16[256,256]{1,0:T(8,128)(2,1)S(1)}, bf16[256,256]{1,0:T(8,128)(2,1)S(1)}, u32[]{:S(2)}, u32[]{:S(2)}) collective-permute-start(bf16[256,256]{1,0:T(8,128)(2,1)S(1)} %get-tuple-element.77), channel_id=1, source_target_pairs={{4,0},{8,4},{12,8},{16,12},{20,16},{24,20},{28,24},{32,28},{36,32}... | collective-permute-start | bytes 393224 | tf_op jit(solution)/shard_map/ppermute | solution.py:451
  35.1 44.9 %all-to-all-start = ((bf16[16,64,1152]{2,1,0:T(8,128)(2,1)}), bf16[16,64,1152]{2,1,0:T(8,128)(2,1)}, u32[]{:S(2)}, u32[]{:S(2)}) async-start(bf16[16,64,1152]{2,1,0:T(8,128)(2,1)} %broadcast_in_dim.24), calls=%async_computation | async-start | bytes 4718592 | tf_op jit(solution)/shard_map/all_to_all | solution.py:490
  41.3 140.3 %reduce-scatter.3.cloned.1.call-start = ((), (), s32[]{:S(2)}) async-start(), calls=%async_computation.5 | async-start | bytes 5242880 | tf_op jit(solution)/shard_map/reduce_scatter | solution.py:47
  41.4 14.5 %copy-start.5 = (bf16[896,256]{1,0:T(8,128)(2,1)}, bf16[896,256]{1,0:T(8,128)(2,1)S(1)}, u32[]{:S(2)}) copy-start(bf16[896,256]{1,0:T(8,128)(2,1)S(1)} %constant_dynamic-update-slice_fusion.x0) | copy-start | bytes 1376260
  41.4 11.3 %collective-permute-start.4 = (bf16[896,256]{1,0:T(8,128)(2,1)S(1)}, bf16[896,256]{1,0:T(8,128)(2,1)S(1)}, u32[]{:S(2)}, u32[]{:S(2)}) collective-permute-start(bf16[896,256]{1,0:T(8,128)(2,1)S(1)} %constant_dynamic-update-slice_fusion.x0), channel_id=1, source_target_pairs={{2,0},{0,2},{3,1},{1,3},{6,4},{4,6},{7,5},{5,7},{10,8},{8,10},{11,... | collective-permute-start | bytes 1376264 | tf_op jit(solution)/shard_map/ppermute | solution.py:39
  41.5 13.6 %collective-permute-start.3 = (bf16[896,256]{1,0:T(8,128)(2,1)S(1)}, bf16[896,256]{1,0:T(8,128)(2,1)S(1)}, u32[]{:S(2)}, u32[]{:S(2)}) collective-permute-start(bf16[896,256]{1,0:T(8,128)(2,1)S(1)} %constant_dynamic-update-slice_fusion.x0), channel_id=1, source_target_pairs={{1,0},{0,1},{3,2},{2,3},{5,4},{4,5},{7,6},{6,7},{9,8},{8,9},{11,10... | collective-permute-start | bytes 1376264 | tf_op jit(solution)/shard_map/ppermute | solution.py:39
  52.7 3.2 %collective-permute-start.5 = (bf16[896,256]{1,0:T(8,128)(2,1)S(1)}, bf16[896,256]{1,0:T(8,128)(2,1)S(1)}, u32[]{:S(2)}, u32[]{:S(2)}) collective-permute-start(bf16[896,256]{1,0:T(8,128)(2,1)S(1)} %collective-permute-done.4.x2), channel_id=1, source_target_pairs={{1,0},{0,1},{3,2},{2,3},{5,4},{4,5},{7,6},{6,7},{9,8},{8,9},{11,10... | collective-permute-start | bytes 1376264 | tf_op jit(solution)/shard_map/ppermute | solution.py:39
  61.6 6.5 %collective-permute-start.7 = (bf16[384,256]{1,0:T(8,128)(2,1)}, bf16[384,256]{1,0:T(8,128)(2,1)S(1)}, u32[]{:S(2)}, u32[]{:S(2)}) collective-permute-start(bf16[384,256]{1,0:T(8,128)(2,1)} %c0), channel_id=1, source_target_pairs={{2,0},{0,2},{3,1},{1,3},{6,4},{4,6},{7,5},{5,7},{10,8},{8,10},{11,... | collective-permute-start | bytes 589832 | tf_op jit(solution)/shard_map/ppermute | solution.py:39
  61.7 10.8 %collective-permute-start.6 = (bf16[384,256]{1,0:T(8,128)(2,1)}, bf16[384,256]{1,0:T(8,128)(2,1)S(1)}, u32[]{:S(2)}, u32[]{:S(2)}) collective-permute-start(bf16[384,256]{1,0:T(8,128)(2,1)} %c0), channel_id=1, source_target_pairs={{1,0},{0,1},{3,2},{2,3},{5,4},{4,5},{7,6},{6,7},{9,8},{8,9},{11,10... | collective-permute-start | bytes 589832 | tf_op jit(solution)/shard_map/ppermute | solution.py:39
  68.1 21.2 %copy-start.17 = (bf16[384,256]{1,0:T(8,128)(2,1)}, bf16[384,256]{1,0:T(8,128)(2,1)S(1)}, u32[]{:S(2)}) copy-start(bf16[384,256]{1,0:T(8,128)(2,1)S(1)} %collective-permute-done.7.c2) | copy-start | bytes 589828
  68.1 4.5 %collective-permute-start.8 = (bf16[384,256]{1,0:T(8,128)(2,1)S(1)}, bf16[384,256]{1,0:T(8,128)(2,1)}, u32[]{:S(2)}, u32[]{:S(2)}) collective-permute-start(bf16[384,256]{1,0:T(8,128)(2,1)S(1)} %collective-permute-done.7.c2), channel_id=1, source_target_pairs={{1,0},{0,1},{3,2},{2,3},{5,4},{4,5},{7,6},{6,7},{9,8},{8,9},{11,10... | collective-permute-start | bytes 589832 | tf_op jit(solution)/shard_map/ppermute | solution.py:39
  72.5 16.7 %copy-start.18 = (bf16[384,256]{1,0:T(8,128)(2,1)}, bf16[384,256]{1,0:T(8,128)(2,1)S(1)}, u32[]{:S(2)}) copy-start(bf16[384,256]{1,0:T(8,128)(2,1)S(1)} %collective-permute-done.6.c1) | copy-start | bytes 589828
  89.3 3.5 %collective-permute-start.9 = (bf16[2,384,256]{2,1,0:T(8,128)(2,1)}, bf16[2,384,256]{2,1,0:T(8,128)(2,1)S(1)}, u32[]{:S(2)}, u32[]{:S(2)}) collective-permute-start(bf16[2,384,256]{2,1,0:T(8,128)(2,1)} %get-tuple-element.89), channel_id=1, source_target_pairs={{1,0},{0,1},{3,2},{2,3},{5,4},{4,5},{7,6},{6,7},{9,8},{8,9},{11,10... | collective-permute-start | bytes 1179656 | tf_op jit(solution)/shard_map/ppermute | solution.py:39
  93.8 13.0 %copy-start.4 = (bf16[2,384,256]{2,1,0:T(8,128)(2,1)}, bf16[2,384,256]{2,1,0:T(8,128)(2,1)S(1)}, u32[]{:S(2)}) copy-start(bf16[2,384,256]{2,1,0:T(8,128)(2,1)S(1)} %add_convert_fusion.1.half) | copy-start | bytes 1179652
  93.8 10.5 %collective-permute-start.10 = (bf16[2,384,256]{2,1,0:T(8,128)(2,1)S(1)}, bf16[2,384,256]{2,1,0:T(8,128)(2,1)S(1)}, u32[]{:S(2)}, u32[]{:S(2)}) collective-permute-start(bf16[2,384,256]{2,1,0:T(8,128)(2,1)S(1)} %add_convert_fusion.1.half), channel_id=1, source_target_pairs={{2,0},{0,2},{3,1},{1,3},{6,4},{4,6},{7,5},{5,7},{10,8},{8,10},{11,... | collective-permute-start | bytes 1179656 | tf_op jit(solution)/shard_map/ppermute | solution.py:39
  93.9 11.5 %collective-permute-start.11 = (bf16[2,384,256]{2,1,0:T(8,128)(2,1)S(1)}, bf16[2,384,256]{2,1,0:T(8,128)(2,1)S(1)}, u32[]{:S(2)}, u32[]{:S(2)}) collective-permute-start(bf16[2,384,256]{2,1,0:T(8,128)(2,1)S(1)} %add_convert_fusion.1.half), channel_id=1, source_target_pairs={{1,0},{0,1},{3,2},{2,3},{5,4},{4,5},{7,6},{6,7},{9,8},{8,9},{11,10... | collective-permute-start | bytes 1179656 | tf_op jit(solution)/shard_map/ppermute | solution.py:39
  104.3 2.5 %collective-permute-start.12 = (bf16[2,384,256]{2,1,0:T(8,128)(2,1)S(1)}, bf16[2,384,256]{2,1,0:T(8,128)(2,1)S(1)}, u32[]{:S(2)}, u32[]{:S(2)}) collective-permute-start(bf16[2,384,256]{2,1,0:T(8,128)(2,1)S(1)} %collective-permute-done.10.far), channel_id=1, source_target_pairs={{1,0},{0,1},{3,2},{2,3},{5,4},{4,5},{7,6},{6,7},{9,8},{8,9},{11,10... | collective-permute-start | bytes 1179656 | tf_op jit(solution)/shard_map/ppermute | solution.py:39
  118.2 1.9 collective-permute-start.13
  121.2 10.6 %copy-start.3 = (bf16[2,384,256]{2,1,0:T(8,128)(2,1)}, bf16[2,384,256]{2,1,0:T(8,128)(2,1)S(1)}, u32[]{:S(2)}) copy-start(bf16[2,384,256]{2,1,0:T(8,128)(2,1)S(1)} %add_convert_fusion.half) | copy-start | bytes 1179652
  121.2 10.5 %collective-permute-start.14 = (bf16[2,384,256]{2,1,0:T(8,128)(2,1)S(1)}, bf16[2,384,256]{2,1,0:T(8,128)(2,1)}, u32[]{:S(2)}, u32[]{:S(2)}) collective-permute-start(bf16[2,384,256]{2,1,0:T(8,128)(2,1)S(1)} %add_convert_fusion.half), channel_id=1, source_target_pairs={{2,0},{0,2},{3,1},{1,3},{6,4},{4,6},{7,5},{5,7},{10,8},{8,10},{11,... | collective-permute-start | bytes 1179656 | tf_op jit(solution)/shard_map/ppermute | solution.py:39
  131.8 76.7 %reduce-scatter.5.cloned.1.call-start = ((), (), s32[]{:S(2)}) async-start(), calls=%async_computation.6 | async-start | bytes 1310720 | tf_op jit(solution)/shard_map/reduce_scatter | solution.py:47
  131.8 3.6 %collective-permute-start.15 = (bf16[2,384,256]{2,1,0:T(8,128)(2,1)S(1)}, bf16[2,384,256]{2,1,0:T(8,128)(2,1)S(1)}, u32[]{:S(2)}, u32[]{:S(2)}) collective-permute-start(bf16[2,384,256]{2,1,0:T(8,128)(2,1)S(1)} %add_convert_fusion.half), channel_id=1, source_target_pairs={{1,0},{0,1},{3,2},{2,3},{5,4},{4,5},{7,6},{6,7},{9,8},{8,9},{11,10... | collective-permute-start | bytes 1179656 | tf_op jit(solution)/shard_map/ppermute | solution.py:39
  133.1 3.1 %collective-permute-start.16 = (bf16[2,384,256]{2,1,0:T(8,128)(2,1)}, bf16[2,384,256]{2,1,0:T(8,128)(2,1)S(1)}, u32[]{:S(2)}, u32[]{:S(2)}) collective-permute-start(bf16[2,384,256]{2,1,0:T(8,128)(2,1)} %collective-permute-done.14.far), channel_id=1, source_target_pairs={{1,0},{0,1},{3,2},{2,3},{5,4},{4,5},{7,6},{6,7},{9,8},{8,9},{11,10... | collective-permute-start | bytes 1179656 | tf_op jit(solution)/shard_map/ppermute | solution.py:39
  133.2 9.3 %collective-permute-start.17 = (bf16[384,256]{1,0:T(8,128)(2,1)S(1)}, bf16[384,256]{1,0:T(8,128)(2,1)S(1)}, u32[]{:S(2)}, u32[]{:S(2)}) collective-permute-start(bf16[384,256]{1,0:T(8,128)(2,1)S(1)} %get-tuple-element.171), channel_id=1, source_target_pairs={{0,1},{1,0},{2,3},{3,2},{4,5},{5,4},{6,7},{7,6},{8,9},{9,8},{10,11... | collective-permute-start | bytes 589832 | tf_op jit(solution)/shard_map/ppermute | solution.py:432
  133.7 8.8 %collective-permute-start.18 = (bf16[384,256]{1,0:T(8,128)(2,1)S(1)}, bf16[384,256]{1,0:T(8,128)(2,1)S(1)}, u32[]{:S(2)}, u32[]{:S(2)}) collective-permute-start(bf16[384,256]{1,0:T(8,128)(2,1)S(1)} %get-tuple-element.170), channel_id=1, source_target_pairs={{0,2},{1,3},{2,0},{3,1},{4,6},{5,7},{6,4},{7,5},{8,10},{9,11},{10,... | collective-permute-start | bytes 589832 | tf_op jit(solution)/shard_map/ppermute | solution.py:432
  133.8 11.2 %collective-permute-start.19 = (bf16[384,256]{1,0:T(8,128)(2,1)S(1)}, bf16[384,256]{1,0:T(8,128)(2,1)S(1)}, u32[]{:S(2)}, u32[]{:S(2)}) collective-permute-start(bf16[384,256]{1,0:T(8,128)(2,1)S(1)} %get-tuple-element.169), channel_id=1, source_target_pairs={{0,3},{1,2},{2,1},{3,0},{4,7},{5,6},{6,5},{7,4},{8,11},{9,10},{10,... | collective-permute-start | bytes 589832 | tf_op jit(solution)/shard_map/ppermute | solution.py:432
  142.5 14.3 %copy-start.14 = (bf16[384,256]{1,0:T(8,128)(2,1)}, bf16[384,256]{1,0:T(8,128)(2,1)S(1)}, u32[]{:S(2)}) copy-start(bf16[384,256]{1,0:T(8,128)(2,1)S(1)} %collective-permute-done.17.a) | copy-start | bytes 589828
  142.6 14.3 %copy-start.15 = (bf16[384,256]{1,0:T(8,128)(2,1)}, bf16[384,256]{1,0:T(8,128)(2,1)S(1)}, u32[]{:S(2)}) copy-start(bf16[384,256]{1,0:T(8,128)(2,1)S(1)} %collective-permute-done.18.b) | copy-start | bytes 589828
  145.0 11.9 %copy-start.16 = (bf16[384,256]{1,0:T(8,128)(2,1)}, bf16[384,256]{1,0:T(8,128)(2,1)S(1)}, u32[]{:S(2)}) copy-start(bf16[384,256]{1,0:T(8,128)(2,1)S(1)} %collective-permute-done.19.c) | copy-start | bytes 589828
  145.0 11.9 %collective-permute-start.20 = (bf16[272,256]{1,0:T(8,128)(2,1)}, bf16[272,256]{1,0:T(8,128)(2,1)S(1)}, u32[]{:S(2)}, u32[]{:S(2)}) collective-permute-start(bf16[272,256]{1,0:T(8,128)(2,1)} %get-tuple-element.125), channel_id=1, source_target_pairs={{0,4},{4,8},{8,12},{12,16},{16,20},{20,24},{24,28},{28,32},{32,36}... | collective-permute-start | bytes 417800 | tf_op jit(solution)/shard_map/ppermute | solution.py:451
  148.5 10.5 %collective-permute-start.21 = (bf16[272,256]{1,0:T(8,128)(2,1)}, bf16[272,256]{1,0:T(8,128)(2,1)S(1)}, u32[]{:S(2)}, u32[]{:S(2)}) collective-permute-start(bf16[272,256]{1,0:T(8,128)(2,1)} %get-tuple-element.126), channel_id=1, source_target_pairs={{4,0},{8,4},{12,8},{16,12},{20,16},{24,20},{28,24},{32,28},{36,32}... | collective-permute-start | bytes 417800 | tf_op jit(solution)/shard_map/ppermute | solution.py:451
  168.4 13.2 %collective-permute-start.22 = (bf16[384,256]{1,0:T(8,128)(2,1)S(1)}, bf16[384,256]{1,0:T(8,128)(2,1)S(1)}, u32[]{:S(2)}, u32[]{:S(2)}) collective-permute-start(bf16[384,256]{1,0:T(8,128)(2,1)S(1)} %get-tuple-element.168), channel_id=1, source_target_pairs={{0,1},{1,0},{2,3},{3,2},{4,5},{5,4},{6,7},{7,6},{8,9},{9,8},{10,11... | collective-permute-start | bytes 589832 | tf_op jit(solution)/shard_map/ppermute | solution.py:432
  168.8 12.8 %collective-permute-start.23 = (bf16[384,256]{1,0:T(8,128)(2,1)S(1)}, bf16[384,256]{1,0:T(8,128)(2,1)S(1)}, u32[]{:S(2)}, u32[]{:S(2)}) collective-permute-start(bf16[384,256]{1,0:T(8,128)(2,1)S(1)} %get-tuple-element.167), channel_id=1, source_target_pairs={{0,2},{1,3},{2,0},{3,1},{4,6},{5,7},{6,4},{7,5},{8,10},{9,11},{10,... | collective-permute-start | bytes 589832 | tf_op jit(solution)/shard_map/ppermute | solution.py:432
  168.9 12.7 %collective-permute-start.24 = (bf16[384,256]{1,0:T(8,128)(2,1)S(1)}, bf16[384,256]{1,0:T(8,128)(2,1)S(1)}, u32[]{:S(2)}, u32[]{:S(2)}) collective-permute-start(bf16[384,256]{1,0:T(8,128)(2,1)S(1)} %get-tuple-element.166), channel_id=1, source_target_pairs={{0,3},{1,2},{2,1},{3,0},{4,7},{5,6},{6,5},{7,4},{8,11},{9,10},{10,... | collective-permute-start | bytes 589832 | tf_op jit(solution)/shard_map/ppermute | solution.py:432
  170.6 1.4 collective-permute-start.25
  170.7 9.4 %collective-permute-start.26 = (f32[8,1408]{1,0:T(8,128)}, f32[8,1408]{1,0:T(8,128)S(1)}, u32[]{:S(2)}, u32[]{:S(2)}) collective-permute-start(f32[8,1408]{1,0:T(8,128)} %get-tuple-element.136.p0), channel_id=1, source_target_pairs={{0,2},{1,3},{2,0},{3,1},{4,6},{5,7},{6,4},{7,5},{8,10},{9,11},{10,... | collective-permute-start | bytes 135176 | tf_op jit(solution)/shard_map/ppermute | solution.py:432
  172.0 9.7 %copy-start.24 = (f32[8,1408]{1,0:T(8,128)}, f32[8,1408]{1,0:T(8,128)S(1)}, u32[]{:S(2)}) copy-start(f32[8,1408]{1,0:T(8,128)S(1)} %collective-permute-done.25.p1) | copy-start | bytes 135172
  172.0 9.6 %collective-permute-start.27 = (f32[8,1408]{1,0:T(8,128)}, f32[8,1408]{1,0:T(8,128)S(1)}, u32[]{:S(2)}, u32[]{:S(2)}) collective-permute-start(f32[8,1408]{1,0:T(8,128)} %get-tuple-element.136.p0), channel_id=1, source_target_pairs={{0,3},{1,2},{2,1},{3,0},{4,7},{5,6},{6,5},{7,4},{8,11},{9,10},{10,... | collective-permute-start | bytes 135176 | tf_op jit(solution)/shard_map/ppermute | solution.py:432
  181.6 4.5 %copy-start.19 = (bf16[384,256]{1,0:T(8,128)(2,1)}, bf16[384,256]{1,0:T(8,128)(2,1)S(1)}, u32[]{:S(2)}) copy-start(bf16[384,256]{1,0:T(8,128)(2,1)S(1)} %collective-permute-done.22.a) | copy-start | bytes 589828
  181.6 4.5 %copy-start.20 = (bf16[384,256]{1,0:T(8,128)(2,1)}, bf16[384,256]{1,0:T(8,128)(2,1)S(1)}, u32[]{:S(2)}) copy-start(bf16[384,256]{1,0:T(8,128)(2,1)S(1)} %collective-permute-done.23.b) | copy-start | bytes 589828
  181.6 4.5 %copy-start.21 = (bf16[384,256]{1,0:T(8,128)(2,1)}, bf16[384,256]{1,0:T(8,128)(2,1)S(1)}, u32[]{:S(2)}) copy-start(bf16[384,256]{1,0:T(8,128)(2,1)S(1)} %collective-permute-done.24.c) | copy-start | bytes 589828
  186.1 48.7 %all-to-all-start.1 = ((bf16[32,32,1152]{2,1,0:T(8,128)(2,1)}), bf16[32,32,1152]{2,1,0:T(8,128)(2,1)}, u32[]{:S(2)}, u32[]{:S(2)}) async-start(bf16[32,32,1152]{2,1,0:T(8,128)(2,1)} %bitcast.48), calls=%async_computation.2 | async-start | bytes 4718592 | tf_op jit(solution)/shard_map/all_to_all | solution.py:566
  209.5 9.8 %collective-permute-start.28 = (bf16[32,2048]{1,0:T(8,128)(2,1)S(1)}, bf16[32,2048]{1,0:T(8,128)(2,1)S(1)}, u32[]{:S(2)}, u32[]{:S(2)}) collective-permute-start(bf16[32,2048]{1,0:T(8,128)(2,1)S(1)} %broadcast_select_fusion.2), channel_id=1, source_target_pairs={{4,0},{0,4},{5,1},{1,5},{6,2},{2,6},{7,3},{3,7},{12,8},{8,12},{13,... | collective-permute-start | bytes 393224 | tf_op jit(solution)/shard_map/ppermute | solution.py:39
  214.7 4.5 %copy-start.1 = (bf16[64,2048]{1,0:T(8,128)(2,1)S(1)}, bf16[64,2048]{1,0:T(8,128)(2,1)}, u32[]{:S(2)}) copy-start(bf16[64,2048]{1,0:T(8,128)(2,1)} %reduce-scatter.5.cloned.1.call-done) | copy-start | bytes 786436
  (13 other events, 19.6 us)
Sparse Core Ops, SparseCore 0:
  33.5 71.1 all-gather.1
  131.9 44.7 reduce-scatter.2
  181.8 26.6 reduce-scatter.4

commit v2 on v1

--- a/solution.py
+++ b/solution.py
@@ -41,6 +41,14 @@
 
 def sum_of(got, n):
     return jnp.sum(got.reshape(n, got.shape[0] // n, -1).astype(F32), axis=0)
+
+
+def sum_over(parts, axis):
+    n = lax.axis_size(axis)
+    total = parts[0].astype(F32)
+    for k in range(1, n):
+        total = total + lax.ppermute(parts[k], axis, [(i, (i + k) % n) for i in range(n)]).astype(F32)
+    return total.astype(BF)
 
 
 def scatter_sum(x, axis):
@@ -341,7 +349,7 @@
 
 def qkv_back_kernel(
     place, dq, dk, dv, da_lo, da_hi, qx, kx, vx, cos, sin, xo, stat, gains, gain2, w,
-    dn, pack, xq, raw, gsum,
+    even, odd, pack, xq, raw, gsum,
 ):
     i = lax.broadcasted_iota(jnp.int32, (256, 64), 0) & 63
     j = lax.broadcasted_iota(jnp.int32, (256, 64), 1)
@@ -383,7 +391,7 @@
     for s in range(4):
         at = block(place, s)
         y = nt(raw[...], w[at, :])
-        dn[s] = y.astype(BF)
+        (even, odd)[s & 1][s >> 1] = y.astype(BF)
         x = normalized(xo[:, at], st)
         if s == 0:
             xq[...] = x
@@ -398,21 +406,37 @@
     pack[1:2, 0:D] = gain2[...]
 
 
-def qkv_grads_kernel(normed, raw, go, p0, p1, p2, p3, g):
+def qkv_grads_kernel(normed, raw, go, g):
     for k in range(4):
         at = slice(k * 256, k * 256 + 256)
         g[at, 0:768] = tn(normed[:, at], raw[...]).astype(BF)
     g[:, 768:1024] = go[...]
+
+
+def gain_columns_kernel(p0, p1, p2, p3, g, out):
     row = lax.broadcasted_iota(jnp.int32, (8, D), 0)
     both = jnp.where(row < 2, p0[:, :D] + p1[:, :D] + p2[:, :D] + p3[:, :D], 0.0)
-    g[:, 1024:1152] = jnp.concatenate([both, jnp.zeros((120, D), F32)], axis=0).T.astype(BF)
-
-
-def leave_kernel(place, grad, own, a, b, c, p0, p1, p2, p3, xq, stat, gains, out):
+    out[...] = jnp.concatenate([both, jnp.zeros((120, D), F32)], axis=0).T.astype(BF)
+
+
+def with_gains(g, packs):
+    return pl.pallas_call(
+        gain_columns_kernel,
+        grid=(1,),
+        out_shape=jax.ShapeDtypeStruct(g.shape, g.dtype),
+        in_specs=[pl.BlockSpec(memory_space=pltpu.VMEM)] * 4 + [pl.BlockSpec(memory_space=pl.ANY)],
+        out_specs=pl.BlockSpec((D, 128), lambda i: (0, 8)),
+        input_output_aliases={4: 0},
+        cost_estimate=pl.CostEstimate(flops=10**9, bytes_accessed=0, transcendentals=0),
+        compiler_params=pltpu.CompilerParams(vmem_limit_bytes=VMEM_MB * 1024 * 1024),
+    )(*packs, g)
+
+
+def leave_kernel(place, grad, own, a, p0, p1, p2, p3, xq, stat, gains, out):
     sums = p0[:, D:] + p1[:, D:] + p2[:, D:] + p3[:, D:]
     sums = jnp.concatenate([sums, jnp.zeros((120, OWN), F32)], axis=0).T
     m1, m2 = sums[:, 0:1], sums[:, 1:2]
-    e = own[0].astype(F32) + a[...].astype(F32) + b[...].astype(F32) + c[...].astype(F32)
+    e = own[0].astype(F32) + a[...].astype(F32)
     e = e * gains[0:1, block(place, 0)]
     y = grad[...] + own_rows(stat)[:, 1:2] * (e - m1 - xq[...] * m2)
     out[...] = y.astype(BF)
@@ -549,20 +573,26 @@
         [],
         place, da, lse, gb, att, qx, kx, vx,
     )
-    (block_output,) = call(2, output_kernel, [((OWN, 256), BF)], [], stream, *down)
-    dn, pack, xq, raw = call(
+    even, odd, pack, xq, raw = call(
         7,
         functools.partial(qkv_in_place, qkv_back_kernel),
-        [((4, OWN, 256), BF), ((8, PACK), F32), ((OWN, 256), F32), ((OWN, 768), BF)],
+        [*slots, ((8, PACK), F32), ((OWN, 256), F32), ((OWN, 768), BF)],
         [((OWN, 256), F32), ((OWN, 256), F32), ((1, D), F32)],
         place, dq, dk, dv, da_lo, da_hi, qx, kx, vx, cos, sin, xo, stat1, gains, gain2, columns(w0, 0, 768),
     )
-    dn = mp_terms(dn)
+    half = mp_reduce(even, odd)
+    half, normed1 = lax.optimization_barrier((half, normed1))
+    dn = [half, turn_by(half[1], "yl", 1)]
     packs = [pack, *(mp_turn(pack, s) for s in (1, 2, 3))]
-    raw, g1, *rest = lax.optimization_barrier((raw, g1, *dn, *packs))
-    dn, packs = rest[:4], rest[4:]
-    g1 = scatter_sum(g1, "x")
-    (g0,) = call(4, qkv_grads_kernel, [((D, 1152), BF)], [], normed1, raw, go, *packs)
+    (g0,) = call(4, qkv_grads_kernel, [((D, 1152), BF)], [], normed1, raw, go)
+    at = lax.axis_index("x")
+    parts = [lax.dynamic_slice_in_dim(g1, ((at + k) % 4) * 64, 64, 0) for k in range(4)]
+    g0, *rest = lax.optimization_barrier((g0, *dn, *packs, *parts))
+    dn, packs, parts = rest[:2], rest[2:6], rest[6:]
+    g1 = sum_over(parts, "x")
+    g0 = with_gains(g0, packs)
+    g0, *down = lax.optimization_barrier((g0, *down))
+    (block_output,) = call(2, output_kernel, [((OWN, 256), BF)], [], stream, *down)
     g0 = sum_of(lax.all_to_all(g0, DP, 0, 0, tiled=True), 32)
     (input_grad,) = call(
         2, leave_kernel, [((OWN, 256), BF)], [],

time: 246 us -> 240 us (0.976); the launches traced: 245 us -> 237 us
  waiting for transfers between devices: 92.6 us -> 80 us
    ppermute x16 -> x18, waiting for transfers between devices: 34.5 us -> 52.4 us  [turn_by(): return lax.ppermute(x, axis, [((i + by) % n, i) for i in range(n)])]
    all_to_all x1, waiting for transfers between devices: 13.9 us -> 3.07 us  [body(): g0 = sum_of(lax.all_to_all(g0, DP, 0, 0, tiled=True), 32)]
    ppermute x9 -> x6, waiting for transfers between devices: 12.6 us -> 2.49 us  [mp_turn(): return lax.ppermute(x, ('yl', 'c'), [(i, i ^ slot) for i in range(4)])]
    reduce_scatter x2 -> x1, waiting for transfers between devices: 11.5 us -> 1.87 us  [scatter_sum(): return lax.psum_scatter(x, axis, scatter_dimension=0, tiled=True)]
    ppermute x0 -> x3, starting transfers between devices: none -> 4.78 us  [sum_over(): lax.ppermute(parts[k], axis, [(i, (i + k) % n) for i in range(n)])]
    ppermute x16 -> x18, starting transfers between devices: 19.6 us -> 17.8 us  [turn_by(): return lax.ppermute(x, axis, [((i + by) % n, i) for i in range(n)])]
    ppermute x9 -> x6, starting transfers between devices: 5.34 us -> 4.36 us  [mp_turn(): return lax.ppermute(x, ('yl', 'c'), [(i, i ^ slot) for i in range(4)])]
    unnamed x60 -> x56, local copies, waits for them, and re-layouts: 6.65 us -> 6.76 us
  transfers between devices with their start and end apart: 34 -> 35, of which waited for: 19 -> 16; matrix products, arithmetic and copies ran while one was open for 4% -> 5% of each run, Pallas kernels for 21% -> 22%
where the time goes in v2:
time: 240 us; the launch traced here: 237 us
  waiting for transfers between devices  80 us (33%)
  Pallas kernels  63.2 us (26%)
  starting transfers between devices  49.8 us (21%)
  local copies, waits for them, and re-layouts  18 us (8%)
  between operations  14.6 us (6%)
  other arithmetic  11.1 us (5%)
    pallas_call x10, Pallas kernels, call(): pl.pallas_call(body, grid=(1,), out_shape=[jax.ShapeDtypeStruct(s, t) for...  61.4 us
    ppermute x18, waiting for transfers between devices, turn_by(): return lax.ppermute(x, axis, [((i + by) % n, i) for i in range(n)])  52.4 us
    ppermute x18, starting transfers between devices, turn_by(): return lax.ppermute(x, axis, [((i + by) % n, i) for i in range(n)])  17.8 us
    ppermute x4, waiting for transfers between devices, dp_turn(): return lax.ppermute(x, ('z', 'x', 'yh'), pairs)  12.6 us
    all_to_all x1, starting transfers between devices, body(): g0 = sum_of(lax.all_to_all(g0, DP, 0, 0, tiled=True), 32)  8.38 us
    ppermute x4, starting transfers between devices, dp_turn(): return lax.ppermute(x, ('z', 'x', 'yh'), pairs)  8.21 us
    all_to_all x1, waiting for transfers between devices, body(): w0 = lax.all_to_all(spread, ('z', 'x'), 0, 0, tiled=True)  7.54 us
    unnamed x56, local copies, waits for them, and re-layouts  6.76 us
  transfers between devices with their start and end apart: 35, of which 16 were waited for; matrix products, arithmetic and copies ran while one was open for 5% of the time, Pallas kernels for 22%

profile of v2, /device:TPU:1, one launch (start us, length us, event | category | flops | bytes accessed | tf_op | source)
XLA Modules:
  0.0 236.6 jit_solution(11349484193679842725)
XLA Ops:
  14.9 3.8 %collective-permute-start.2 = (bf16[32,3200]{1,0:T(8,128)(2,1)S(1)}, bf16[32,3200]{1,0:T(8,128)(2,1)S(1)}, u32[]{:S(2)}, u32[]{:S(2)}) collective-permute-start(bf16[32,3200]{1,0:T(8,128)(2,1)S(1)} %concatenate.41), channel_id=1, source_target_pairs={{4,0},{0,4},{5,1},{1,5},{6,2},{2,6},{7,3},{3,7},{12,8},{8,12},{13,... | collective-permute-start | bytes 614408 | tf_op jit(solution)/shard_map/ppermute | solution.py:39
  18.8 1.9 collective-permute-start
  20.7 1.3 collective-permute-start.1
  22.0 3.3 %collective-permute-done = bf16[256,256]{1,0:T(8,128)(2,1)S(1)} collective-permute-done((bf16[256,256]{1,0:T(8,128)(2,1)S(1)}, bf16[256,256]{1,0:T(8,128)(2,1)S(1)}, u32[]{:S(2)}, u32[]{:S(2)}) %collective-permute-start) | collective-permute-done | bytes 131104 | tf_op jit(solution)/shard_map/ppermute | solution.py:475
  25.3 7.3 %collective-permute-done.1 = bf16[256,256]{1,0:T(8,128)(2,1)S(1)} collective-permute-done((bf16[256,256]{1,0:T(8,128)(2,1)S(1)}, bf16[256,256]{1,0:T(8,128)(2,1)S(1)}, u32[]{:S(2)}, u32[]{:S(2)}) %collective-permute-start.1) | collective-permute-done | bytes 131104 | tf_op jit(solution)/shard_map/ppermute | solution.py:475
  33.4 1.7 broadcast_in_dim.24
  35.2 6.2 %all-to-all-start = ((bf16[16,64,1152]{2,1,0:T(8,128)(2,1)}), bf16[16,64,1152]{2,1,0:T(8,128)(2,1)}, u32[]{:S(2)}, u32[]{:S(2)}) async-start(bf16[16,64,1152]{2,1,0:T(8,128)(2,1)} %broadcast_in_dim.24), calls=%async_computation | async-start | bytes 4718592 | tf_op jit(solution)/shard_map/all_to_all | solution.py:514
  41.6 1.6 collective-permute-start.3
  43.2 9.6 %collective-permute-done.4.x2 = bf16[896,256]{1,0:T(8,128)(2,1)S(1)} collective-permute-done((bf16[896,256]{1,0:T(8,128)(2,1)S(1)}, bf16[896,256]{1,0:T(8,128)(2,1)S(1)}, u32[]{:S(2)}, u32[]{:S(2)}) %collective-permute-start.4) | collective-permute-done | bytes 458784 | tf_op jit(solution)/shard_map/ppermute | solution.py:39
  52.7 1.7 collective-permute-start.5
  56.7 4.9 %shard_map.126 = (bf16[896,1024]{1,0:T(8,128)(2,1)}, bf16[384,1024]{1,0:T(8,128)(2,1)}, f32[896,128]{1,0:T(8,128)}) custom-call(s32[2]{0:T(128)} %pad_add_fusion.place, bf16[896,256]{1,0:T(8,128)(2,1)} %copy-done.5, bf16[896,256]{1,0:T(8,128)(2,1)} %copy-done.10, bf16[896,256]{1,0:T(8,128)(2,1)} %copy-done.9, bf16[896,256]{1,0:T(8,128)(2,1)} %copy-done.11), custom_call_target="tpu_custom_call" | custom-call | flops 5000000000 | tf_op jit(solution)/shard_map/pallas_call | solution.py:70
  62.4 5.7 %collective-permute-done.7.c2 = bf16[384,256]{1,0:T(8,128)(2,1)S(1)} collective-permute-done((bf16[384,256]{1,0:T(8,128)(2,1)}, bf16[384,256]{1,0:T(8,128)(2,1)S(1)}, u32[]{:S(2)}, u32[]{:S(2)}) %collective-permute-start.7) | collective-permute-done | bytes 196640 | tf_op jit(solution)/shard_map/ppermute | solution.py:39
  69.2 1.7 fusion
  70.9 1.7 pad_maximum_fusion
  72.6 7.5 %all-to-all-done = bf16[16,64,1152]{2,1,0:T(8,128)(2,1)} async-done(((bf16[16,64,1152]{2,1,0:T(8,128)(2,1)}), bf16[16,64,1152]{2,1,0:T(8,128)(2,1)}, u32[]{:S(2)}, u32[]{:S(2)}) %all-to-all-start) | async-done | bytes 2359328 | tf_op jit(solution)/shard_map/all_to_all | solution.py:514
  80.1 9.2 %shard_map.127 = (f32[8,1024]{1,0:T(8,128)}, bf16[384,1024]{1,0:T(8,128)(2,1)}, bf16[896,256]{1,0:T(8,128)(2,1)}, bf16[896,256]{1,0:T(8,128)(2,1)}, bf16[896,256...) custom-call(s32[2]{0:T(128)} %pad_add_fusion.place, ...), custom_call_target="tpu_custom_call" | custom-call | flops 10000000000 | tf_op jit(solution)/shard_map/pallas_call | solution.py:70
  89.3 1.9 collective-permute-start.9
  91.2 1.6 collective-permute-done.9
  94.4 9.9 %collective-permute-done.10.far = bf16[2,384,256]{2,1,0:T(8,128)(2,1)S(1)} collective-permute-done((bf16[2,384,256]{2,1,0:T(8,128)(2,1)S(1)}, bf16[2,384,256]{2,1,0:T(8,128)(2,1)S(1)}, u32[]{:S(2)}, u32[]{:S(2)}) %collective-permute-start.10) | collective-permute-done | bytes 393248 | tf_op jit(solution)/shard_map/ppermute | solution.py:39
  105.5 1.3 collective-permute-done.12.far_c
  107.6 10.7 %shard_map.128 = (bf16[384,1024]{1,0:T(8,128)(2,1)}, f32[384,256]{1,0:T(8,128)}, f32[384,1024]{1,0:T(8,128)}, f32[384,128]{1,0:T(8,128)}, bf16[384,1024]{1,0:T(8...) custom-call(s32[2]{0:T(128)} %pad_add_fusion.place, ...), custom_call_target="tpu_custom_call" | custom-call | flops 10000000000 | tf_op jit(solution)/shard_map/pallas_call | solution.py:70
  118.6 1.6 collective-permute-done.13
  121.4 8.1 %shard_map.129 = (bf16[4,384,256]{2,1,0:T(8,128)(2,1)}, bf16[1024,2048]{1,0:T(8,128)(2,1)}) custom-call(s32[2]{0:T(128)} %pad_add_fusion.place, bf16[384,1024]{1,0:T(8,128)(2,1)} %get-tuple-element.107.normed, bf16[384,768]{1,0:T(8,128)(2,1)} %get-tuple-element.108.act, bf16[384,768]{1,0:T(8,128)(2,1)} %get-tuple-element.109.de0, ...), custom_call_target="tpu_custom_call" | custom-call | flops 8999999488 | tf_op jit(solution)/shard_map/pallas_call | solution.py:70
  129.5 2.3 collective-permute-done.14.far
  131.8 1.3 collective-permute-start.15
  133.8 1.7 collective-permute-start.19
  137.0 5.5 %shard_map.130 = (f32[384,256]{1,0:T(8,128)}, bf16[384,1024]{1,0:T(8,128)(2,1)}, bf16[384,256]{1,0:T(8,128)(2,1)}, bf16[272,256]{1,0:T(8,128)(2,1)}, bf16[272,256]{1,0:T(8,128)(2,1)}) custom-call(s32[2]{0:T(128)} %pad_add_fusion.place, bf16[2,384,256]{2,1,0:T(8,128)(2,1)} %copy-done.3, bf16[2,384,256]{2,1,0:T(8,128)(2,1)} %collective-permute-done.14.far, ...), custom_call_target="tpu_custom_call" | custom-call | flops 6000000000 | tf_op jit(solution)/shard_map/pallas_call | solution.py:70
  142.5 2.5 %collective-permute-done.19.c = bf16[384,256]{1,0:T(8,128)(2,1)S(1)} collective-permute-done((bf16[384,256]{1,0:T(8,128)(2,1)S(1)}, bf16[384,256]{1,0:T(8,128)(2,1)S(1)}, u32[]{:S(2)}, u32[]{:S(2)}) %collective-permute-start.19) | collective-permute-done | bytes 196640 | tf_op jit(solution)/shard_map/ppermute | solution.py:456
  145.0 3.5 %collective-permute-start.20 = (bf16[272,256]{1,0:T(8,128)(2,1)}, bf16[272,256]{1,0:T(8,128)(2,1)S(1)}, u32[]{:S(2)}, u32[]{:S(2)}) collective-permute-start(bf16[272,256]{1,0:T(8,128)(2,1)} %get-tuple-element.129), channel_id=1, source_target_pairs={{0,4},{4,8},{8,12},{12,16},{16,20},{20,24},{24,28},{28,32},{32,36}... | collective-permute-start | bytes 417800 | tf_op jit(solution)/shard_map/ppermute | solution.py:475
  148.5 1.5 collective-permute-start.21
  150.0 6.9 %shard_map.131 = (bf16[1024,256]{1,0:T(8,128)(2,1)}, f32[384,256]{1,0:T(8,128)}, f32[384,256]{1,0:T(8,128)}, f32[384,256]{1,0:T(8,128)}) custom-call(s32[2]{0:T(128)} %pad_add_fusion.place, bf16[384,256]{1,0:T(8,128)(2,1)} %get-tuple-element.119.da, f32[384,128]{1,0:T(8,128)} %get-tuple-element.118.lse, bf16[384,1024]{1,0:T(8,128)(2,1)} %get-tuple-element.122.gb, ...), custom_call_target="tpu_custom_call" | custom-call | flops 8000000000 | tf_op jit(solution)/shard_map/pallas_call | solution.py:70
  157.0 2.0 collective-permute-done.21.refs_1_
  159.6 7.5 %shard_map.132 = (bf16[2,384,256]{2,1,0:T(8,128)(2,1)}, bf16[2,384,256]{2,1,0:T(8,128)(2,1)}, f32[8,1408]{1,0:T(8,128)}, f32[384,256]{1,0:T(8,128)}, bf16[384,768]{1,0:T(8,128)(2,1)}) custom-call(s32[2]{0:T(128)} %pad_add_fusion.place, f32[384,256]{1,0:T(8,128)} %get-tuple-element.126.dq, f32[384,256]{1,0:T(8,128)} %get-tuple-element.127.dk, ...), custom_call_target="tpu_custom_call" | custom-call | flops 7000000000 | tf_op jit(solution)/shard_map/pallas_call | solution.py:70
  167.8 1.9 collective-permute-start.26
  171.0 3.9 %shard_map.133.g = bf16[1024,1152]{1,0:T(8,128)(2,1)} custom-call(bf16[384,1024]{1,0:T(8,128)(2,1)} %get-tuple-element.135.normed, bf16[384,768]{1,0:T(8,128)(2,1)} %get-tuple-element.136.raw, bf16[1024,256]{1,0:T(8,128)(2,1)} %get-tuple-element.137.go), custom_call_target="tpu_custom_call" | custom-call | flops 4000000000 | tf_op jit(solution)/shard_map/pallas_call | solution.py:70
  174.8 1.9 reduce-scatter.2.cloned.1.call-done
  176.7 1.3 constant_dynamic-slice_fusion
  178.8 1.2 collective-permute-start.27
  180.0 2.4 %collective-permute-start.28 = (bf16[64,2048]{1,0:T(8,128)(2,1)S(1)}, bf16[64,2048]{1,0:T(8,128)(2,1)S(1)}, u32[]{:S(2)}, u32[]{:S(2)}) collective-permute-start(bf16[64,2048]{1,0:T(8,128)(2,1)S(1)} %get-tuple-element.161), channel_id=1, source_target_pairs={{0,16},{8,24},{16,0},{24,8},{1,17},{9,25},{17,1},{25,9},{2,18},{10... | collective-permute-start | bytes 786440 | tf_op jit(solution)/shard_map/ppermute | solution.py:50
  182.4 1.2 collective-permute-start.29
  183.5 1.8 shard_map.134
  185.3 8.4 %all-to-all-start.1 = ((bf16[32,32,1152]{2,1,0:T(8,128)(2,1)}), bf16[32,32,1152]{2,1,0:T(8,128)(2,1)}, u32[]{:S(2)}, u32[]{:S(2)}) async-start(bf16[32,32,1152]{2,1,0:T(8,128)(2,1)} %bitcast.44), calls=%async_computation.2 | async-start | bytes 4718592 | tf_op jit(solution)/shard_map/all_to_all | solution.py:596
  193.7 2.6 %shard_map.136 = bf16[384,256]{1,0:T(8,128)(2,1)} custom-call(s32[2]{0:T(128)} %pad_add_fusion.place, f32[384,256]{1,0:T(8,128)} %get-tuple-element.154.grad, bf16[2,384,256]{2,1,0:T(8,128)(2,1)} %copy-done.1, bf16[384,256]{1,0:T(8,128)(2,1)} %copy-done.22, f32[8,1408]{1,0:T(8,128)} %get-tuple-element.141.p0, f32[8,1408]{1,0:T(8,128)} %copy-done.6, ...), custom_call_target="tpu_custom_call" | custom-call | flops 2000000000 | tf_op jit(solution)/shard_map/pallas_call | solution.py:70
  196.5 2.7 %collective-permute-start.30 = (bf16[32,2048]{1,0:T(8,128)(2,1)S(1)}, bf16[32,2048]{1,0:T(8,128)(2,1)S(1)}, u32[]{:S(2)}, u32[]{:S(2)}) collective-permute-start(bf16[32,2048]{1,0:T(8,128)(2,1)S(1)} %broadcast_select_fusion.2), channel_id=1, source_target_pairs={{4,0},{0,4},{5,1},{1,5},{6,2},{2,6},{7,3},{3,7},{12,8},{8,12},{13,... | collective-permute-start | bytes 393224 | tf_op jit(solution)/shard_map/ppermute | solution.py:39
  199.2 2.2 shard_map.135
  201.4 19.6 %collective-permute-done.30 = bf16[32,2048]{1,0:T(8,128)(2,1)S(1)} collective-permute-done((bf16[32,2048]{1,0:T(8,128)(2,1)S(1)}, bf16[32,2048]{1,0:T(8,128)(2,1)S(1)}, u32[]{:S(2)}, u32[]{:S(2)}) %collective-permute-start.30) | collective-permute-done | bytes 131104 | tf_op jit(solution)/shard_map/ppermute | solution.py:39
  222.7 3.1 %all-to-all-done.1 = bf16[32,32,1152]{2,1,0:T(8,128)(2,1)} async-done(((bf16[32,32,1152]{2,1,0:T(8,128)(2,1)}), bf16[32,32,1152]{2,1,0:T(8,128)(2,1)}, u32[]{:S(2)}, u32[]{:S(2)}) %all-to-all-start.1) | async-done | bytes 2359328 | tf_op jit(solution)/shard_map/all_to_all | solution.py:596
  225.8 2.0 convert_reduce_fusion
  (140 shorter events, 27.1 us)
Async XLA Ops:
  7.2 26.2 %copy-start = (bf16[384,256]{1,0:T(8,128)(2,1)S(1)}, bf16[384,256]{1,0:T(8,128)(2,1)}, u32[]{:S(2)}) copy-start(bf16[384,256]{1,0:T(8,128)(2,1)} %param.7) | copy-start | bytes 589828
  7.2 99.7 %all-gather.2.cloned.1.call-start = ((), (), s32[]{:S(2)}) async-start(), calls=%async_computation.3 | async-start | bytes 4456448 | tf_op jit(solution)/shard_map/all_gather | solution.py:515
  14.9 17.6 %collective-permute-start.2 = (bf16[32,3200]{1,0:T(8,128)(2,1)S(1)}, bf16[32,3200]{1,0:T(8,128)(2,1)S(1)}, u32[]{:S(2)}, u32[]{:S(2)}) collective-permute-start(bf16[32,3200]{1,0:T(8,128)(2,1)S(1)} %concatenate.41), channel_id=1, source_target_pairs={{4,0},{0,4},{5,1},{1,5},{6,2},{2,6},{7,3},{3,7},{12,8},{8,12},{13,... | collective-permute-start | bytes 614408 | tf_op jit(solution)/shard_map/ppermute | solution.py:39
  18.8 6.6 %collective-permute-start = (bf16[256,256]{1,0:T(8,128)(2,1)S(1)}, bf16[256,256]{1,0:T(8,128)(2,1)S(1)}, u32[]{:S(2)}, u32[]{:S(2)}) collective-permute-start(bf16[256,256]{1,0:T(8,128)(2,1)S(1)} %get-tuple-element.85), channel_id=1, source_target_pairs={{0,4},{4,8},{8,12},{12,16},{16,20},{20,24},{24,28},{28,32},{32,36}... | collective-permute-start | bytes 393224 | tf_op jit(solution)/shard_map/ppermute | solution.py:475
  20.7 11.9 %collective-permute-start.1 = (bf16[256,256]{1,0:T(8,128)(2,1)S(1)}, bf16[256,256]{1,0:T(8,128)(2,1)S(1)}, u32[]{:S(2)}, u32[]{:S(2)}) collective-permute-start(bf16[256,256]{1,0:T(8,128)(2,1)S(1)} %get-tuple-element.86), channel_id=1, source_target_pairs={{4,0},{8,4},{12,8},{16,12},{20,16},{24,20},{28,24},{32,28},{36,32}... | collective-permute-start | bytes 393224 | tf_op jit(solution)/shard_map/ppermute | solution.py:475
  35.2 44.9 %all-to-all-start = ((bf16[16,64,1152]{2,1,0:T(8,128)(2,1)}), bf16[16,64,1152]{2,1,0:T(8,128)(2,1)}, u32[]{:S(2)}, u32[]{:S(2)}) async-start(bf16[16,64,1152]{2,1,0:T(8,128)(2,1)} %broadcast_in_dim.24), calls=%async_computation | async-start | bytes 4718592 | tf_op jit(solution)/shard_map/all_to_all | solution.py:514
  41.4 135.3 %reduce-scatter.2.cloned.1.call-start = ((), (), s32[]{:S(2)}) async-start(), calls=%async_computation.4 | async-start | bytes 5242880 | tf_op jit(solution)/shard_map/reduce_scatter | solution.py:55
  41.5 14.5 %copy-start.5 = (bf16[896,256]{1,0:T(8,128)(2,1)}, bf16[896,256]{1,0:T(8,128)(2,1)S(1)}, u32[]{:S(2)}) copy-start(bf16[896,256]{1,0:T(8,128)(2,1)S(1)} %constant_dynamic-update-slice_fusion.x0) | copy-start | bytes 1376260
  41.5 11.3 %collective-permute-start.4 = (bf16[896,256]{1,0:T(8,128)(2,1)S(1)}, bf16[896,256]{1,0:T(8,128)(2,1)S(1)}, u32[]{:S(2)}, u32[]{:S(2)}) collective-permute-start(bf16[896,256]{1,0:T(8,128)(2,1)S(1)} %constant_dynamic-update-slice_fusion.x0), channel_id=1, source_target_pairs={{2,0},{0,2},{3,1},{1,3},{6,4},{4,6},{7,5},{5,7},{10,8},{8,10},{11,... | collective-permute-start | bytes 1376264 | tf_op jit(solution)/shard_map/ppermute | solution.py:39
  41.6 13.5 %collective-permute-start.3 = (bf16[896,256]{1,0:T(8,128)(2,1)S(1)}, bf16[896,256]{1,0:T(8,128)(2,1)S(1)}, u32[]{:S(2)}, u32[]{:S(2)}) collective-permute-start(bf16[896,256]{1,0:T(8,128)(2,1)S(1)} %constant_dynamic-update-slice_fusion.x0), channel_id=1, source_target_pairs={{1,0},{0,1},{3,2},{2,3},{5,4},{4,5},{7,6},{6,7},{9,8},{8,9},{11,10... | collective-permute-start | bytes 1376264 | tf_op jit(solution)/shard_map/ppermute | solution.py:39
  52.7 3.2 %collective-permute-start.5 = (bf16[896,256]{1,0:T(8,128)(2,1)S(1)}, bf16[896,256]{1,0:T(8,128)(2,1)S(1)}, u32[]{:S(2)}, u32[]{:S(2)}) collective-permute-start(bf16[896,256]{1,0:T(8,128)(2,1)S(1)} %collective-permute-done.4.x2), channel_id=1, source_target_pairs={{1,0},{0,1},{3,2},{2,3},{5,4},{4,5},{7,6},{6,7},{9,8},{8,9},{11,10... | collective-permute-start | bytes 1376264 | tf_op jit(solution)/shard_map/ppermute | solution.py:39
  61.6 6.4 %collective-permute-start.7 = (bf16[384,256]{1,0:T(8,128)(2,1)}, bf16[384,256]{1,0:T(8,128)(2,1)S(1)}, u32[]{:S(2)}, u32[]{:S(2)}) collective-permute-start(bf16[384,256]{1,0:T(8,128)(2,1)} %c0), channel_id=1, source_target_pairs={{2,0},{0,2},{3,1},{1,3},{6,4},{4,6},{7,5},{5,7},{10,8},{8,10},{11,... | collective-permute-start | bytes 589832 | tf_op jit(solution)/shard_map/ppermute | solution.py:39
  61.7 10.8 %collective-permute-start.6 = (bf16[384,256]{1,0:T(8,128)(2,1)}, bf16[384,256]{1,0:T(8,128)(2,1)S(1)}, u32[]{:S(2)}, u32[]{:S(2)}) collective-permute-start(bf16[384,256]{1,0:T(8,128)(2,1)} %c0), channel_id=1, source_target_pairs={{1,0},{0,1},{3,2},{2,3},{5,4},{4,5},{7,6},{6,7},{9,8},{8,9},{11,10... | collective-permute-start | bytes 589832 | tf_op jit(solution)/shard_map/ppermute | solution.py:39
  68.1 21.2 %copy-start.20 = (bf16[384,256]{1,0:T(8,128)(2,1)}, bf16[384,256]{1,0:T(8,128)(2,1)S(1)}, u32[]{:S(2)}) copy-start(bf16[384,256]{1,0:T(8,128)(2,1)S(1)} %collective-permute-done.7.c2) | copy-start | bytes 589828
  68.1 4.5 %collective-permute-start.8 = (bf16[384,256]{1,0:T(8,128)(2,1)S(1)}, bf16[384,256]{1,0:T(8,128)(2,1)}, u32[]{:S(2)}, u32[]{:S(2)}) collective-permute-start(bf16[384,256]{1,0:T(8,128)(2,1)S(1)} %collective-permute-done.7.c2), channel_id=1, source_target_pairs={{1,0},{0,1},{3,2},{2,3},{5,4},{4,5},{7,6},{6,7},{9,8},{8,9},{11,10... | collective-permute-start | bytes 589832 | tf_op jit(solution)/shard_map/ppermute | solution.py:39
  72.6 16.7 %copy-start.21 = (bf16[384,256]{1,0:T(8,128)(2,1)}, bf16[384,256]{1,0:T(8,128)(2,1)S(1)}, u32[]{:S(2)}) copy-start(bf16[384,256]{1,0:T(8,128)(2,1)S(1)} %collective-permute-done.6.c1) | copy-start | bytes 589828
  89.3 3.5 %collective-permute-start.9 = (bf16[2,384,256]{2,1,0:T(8,128)(2,1)}, bf16[2,384,256]{2,1,0:T(8,128)(2,1)S(1)}, u32[]{:S(2)}, u32[]{:S(2)}) collective-permute-start(bf16[2,384,256]{2,1,0:T(8,128)(2,1)} %get-tuple-element.98), channel_id=1, source_target_pairs={{1,0},{0,1},{3,2},{2,3},{5,4},{4,5},{7,6},{6,7},{9,8},{8,9},{11,10... | collective-permute-start | bytes 1179656 | tf_op jit(solution)/shard_map/ppermute | solution.py:39
  93.9 13.0 %copy-start.4 = (bf16[2,384,256]{2,1,0:T(8,128)(2,1)}, bf16[2,384,256]{2,1,0:T(8,128)(2,1)S(1)}, u32[]{:S(2)}) copy-start(bf16[2,384,256]{2,1,0:T(8,128)(2,1)S(1)} %add_convert_fusion.2.half) | copy-start | bytes 1179652
  93.9 10.5 %collective-permute-start.10 = (bf16[2,384,256]{2,1,0:T(8,128)(2,1)S(1)}, bf16[2,384,256]{2,1,0:T(8,128)(2,1)S(1)}, u32[]{:S(2)}, u32[]{:S(2)}) collective-permute-start(bf16[2,384,256]{2,1,0:T(8,128)(2,1)S(1)} %add_convert_fusion.2.half), channel_id=1, source_target_pairs={{2,0},{0,2},{3,1},{1,3},{6,4},{4,6},{7,5},{5,7},{10,8},{8,10},{11,... | collective-permute-start | bytes 1179656 | tf_op jit(solution)/shard_map/ppermute | solution.py:39
  94.0 11.5 %collective-permute-start.11 = (bf16[2,384,256]{2,1,0:T(8,128)(2,1)S(1)}, bf16[2,384,256]{2,1,0:T(8,128)(2,1)S(1)}, u32[]{:S(2)}, u32[]{:S(2)}) collective-permute-start(bf16[2,384,256]{2,1,0:T(8,128)(2,1)S(1)} %add_convert_fusion.2.half), channel_id=1, source_target_pairs={{1,0},{0,1},{3,2},{2,3},{5,4},{4,5},{7,6},{6,7},{9,8},{8,9},{11,10... | collective-permute-start | bytes 1179656 | tf_op jit(solution)/shard_map/ppermute | solution.py:39
  104.4 2.5 %collective-permute-start.12 = (bf16[2,384,256]{2,1,0:T(8,128)(2,1)S(1)}, bf16[2,384,256]{2,1,0:T(8,128)(2,1)S(1)}, u32[]{:S(2)}, u32[]{:S(2)}) collective-permute-start(bf16[2,384,256]{2,1,0:T(8,128)(2,1)S(1)} %collective-permute-done.10.far), channel_id=1, source_target_pairs={{1,0},{0,1},{3,2},{2,3},{5,4},{4,5},{7,6},{6,7},{9,8},{8,9},{11,10... | collective-permute-start | bytes 1179656 | tf_op jit(solution)/shard_map/ppermute | solution.py:39
  118.2 1.9 collective-permute-start.13
  121.3 10.6 %copy-start.3 = (bf16[2,384,256]{2,1,0:T(8,128)(2,1)}, bf16[2,384,256]{2,1,0:T(8,128)(2,1)S(1)}, u32[]{:S(2)}) copy-start(bf16[2,384,256]{2,1,0:T(8,128)(2,1)S(1)} %add_convert_fusion.1.half) | copy-start | bytes 1179652
  121.3 10.5 %collective-permute-start.14 = (bf16[2,384,256]{2,1,0:T(8,128)(2,1)S(1)}, bf16[2,384,256]{2,1,0:T(8,128)(2,1)}, u32[]{:S(2)}, u32[]{:S(2)}) collective-permute-start(bf16[2,384,256]{2,1,0:T(8,128)(2,1)S(1)} %add_convert_fusion.1.half), channel_id=1, source_target_pairs={{2,0},{0,2},{3,1},{1,3},{6,4},{4,6},{7,5},{5,7},{10,8},{8,10},{11,... | collective-permute-start | bytes 1179656 | tf_op jit(solution)/shard_map/ppermute | solution.py:39
  131.8 3.6 %collective-permute-start.15 = (bf16[2,384,256]{2,1,0:T(8,128)(2,1)S(1)}, bf16[2,384,256]{2,1,0:T(8,128)(2,1)S(1)}, u32[]{:S(2)}, u32[]{:S(2)}) collective-permute-start(bf16[2,384,256]{2,1,0:T(8,128)(2,1)S(1)} %add_convert_fusion.1.half), channel_id=1, source_target_pairs={{1,0},{0,1},{3,2},{2,3},{5,4},{4,5},{7,6},{6,7},{9,8},{8,9},{11,10... | collective-permute-start | bytes 1179656 | tf_op jit(solution)/shard_map/ppermute | solution.py:39
  133.1 3.1 %collective-permute-start.16 = (bf16[2,384,256]{2,1,0:T(8,128)(2,1)}, bf16[2,384,256]{2,1,0:T(8,128)(2,1)S(1)}, u32[]{:S(2)}, u32[]{:S(2)}) collective-permute-start(bf16[2,384,256]{2,1,0:T(8,128)(2,1)} %collective-permute-done.14.far), channel_id=1, source_target_pairs={{1,0},{0,1},{3,2},{2,3},{5,4},{4,5},{7,6},{6,7},{9,8},{8,9},{11,10... | collective-permute-start | bytes 1179656 | tf_op jit(solution)/shard_map/ppermute | solution.py:39
  133.3 9.2 %collective-permute-start.17 = (bf16[384,256]{1,0:T(8,128)(2,1)S(1)}, bf16[384,256]{1,0:T(8,128)(2,1)S(1)}, u32[]{:S(2)}, u32[]{:S(2)}) collective-permute-start(bf16[384,256]{1,0:T(8,128)(2,1)S(1)} %get-tuple-element.190), channel_id=1, source_target_pairs={{0,1},{1,0},{2,3},{3,2},{4,5},{5,4},{6,7},{7,6},{8,9},{9,8},{10,11... | collective-permute-start | bytes 589832 | tf_op jit(solution)/shard_map/ppermute | solution.py:456
  133.8 8.8 %collective-permute-start.18 = (bf16[384,256]{1,0:T(8,128)(2,1)S(1)}, bf16[384,256]{1,0:T(8,128)(2,1)S(1)}, u32[]{:S(2)}, u32[]{:S(2)}) collective-permute-start(bf16[384,256]{1,0:T(8,128)(2,1)S(1)} %get-tuple-element.189), channel_id=1, source_target_pairs={{0,2},{1,3},{2,0},{3,1},{4,6},{5,7},{6,4},{7,5},{8,10},{9,11},{10,... | collective-permute-start | bytes 589832 | tf_op jit(solution)/shard_map/ppermute | solution.py:456
  133.8 11.2 %collective-permute-start.19 = (bf16[384,256]{1,0:T(8,128)(2,1)S(1)}, bf16[384,256]{1,0:T(8,128)(2,1)S(1)}, u32[]{:S(2)}, u32[]{:S(2)}) collective-permute-start(bf16[384,256]{1,0:T(8,128)(2,1)S(1)} %get-tuple-element.188), channel_id=1, source_target_pairs={{0,3},{1,2},{2,1},{3,0},{4,7},{5,6},{6,5},{7,4},{8,11},{9,10},{10,... | collective-permute-start | bytes 589832 | tf_op jit(solution)/shard_map/ppermute | solution.py:456
  142.5 14.4 %copy-start.17 = (bf16[384,256]{1,0:T(8,128)(2,1)}, bf16[384,256]{1,0:T(8,128)(2,1)S(1)}, u32[]{:S(2)}) copy-start(bf16[384,256]{1,0:T(8,128)(2,1)S(1)} %collective-permute-done.17.a) | copy-start | bytes 589828
  142.5 14.4 %copy-start.18 = (bf16[384,256]{1,0:T(8,128)(2,1)}, bf16[384,256]{1,0:T(8,128)(2,1)S(1)}, u32[]{:S(2)}) copy-start(bf16[384,256]{1,0:T(8,128)(2,1)S(1)} %collective-permute-done.18.b) | copy-start | bytes 589828
  145.0 11.9 %copy-start.19 = (bf16[384,256]{1,0:T(8,128)(2,1)}, bf16[384,256]{1,0:T(8,128)(2,1)S(1)}, u32[]{:S(2)}) copy-start(bf16[384,256]{1,0:T(8,128)(2,1)S(1)} %collective-permute-done.19.c) | copy-start | bytes 589828
  145.0 11.9 %collective-permute-start.20 = (bf16[272,256]{1,0:T(8,128)(2,1)}, bf16[272,256]{1,0:T(8,128)(2,1)S(1)}, u32[]{:S(2)}, u32[]{:S(2)}) collective-permute-start(bf16[272,256]{1,0:T(8,128)(2,1)} %get-tuple-element.129), channel_id=1, source_target_pairs={{0,4},{4,8},{8,12},{12,16},{16,20},{20,24},{24,28},{28,32},{32,36}... | collective-permute-start | bytes 417800 | tf_op jit(solution)/shard_map/ppermute | solution.py:475
  148.5 10.5 %collective-permute-start.21 = (bf16[272,256]{1,0:T(8,128)(2,1)}, bf16[272,256]{1,0:T(8,128)(2,1)S(1)}, u32[]{:S(2)}, u32[]{:S(2)}) collective-permute-start(bf16[272,256]{1,0:T(8,128)(2,1)} %get-tuple-element.130), channel_id=1, source_target_pairs={{4,0},{8,4},{12,8},{16,12},{20,16},{24,20},{28,24},{32,28},{36,32}... | collective-permute-start | bytes 417800 | tf_op jit(solution)/shard_map/ppermute | solution.py:475
  167.1 2.6 %collective-permute-start.22 = (bf16[2,384,256]{2,1,0:T(8,128)(2,1)}, bf16[2,384,256]{2,1,0:T(8,128)(2,1)S(1)}, u32[]{:S(2)}, u32[]{:S(2)}) collective-permute-start(bf16[2,384,256]{2,1,0:T(8,128)(2,1)} %get-tuple-element.133), channel_id=1, source_target_pairs={{1,0},{0,1},{3,2},{2,3},{5,4},{4,5},{7,6},{6,7},{9,8},{8,9},{11,10... | collective-permute-start | bytes 1179656 | tf_op jit(solution)/shard_map/ppermute | solution.py:39
  167.6 10.4 %collective-permute-start.24 = (f32[8,1408]{1,0:T(8,128)}, f32[8,1408]{1,0:T(8,128)S(1)}, u32[]{:S(2)}, u32[]{:S(2)}) collective-permute-start(f32[8,1408]{1,0:T(8,128)} %get-tuple-element.141.p0), channel_id=1, source_target_pairs={{0,1},{1,0},{2,3},{3,2},{4,5},{5,4},{6,7},{7,6},{8,9},{9,8},{10,11... | collective-permute-start | bytes 135176 | tf_op jit(solution)/shard_map/ppermute | solution.py:456
  167.7 10.3 %collective-permute-start.25 = (f32[8,1408]{1,0:T(8,128)}, f32[8,1408]{1,0:T(8,128)S(1)}, u32[]{:S(2)}, u32[]{:S(2)}) collective-permute-start(f32[8,1408]{1,0:T(8,128)} %get-tuple-element.141.p0), channel_id=1, source_target_pairs={{0,2},{1,3},{2,0},{3,1},{4,6},{5,7},{6,4},{7,5},{8,10},{9,11},{10,... | collective-permute-start | bytes 135176 | tf_op jit(solution)/shard_map/ppermute | solution.py:456
  167.8 10.3 %collective-permute-start.26 = (f32[8,1408]{1,0:T(8,128)}, f32[8,1408]{1,0:T(8,128)S(1)}, u32[]{:S(2)}, u32[]{:S(2)}) collective-permute-start(f32[8,1408]{1,0:T(8,128)} %get-tuple-element.141.p0), channel_id=1, source_target_pairs={{0,3},{1,2},{2,1},{3,0},{4,7},{5,6},{6,5},{7,4},{8,11},{9,10},{10,... | collective-permute-start | bytes 135176 | tf_op jit(solution)/shard_map/ppermute | solution.py:456
  170.8 4.0 %copy-start.1 = (bf16[2,384,256]{2,1,0:T(8,128)(2,1)}, bf16[2,384,256]{2,1,0:T(8,128)(2,1)S(1)}, u32[]{:S(2)}) copy-start(bf16[2,384,256]{2,1,0:T(8,128)(2,1)S(1)} %add_convert_fusion.own) | copy-start | bytes 1179652
  170.8 7.2 %collective-permute-start.23 = (bf16[384,256]{1,0:T(8,128)(2,1)S(1)}, bf16[384,256]{1,0:T(8,128)(2,1)S(1)}, u32[]{:S(2)}, u32[]{:S(2)}) collective-permute-start(bf16[384,256]{1,0:T(8,128)(2,1)S(1)} %slice_bitcast_fusion), channel_id=1, source_target_pairs={{2,0},{0,2},{3,1},{1,3},{6,4},{4,6},{7,5},{5,7},{10,8},{8,10},{11,... | collective-permute-start | bytes 589832 | tf_op jit(solution)/shard_map/ppermute | solution.py:39
  178.0 5.5 %copy-start.6 = (f32[8,1408]{1,0:T(8,128)}, f32[8,1408]{1,0:T(8,128)S(1)}, u32[]{:S(2)}) copy-start(f32[8,1408]{1,0:T(8,128)S(1)} %collective-permute-done.24.p1) | copy-start | bytes 135172
  178.0 5.5 %copy-start.7 = (f32[8,1408]{1,0:T(8,128)}, f32[8,1408]{1,0:T(8,128)S(1)}, u32[]{:S(2)}) copy-start(f32[8,1408]{1,0:T(8,128)S(1)} %collective-permute-done.25.p2) | copy-start | bytes 135172
  178.1 5.5 %copy-start.8 = (f32[8,1408]{1,0:T(8,128)}, f32[8,1408]{1,0:T(8,128)S(1)}, u32[]{:S(2)}) copy-start(f32[8,1408]{1,0:T(8,128)S(1)} %collective-permute-done.26.p3) | copy-start | bytes 135172
  178.8 17.5 %collective-permute-start.27 = (bf16[64,2048]{1,0:T(8,128)(2,1)S(1)}, bf16[64,2048]{1,0:T(8,128)(2,1)S(1)}, u32[]{:S(2)}, u32[]{:S(2)}) collective-permute-start(bf16[64,2048]{1,0:T(8,128)(2,1)S(1)} %get-tuple-element.160), channel_id=1, source_target_pairs={{0,8},{8,16},{16,24},{24,0},{1,9},{9,17},{17,25},{25,1},{2,10},{10... | collective-permute-start | bytes 786440 | tf_op jit(solution)/shard_map/ppermute | solution.py:50
  180.0 16.3 %collective-permute-start.28 = (bf16[64,2048]{1,0:T(8,128)(2,1)S(1)}, bf16[64,2048]{1,0:T(8,128)(2,1)S(1)}, u32[]{:S(2)}, u32[]{:S(2)}) collective-permute-start(bf16[64,2048]{1,0:T(8,128)(2,1)S(1)} %get-tuple-element.161), channel_id=1, source_target_pairs={{0,16},{8,24},{16,0},{24,8},{1,17},{9,25},{17,1},{25,9},{2,18},{10... | collective-permute-start | bytes 786440 | tf_op jit(solution)/shard_map/ppermute | solution.py:50
  182.4 13.9 %collective-permute-start.29 = (bf16[64,2048]{1,0:T(8,128)(2,1)S(1)}, bf16[64,2048]{1,0:T(8,128)(2,1)S(1)}, u32[]{:S(2)}, u32[]{:S(2)}) collective-permute-start(bf16[64,2048]{1,0:T(8,128)(2,1)S(1)} %get-tuple-element.162), channel_id=1, source_target_pairs={{0,24},{8,0},{16,8},{24,16},{1,25},{9,1},{17,9},{25,17},{2,26},{10... | collective-permute-start | bytes 786440 | tf_op jit(solution)/shard_map/ppermute | solution.py:50
  185.3 40.5 %all-to-all-start.1 = ((bf16[32,32,1152]{2,1,0:T(8,128)(2,1)}), bf16[32,32,1152]{2,1,0:T(8,128)(2,1)}, u32[]{:S(2)}, u32[]{:S(2)}) async-start(bf16[32,32,1152]{2,1,0:T(8,128)(2,1)} %bitcast.44), calls=%async_computation.2 | async-start | bytes 4718592 | tf_op jit(solution)/shard_map/all_to_all | solution.py:596
  196.5 24.6 %collective-permute-start.30 = (bf16[32,2048]{1,0:T(8,128)(2,1)S(1)}, bf16[32,2048]{1,0:T(8,128)(2,1)S(1)}, u32[]{:S(2)}, u32[]{:S(2)}) collective-permute-start(bf16[32,2048]{1,0:T(8,128)(2,1)S(1)} %broadcast_select_fusion.2), channel_id=1, source_target_pairs={{4,0},{0,4},{5,1},{1,5},{6,2},{2,6},{7,3},{3,7},{12,8},{8,12},{13,... | collective-permute-start | bytes 393224 | tf_op jit(solution)/shard_map/ppermute | solution.py:39
  (12 other events, 17.9 us)
Sparse Core Ops, SparseCore 0:
  33.5 71.2 all-gather.1
  131.9 44.7 reduce-scatter.1

commit v3 on v2

--- a/solution.py
+++ b/solution.py
@@ -564,8 +564,8 @@
         [((OWN, D), F32), ((OWN, 128), F32)],
         place, half, far, half_c, far_c, ct, xhat2, rinv2, gains, columns(w0, 3, 256), att, lse,
     )
-    gb, *down = lax.optimization_barrier((gb, *down))
     da_lo, da_hi = dp_turn(da_last, 1), dp_turn(da_first, -1)
+    da_lo, da_hi, *down = lax.optimization_barrier((da_lo, da_hi, *down))
     go, dq, dk, dv = call(
         8,
         attend_back_kernel,

time: 240 us -> 240 us (level)
    reduce_scatter x1, waiting for transfers between devices: 1.87 us -> 5.06 us  [scatter_sum(): return lax.psum_scatter(x, axis, scatter_dimension=0, tiled=True)]
    ppermute x6, waiting for transfers between devices: 2.49 us -> 0.02 us  [mp_turn(): return lax.ppermute(x, ('yl', 'c'), [(i, i ^ slot) for i in range(4)])]
  transfers between devices with their start and end apart: 35 -> 35, of which waited for: 16 -> 15; matrix products, arithmetic and copies ran while one was open for 5% -> 5% of each run, Pallas kernels for 22% -> 22%
where the time goes in v3:
time: 240 us; the launch traced here: 237 us
  waiting for transfers between devices  80.7 us (34%)
  Pallas kernels  63.1 us (26%)
  starting transfers between devices  49.1 us (20%)
  local copies, waits for them, and re-layouts  18 us (8%)
  between operations  14.6 us (6%)
  other arithmetic  11.1 us (5%)
    pallas_call x10, Pallas kernels, call(): pl.pallas_call(body, grid=(1,), out_shape=[jax.ShapeDtypeStruct(s, t) for...  61.4 us
    ppermute x18, waiting for transfers between devices, turn_by(): return lax.ppermute(x, axis, [((i + by) % n, i) for i in range(n)])  52.4 us
    ppermute x18, starting transfers between devices, turn_by(): return lax.ppermute(x, axis, [((i + by) % n, i) for i in range(n)])  17.9 us
    ppermute x4, waiting for transfers between devices, dp_turn(): return lax.ppermute(x, ('z', 'x', 'yh'), pairs)  12.5 us
    all_to_all x1, starting transfers between devices, body(): g0 = sum_of(lax.all_to_all(g0, DP, 0, 0, tiled=True), 32)  8.4 us
    all_to_all x1, waiting for transfers between devices, body(): w0 = lax.all_to_all(spread, ('z', 'x'), 0, 0, tiled=True)  7.54 us
    ppermute x4, starting transfers between devices, dp_turn(): return lax.ppermute(x, ('z', 'x', 'yh'), pairs)  7.45 us
    unnamed x56, local copies, waits for them, and re-layouts  6.76 us
  transfers between devices with their start and end apart: 35, of which 15 were waited for; matrix products, arithmetic and copies ran while one was open for 5% of the time, Pallas kernels for 22%

profile of v3, /device:TPU:1, one launch (start us, length us, event | category | flops | bytes accessed | tf_op | source)
XLA Modules:
  0.0 236.6 jit_solution(6659042762955952881)
XLA Ops:
  7.2 1.1 fusion.6
  14.9 3.8 %collective-permute-start.2 = (bf16[32,3200]{1,0:T(8,128)(2,1)S(1)}, bf16[32,3200]{1,0:T(8,128)(2,1)S(1)}, u32[]{:S(2)}, u32[]{:S(2)}) collective-permute-start(bf16[32,3200]{1,0:T(8,128)(2,1)S(1)} %concatenate.41), channel_id=1, source_target_pairs={{4,0},{0,4},{5,1},{1,5},{6,2},{2,6},{7,3},{3,7},{12,8},{8,12},{13,... | collective-permute-start | bytes 614408 | tf_op jit(solution)/shard_map/ppermute | solution.py:39
  18.8 1.9 collective-permute-start
  20.7 1.3 collective-permute-start.1
  22.0 3.3 %collective-permute-done = bf16[256,256]{1,0:T(8,128)(2,1)S(1)} collective-permute-done((bf16[256,256]{1,0:T(8,128)(2,1)S(1)}, bf16[256,256]{1,0:T(8,128)(2,1)S(1)}, u32[]{:S(2)}, u32[]{:S(2)}) %collective-permute-start) | collective-permute-done | bytes 131104 | tf_op jit(solution)/shard_map/ppermute | solution.py:475
  25.3 7.3 %collective-permute-done.1 = bf16[256,256]{1,0:T(8,128)(2,1)S(1)} collective-permute-done((bf16[256,256]{1,0:T(8,128)(2,1)S(1)}, bf16[256,256]{1,0:T(8,128)(2,1)S(1)}, u32[]{:S(2)}, u32[]{:S(2)}) %collective-permute-start.1) | collective-permute-done | bytes 131104 | tf_op jit(solution)/shard_map/ppermute | solution.py:475
  33.4 1.7 broadcast_in_dim.24
  35.2 6.2 %all-to-all-start = ((bf16[16,64,1152]{2,1,0:T(8,128)(2,1)}), bf16[16,64,1152]{2,1,0:T(8,128)(2,1)}, u32[]{:S(2)}, u32[]{:S(2)}) async-start(bf16[16,64,1152]{2,1,0:T(8,128)(2,1)} %broadcast_in_dim.24), calls=%async_computation | async-start | bytes 4718592 | tf_op jit(solution)/shard_map/all_to_all | solution.py:514
  41.6 1.6 collective-permute-start.3
  43.2 9.6 %collective-permute-done.4.x2 = bf16[896,256]{1,0:T(8,128)(2,1)S(1)} collective-permute-done((bf16[896,256]{1,0:T(8,128)(2,1)S(1)}, bf16[896,256]{1,0:T(8,128)(2,1)S(1)}, u32[]{:S(2)}, u32[]{:S(2)}) %collective-permute-start.4) | collective-permute-done | bytes 458784 | tf_op jit(solution)/shard_map/ppermute | solution.py:39
  52.7 1.7 collective-permute-start.5
  56.7 4.9 %shard_map.126 = (bf16[896,1024]{1,0:T(8,128)(2,1)}, bf16[384,1024]{1,0:T(8,128)(2,1)}, f32[896,128]{1,0:T(8,128)}) custom-call(s32[2]{0:T(128)} %pad_add_fusion.place, bf16[896,256]{1,0:T(8,128)(2,1)} %copy-done.5, bf16[896,256]{1,0:T(8,128)(2,1)} %copy-done.10, bf16[896,256]{1,0:T(8,128)(2,1)} %copy-done.9, bf16[896,256]{1,0:T(8,128)(2,1)} %copy-done.11), custom_call_target="tpu_custom_call" | custom-call | flops 5000000000 | tf_op jit(solution)/shard_map/pallas_call | solution.py:70
  62.4 5.7 %collective-permute-done.7.c2 = bf16[384,256]{1,0:T(8,128)(2,1)S(1)} collective-permute-done((bf16[384,256]{1,0:T(8,128)(2,1)}, bf16[384,256]{1,0:T(8,128)(2,1)S(1)}, u32[]{:S(2)}, u32[]{:S(2)}) %collective-permute-start.7) | collective-permute-done | bytes 196640 | tf_op jit(solution)/shard_map/ppermute | solution.py:39
  69.2 1.7 fusion
  70.9 1.7 pad_maximum_fusion
  72.6 7.5 %all-to-all-done = bf16[16,64,1152]{2,1,0:T(8,128)(2,1)} async-done(((bf16[16,64,1152]{2,1,0:T(8,128)(2,1)}), bf16[16,64,1152]{2,1,0:T(8,128)(2,1)}, u32[]{:S(2)}, u32[]{:S(2)}) %all-to-all-start) | async-done | bytes 2359328 | tf_op jit(solution)/shard_map/all_to_all | solution.py:514
  80.1 9.2 %shard_map.127 = (f32[8,1024]{1,0:T(8,128)}, bf16[384,1024]{1,0:T(8,128)(2,1)}, bf16[896,256]{1,0:T(8,128)(2,1)}, bf16[896,256]{1,0:T(8,128)(2,1)}, bf16[896,256...) custom-call(s32[2]{0:T(128)} %pad_add_fusion.place, ...), custom_call_target="tpu_custom_call" | custom-call | flops 10000000000 | tf_op jit(solution)/shard_map/pallas_call | solution.py:70
  89.3 1.9 collective-permute-start.9
  91.2 1.6 collective-permute-done.9
  94.4 9.9 %collective-permute-done.10.far = bf16[2,384,256]{2,1,0:T(8,128)(2,1)S(1)} collective-permute-done((bf16[2,384,256]{2,1,0:T(8,128)(2,1)S(1)}, bf16[2,384,256]{2,1,0:T(8,128)(2,1)S(1)}, u32[]{:S(2)}, u32[]{:S(2)}) %collective-permute-start.10) | collective-permute-done | bytes 393248 | tf_op jit(solution)/shard_map/ppermute | solution.py:39
  105.5 1.3 collective-permute-done.12.far_c
  107.6 10.7 %shard_map.128 = (bf16[384,1024]{1,0:T(8,128)(2,1)}, f32[384,256]{1,0:T(8,128)}, f32[384,1024]{1,0:T(8,128)}, f32[384,128]{1,0:T(8,128)}, bf16[384,1024]{1,0:T(8...) custom-call(s32[2]{0:T(128)} %pad_add_fusion.place, ...), custom_call_target="tpu_custom_call" | custom-call | flops 10000000000 | tf_op jit(solution)/shard_map/pallas_call | solution.py:70
  118.6 1.6 collective-permute-done.13
  121.4 8.1 %shard_map.129 = (bf16[4,384,256]{2,1,0:T(8,128)(2,1)}, bf16[1024,2048]{1,0:T(8,128)(2,1)}) custom-call(s32[2]{0:T(128)} %pad_add_fusion.place, bf16[384,1024]{1,0:T(8,128)(2,1)} %get-tuple-element.108.normed, bf16[384,768]{1,0:T(8,128)(2,1)} %get-tuple-element.109.act, bf16[384,768]{1,0:T(8,128)(2,1)} %get-tuple-element.110.de0, ...), custom_call_target="tpu_custom_call" | custom-call | flops 8999999488 | tf_op jit(solution)/shard_map/pallas_call | solution.py:70
  129.5 2.3 collective-permute-done.14.far
  131.8 1.3 collective-permute-start.15
  133.8 1.7 collective-permute-start.21
  137.0 5.5 %shard_map.130 = (f32[384,256]{1,0:T(8,128)}, bf16[384,1024]{1,0:T(8,128)(2,1)}, bf16[384,256]{1,0:T(8,128)(2,1)}, bf16[272,256]{1,0:T(8,128)(2,1)}, bf16[272,256]{1,0:T(8,128)(2,1)}) custom-call(s32[2]{0:T(128)} %pad_add_fusion.place, bf16[2,384,256]{2,1,0:T(8,128)(2,1)} %copy-done.3, bf16[2,384,256]{2,1,0:T(8,128)(2,1)} %collective-permute-done.14.far, ...), custom_call_target="tpu_custom_call" | custom-call | flops 6000000000 | tf_op jit(solution)/shard_map/pallas_call | solution.py:70
  142.5 2.7 %collective-permute-start.17 = (bf16[272,256]{1,0:T(8,128)(2,1)}, bf16[272,256]{1,0:T(8,128)(2,1)S(1)}, u32[]{:S(2)}, u32[]{:S(2)}) collective-permute-start(bf16[272,256]{1,0:T(8,128)(2,1)} %get-tuple-element.128), channel_id=1, source_target_pairs={{0,4},{4,8},{8,12},{12,16},{16,20},{20,24},{24,28},{28,32},{32,36}... | collective-permute-start | bytes 417800 | tf_op jit(solution)/shard_map/ppermute | solution.py:475
  145.2 1.5 collective-permute-start.18
  146.8 6.9 %shard_map.131 = (bf16[1024,256]{1,0:T(8,128)(2,1)}, f32[384,256]{1,0:T(8,128)}, f32[384,256]{1,0:T(8,128)}, f32[384,256]{1,0:T(8,128)}) custom-call(s32[2]{0:T(128)} %pad_add_fusion.place, bf16[384,256]{1,0:T(8,128)(2,1)} %get-tuple-element.120.da, f32[384,128]{1,0:T(8,128)} %get-tuple-element.119.lse, bf16[384,1024]{1,0:T(8,128)(2,1)} %get-tuple-element.121.gb, ...), custom_call_target="tpu_custom_call" | custom-call | flops 8000000000 | tf_op jit(solution)/shard_map/pallas_call | solution.py:70
  153.7 2.0 collective-permute-done.18.refs_1_
  156.3 7.4 %shard_map.132 = (bf16[2,384,256]{2,1,0:T(8,128)(2,1)}, bf16[2,384,256]{2,1,0:T(8,128)(2,1)}, f32[8,1408]{1,0:T(8,128)}, f32[384,256]{1,0:T(8,128)}, bf16[384,768]{1,0:T(8,128)(2,1)}) custom-call(s32[2]{0:T(128)} %pad_add_fusion.place, f32[384,256]{1,0:T(8,128)} %get-tuple-element.125.dq, f32[384,256]{1,0:T(8,128)} %get-tuple-element.126.dk, ...), custom_call_target="tpu_custom_call" | custom-call | flops 7000000000 | tf_op jit(solution)/shard_map/pallas_call | solution.py:70
  164.6 1.9 collective-permute-start.26
  167.8 3.9 %shard_map.133.g = bf16[1024,1152]{1,0:T(8,128)(2,1)} custom-call(bf16[384,1024]{1,0:T(8,128)(2,1)} %get-tuple-element.137.normed, bf16[384,768]{1,0:T(8,128)(2,1)} %get-tuple-element.138.raw, bf16[1024,256]{1,0:T(8,128)(2,1)} %get-tuple-element.139.go), custom_call_target="tpu_custom_call" | custom-call | flops 4000000000 | tf_op jit(solution)/shard_map/pallas_call | solution.py:70
  171.7 5.1 %reduce-scatter.2.cloned.1.call-done = bf16[256,2048]{1,0:T(8,128)(2,1)} async-done(((bf16[1024,2048]{1,0:T(8,128)(2,1)}), bf16[256,2048]{1,0:T(8,128)(2,1)}) %reduce-scatter.2.cloned.1.call-update) | async-done | bytes 1048592 | tf_op jit(solution)/shard_map/reduce_scatter | solution.py:55
  176.7 1.3 constant_dynamic-slice_fusion
  178.8 1.2 collective-permute-start.27
  180.0 2.4 %collective-permute-start.28 = (bf16[64,2048]{1,0:T(8,128)(2,1)S(1)}, bf16[64,2048]{1,0:T(8,128)(2,1)S(1)}, u32[]{:S(2)}, u32[]{:S(2)}) collective-permute-start(bf16[64,2048]{1,0:T(8,128)(2,1)S(1)} %get-tuple-element.163), channel_id=1, source_target_pairs={{0,16},{8,24},{16,0},{24,8},{1,17},{9,25},{17,1},{25,9},{2,18},{10... | collective-permute-start | bytes 786440 | tf_op jit(solution)/shard_map/ppermute | solution.py:50
  182.4 1.1 collective-permute-start.29
  183.5 1.8 shard_map.134
  185.3 8.4 %all-to-all-start.1 = ((bf16[32,32,1152]{2,1,0:T(8,128)(2,1)}), bf16[32,32,1152]{2,1,0:T(8,128)(2,1)}, u32[]{:S(2)}, u32[]{:S(2)}) async-start(bf16[32,32,1152]{2,1,0:T(8,128)(2,1)} %bitcast.44), calls=%async_computation.2 | async-start | bytes 4718592 | tf_op jit(solution)/shard_map/all_to_all | solution.py:596
  193.7 2.6 %shard_map.136 = bf16[384,256]{1,0:T(8,128)(2,1)} custom-call(s32[2]{0:T(128)} %pad_add_fusion.place, f32[384,256]{1,0:T(8,128)} %get-tuple-element.156.grad, bf16[2,384,256]{2,1,0:T(8,128)(2,1)} %copy-done.1, bf16[384,256]{1,0:T(8,128)(2,1)} %copy-done.22, f32[8,1408]{1,0:T(8,128)} %get-tuple-element.143.p0, f32[8,1408]{1,0:T(8,128)} %copy-done.6, ...), custom_call_target="tpu_custom_call" | custom-call | flops 2000000000 | tf_op jit(solution)/shard_map/pallas_call | solution.py:70
  196.5 2.7 %collective-permute-start.30 = (bf16[32,2048]{1,0:T(8,128)(2,1)S(1)}, bf16[32,2048]{1,0:T(8,128)(2,1)S(1)}, u32[]{:S(2)}, u32[]{:S(2)}) collective-permute-start(bf16[32,2048]{1,0:T(8,128)(2,1)S(1)} %broadcast_select_fusion.2), channel_id=1, source_target_pairs={{4,0},{0,4},{5,1},{1,5},{6,2},{2,6},{7,3},{3,7},{12,8},{8,12},{13,... | collective-permute-start | bytes 393224 | tf_op jit(solution)/shard_map/ppermute | solution.py:39
  199.2 2.2 shard_map.135
  201.4 19.6 %collective-permute-done.30 = bf16[32,2048]{1,0:T(8,128)(2,1)S(1)} collective-permute-done((bf16[32,2048]{1,0:T(8,128)(2,1)S(1)}, bf16[32,2048]{1,0:T(8,128)(2,1)S(1)}, u32[]{:S(2)}, u32[]{:S(2)}) %collective-permute-start.30) | collective-permute-done | bytes 131104 | tf_op jit(solution)/shard_map/ppermute | solution.py:39
  222.7 3.1 %all-to-all-done.1 = bf16[32,32,1152]{2,1,0:T(8,128)(2,1)} async-done(((bf16[32,32,1152]{2,1,0:T(8,128)(2,1)}), bf16[32,32,1152]{2,1,0:T(8,128)(2,1)}, u32[]{:S(2)}, u32[]{:S(2)}) %all-to-all-start.1) | async-done | bytes 2359328 | tf_op jit(solution)/shard_map/all_to_all | solution.py:596
  225.8 2.0 convert_reduce_fusion
  (140 shorter events, 26.1 us)
Async XLA Ops:
  7.2 26.2 %copy-start = (bf16[384,256]{1,0:T(8,128)(2,1)S(1)}, bf16[384,256]{1,0:T(8,128)(2,1)}, u32[]{:S(2)}) copy-start(bf16[384,256]{1,0:T(8,128)(2,1)} %param.7) | copy-start | bytes 589828
  7.2 99.7 %all-gather.2.cloned.1.call-start = ((), (), s32[]{:S(2)}) async-start(), calls=%async_computation.3 | async-start | bytes 4456448 | tf_op jit(solution)/shard_map/all_gather | solution.py:515
  14.9 17.6 %collective-permute-start.2 = (bf16[32,3200]{1,0:T(8,128)(2,1)S(1)}, bf16[32,3200]{1,0:T(8,128)(2,1)S(1)}, u32[]{:S(2)}, u32[]{:S(2)}) collective-permute-start(bf16[32,3200]{1,0:T(8,128)(2,1)S(1)} %concatenate.41), channel_id=1, source_target_pairs={{4,0},{0,4},{5,1},{1,5},{6,2},{2,6},{7,3},{3,7},{12,8},{8,12},{13,... | collective-permute-start | bytes 614408 | tf_op jit(solution)/shard_map/ppermute | solution.py:39
  18.8 6.6 %collective-permute-start = (bf16[256,256]{1,0:T(8,128)(2,1)S(1)}, bf16[256,256]{1,0:T(8,128)(2,1)S(1)}, u32[]{:S(2)}, u32[]{:S(2)}) collective-permute-start(bf16[256,256]{1,0:T(8,128)(2,1)S(1)} %get-tuple-element.86), channel_id=1, source_target_pairs={{0,4},{4,8},{8,12},{12,16},{16,20},{20,24},{24,28},{28,32},{32,36}... | collective-permute-start | bytes 393224 | tf_op jit(solution)/shard_map/ppermute | solution.py:475
  20.7 11.9 %collective-permute-start.1 = (bf16[256,256]{1,0:T(8,128)(2,1)S(1)}, bf16[256,256]{1,0:T(8,128)(2,1)S(1)}, u32[]{:S(2)}, u32[]{:S(2)}) collective-permute-start(bf16[256,256]{1,0:T(8,128)(2,1)S(1)} %get-tuple-element.87), channel_id=1, source_target_pairs={{4,0},{8,4},{12,8},{16,12},{20,16},{24,20},{28,24},{32,28},{36,32}... | collective-permute-start | bytes 393224 | tf_op jit(solution)/shard_map/ppermute | solution.py:475
  35.2 44.9 %all-to-all-start = ((bf16[16,64,1152]{2,1,0:T(8,128)(2,1)}), bf16[16,64,1152]{2,1,0:T(8,128)(2,1)}, u32[]{:S(2)}, u32[]{:S(2)}) async-start(bf16[16,64,1152]{2,1,0:T(8,128)(2,1)} %broadcast_in_dim.24), calls=%async_computation | async-start | bytes 4718592 | tf_op jit(solution)/shard_map/all_to_all | solution.py:514
  41.4 135.3 %reduce-scatter.2.cloned.1.call-start = ((), (), s32[]{:S(2)}) async-start(), calls=%async_computation.4 | async-start | bytes 5242880 | tf_op jit(solution)/shard_map/reduce_scatter | solution.py:55
  41.5 14.5 %copy-start.5 = (bf16[896,256]{1,0:T(8,128)(2,1)}, bf16[896,256]{1,0:T(8,128)(2,1)S(1)}, u32[]{:S(2)}) copy-start(bf16[896,256]{1,0:T(8,128)(2,1)S(1)} %constant_dynamic-update-slice_fusion.x0) | copy-start | bytes 1376260
  41.5 11.3 %collective-permute-start.4 = (bf16[896,256]{1,0:T(8,128)(2,1)S(1)}, bf16[896,256]{1,0:T(8,128)(2,1)S(1)}, u32[]{:S(2)}, u32[]{:S(2)}) collective-permute-start(bf16[896,256]{1,0:T(8,128)(2,1)S(1)} %constant_dynamic-update-slice_fusion.x0), channel_id=1, source_target_pairs={{2,0},{0,2},{3,1},{1,3},{6,4},{4,6},{7,5},{5,7},{10,8},{8,10},{11,... | collective-permute-start | bytes 1376264 | tf_op jit(solution)/shard_map/ppermute | solution.py:39
  41.6 13.5 %collective-permute-start.3 = (bf16[896,256]{1,0:T(8,128)(2,1)S(1)}, bf16[896,256]{1,0:T(8,128)(2,1)S(1)}, u32[]{:S(2)}, u32[]{:S(2)}) collective-permute-start(bf16[896,256]{1,0:T(8,128)(2,1)S(1)} %constant_dynamic-update-slice_fusion.x0), channel_id=1, source_target_pairs={{1,0},{0,1},{3,2},{2,3},{5,4},{4,5},{7,6},{6,7},{9,8},{8,9},{11,10... | collective-permute-start | bytes 1376264 | tf_op jit(solution)/shard_map/ppermute | solution.py:39
  52.7 3.2 %collective-permute-start.5 = (bf16[896,256]{1,0:T(8,128)(2,1)S(1)}, bf16[896,256]{1,0:T(8,128)(2,1)S(1)}, u32[]{:S(2)}, u32[]{:S(2)}) collective-permute-start(bf16[896,256]{1,0:T(8,128)(2,1)S(1)} %collective-permute-done.4.x2), channel_id=1, source_target_pairs={{1,0},{0,1},{3,2},{2,3},{5,4},{4,5},{7,6},{6,7},{9,8},{8,9},{11,10... | collective-permute-start | bytes 1376264 | tf_op jit(solution)/shard_map/ppermute | solution.py:39
  61.6 6.4 %collective-permute-start.7 = (bf16[384,256]{1,0:T(8,128)(2,1)}, bf16[384,256]{1,0:T(8,128)(2,1)S(1)}, u32[]{:S(2)}, u32[]{:S(2)}) collective-permute-start(bf16[384,256]{1,0:T(8,128)(2,1)} %c0), channel_id=1, source_target_pairs={{2,0},{0,2},{3,1},{1,3},{6,4},{4,6},{7,5},{5,7},{10,8},{8,10},{11,... | collective-permute-start | bytes 589832 | tf_op jit(solution)/shard_map/ppermute | solution.py:39
  61.7 10.8 %collective-permute-start.6 = (bf16[384,256]{1,0:T(8,128)(2,1)}, bf16[384,256]{1,0:T(8,128)(2,1)S(1)}, u32[]{:S(2)}, u32[]{:S(2)}) collective-permute-start(bf16[384,256]{1,0:T(8,128)(2,1)} %c0), channel_id=1, source_target_pairs={{1,0},{0,1},{3,2},{2,3},{5,4},{4,5},{7,6},{6,7},{9,8},{8,9},{11,10... | collective-permute-start | bytes 589832 | tf_op jit(solution)/shard_map/ppermute | solution.py:39
  68.1 21.2 %copy-start.20 = (bf16[384,256]{1,0:T(8,128)(2,1)}, bf16[384,256]{1,0:T(8,128)(2,1)S(1)}, u32[]{:S(2)}) copy-start(bf16[384,256]{1,0:T(8,128)(2,1)S(1)} %collective-permute-done.7.c2) | copy-start | bytes 589828
  68.1 4.5 %collective-permute-start.8 = (bf16[384,256]{1,0:T(8,128)(2,1)S(1)}, bf16[384,256]{1,0:T(8,128)(2,1)}, u32[]{:S(2)}, u32[]{:S(2)}) collective-permute-start(bf16[384,256]{1,0:T(8,128)(2,1)S(1)} %collective-permute-done.7.c2), channel_id=1, source_target_pairs={{1,0},{0,1},{3,2},{2,3},{5,4},{4,5},{7,6},{6,7},{9,8},{8,9},{11,10... | collective-permute-start | bytes 589832 | tf_op jit(solution)/shard_map/ppermute | solution.py:39
  72.6 16.7 %copy-start.21 = (bf16[384,256]{1,0:T(8,128)(2,1)}, bf16[384,256]{1,0:T(8,128)(2,1)S(1)}, u32[]{:S(2)}) copy-start(bf16[384,256]{1,0:T(8,128)(2,1)S(1)} %collective-permute-done.6.c1) | copy-start | bytes 589828
  89.3 3.5 %collective-permute-start.9 = (bf16[2,384,256]{2,1,0:T(8,128)(2,1)}, bf16[2,384,256]{2,1,0:T(8,128)(2,1)S(1)}, u32[]{:S(2)}, u32[]{:S(2)}) collective-permute-start(bf16[2,384,256]{2,1,0:T(8,128)(2,1)} %get-tuple-element.99), channel_id=1, source_target_pairs={{1,0},{0,1},{3,2},{2,3},{5,4},{4,5},{7,6},{6,7},{9,8},{8,9},{11,10... | collective-permute-start | bytes 1179656 | tf_op jit(solution)/shard_map/ppermute | solution.py:39
  93.9 13.0 %copy-start.4 = (bf16[2,384,256]{2,1,0:T(8,128)(2,1)}, bf16[2,384,256]{2,1,0:T(8,128)(2,1)S(1)}, u32[]{:S(2)}) copy-start(bf16[2,384,256]{2,1,0:T(8,128)(2,1)S(1)} %add_convert_fusion.2.half) | copy-start | bytes 1179652
  93.9 10.5 %collective-permute-start.10 = (bf16[2,384,256]{2,1,0:T(8,128)(2,1)S(1)}, bf16[2,384,256]{2,1,0:T(8,128)(2,1)S(1)}, u32[]{:S(2)}, u32[]{:S(2)}) collective-permute-start(bf16[2,384,256]{2,1,0:T(8,128)(2,1)S(1)} %add_convert_fusion.2.half), channel_id=1, source_target_pairs={{2,0},{0,2},{3,1},{1,3},{6,4},{4,6},{7,5},{5,7},{10,8},{8,10},{11,... | collective-permute-start | bytes 1179656 | tf_op jit(solution)/shard_map/ppermute | solution.py:39
  94.0 11.5 %collective-permute-start.11 = (bf16[2,384,256]{2,1,0:T(8,128)(2,1)S(1)}, bf16[2,384,256]{2,1,0:T(8,128)(2,1)S(1)}, u32[]{:S(2)}, u32[]{:S(2)}) collective-permute-start(bf16[2,384,256]{2,1,0:T(8,128)(2,1)S(1)} %add_convert_fusion.2.half), channel_id=1, source_target_pairs={{1,0},{0,1},{3,2},{2,3},{5,4},{4,5},{7,6},{6,7},{9,8},{8,9},{11,10... | collective-permute-start | bytes 1179656 | tf_op jit(solution)/shard_map/ppermute | solution.py:39
  104.4 2.5 %collective-permute-start.12 = (bf16[2,384,256]{2,1,0:T(8,128)(2,1)S(1)}, bf16[2,384,256]{2,1,0:T(8,128)(2,1)S(1)}, u32[]{:S(2)}, u32[]{:S(2)}) collective-permute-start(bf16[2,384,256]{2,1,0:T(8,128)(2,1)S(1)} %collective-permute-done.10.far), channel_id=1, source_target_pairs={{1,0},{0,1},{3,2},{2,3},{5,4},{4,5},{7,6},{6,7},{9,8},{8,9},{11,10... | collective-permute-start | bytes 1179656 | tf_op jit(solution)/shard_map/ppermute | solution.py:39
  118.2 1.9 collective-permute-start.13
  121.3 10.6 %copy-start.3 = (bf16[2,384,256]{2,1,0:T(8,128)(2,1)}, bf16[2,384,256]{2,1,0:T(8,128)(2,1)S(1)}, u32[]{:S(2)}) copy-start(bf16[2,384,256]{2,1,0:T(8,128)(2,1)S(1)} %add_convert_fusion.1.half) | copy-start | bytes 1179652
  121.3 10.5 %collective-permute-start.14 = (bf16[2,384,256]{2,1,0:T(8,128)(2,1)S(1)}, bf16[2,384,256]{2,1,0:T(8,128)(2,1)}, u32[]{:S(2)}, u32[]{:S(2)}) collective-permute-start(bf16[2,384,256]{2,1,0:T(8,128)(2,1)S(1)} %add_convert_fusion.1.half), channel_id=1, source_target_pairs={{2,0},{0,2},{3,1},{1,3},{6,4},{4,6},{7,5},{5,7},{10,8},{8,10},{11,... | collective-permute-start | bytes 1179656 | tf_op jit(solution)/shard_map/ppermute | solution.py:39
  131.8 3.6 %collective-permute-start.15 = (bf16[2,384,256]{2,1,0:T(8,128)(2,1)S(1)}, bf16[2,384,256]{2,1,0:T(8,128)(2,1)S(1)}, u32[]{:S(2)}, u32[]{:S(2)}) collective-permute-start(bf16[2,384,256]{2,1,0:T(8,128)(2,1)S(1)} %add_convert_fusion.1.half), channel_id=1, source_target_pairs={{1,0},{0,1},{3,2},{2,3},{5,4},{4,5},{7,6},{6,7},{9,8},{8,9},{11,10... | collective-permute-start | bytes 1179656 | tf_op jit(solution)/shard_map/ppermute | solution.py:39
  133.1 3.1 %collective-permute-start.16 = (bf16[2,384,256]{2,1,0:T(8,128)(2,1)}, bf16[2,384,256]{2,1,0:T(8,128)(2,1)S(1)}, u32[]{:S(2)}, u32[]{:S(2)}) collective-permute-start(bf16[2,384,256]{2,1,0:T(8,128)(2,1)} %collective-permute-done.14.far), channel_id=1, source_target_pairs={{1,0},{0,1},{3,2},{2,3},{5,4},{4,5},{7,6},{6,7},{9,8},{8,9},{11,10... | collective-permute-start | bytes 1179656 | tf_op jit(solution)/shard_map/ppermute | solution.py:39
  133.3 20.4 %collective-permute-start.19 = (bf16[384,256]{1,0:T(8,128)(2,1)S(1)}, bf16[384,256]{1,0:T(8,128)(2,1)S(1)}, u32[]{:S(2)}, u32[]{:S(2)}) collective-permute-start(bf16[384,256]{1,0:T(8,128)(2,1)S(1)} %get-tuple-element.192), channel_id=1, source_target_pairs={{0,1},{1,0},{2,3},{3,2},{4,5},{5,4},{6,7},{7,6},{8,9},{9,8},{10,11... | collective-permute-start | bytes 589832 | tf_op jit(solution)/shard_map/ppermute | solution.py:456
  133.8 19.9 %collective-permute-start.20 = (bf16[384,256]{1,0:T(8,128)(2,1)S(1)}, bf16[384,256]{1,0:T(8,128)(2,1)S(1)}, u32[]{:S(2)}, u32[]{:S(2)}) collective-permute-start(bf16[384,256]{1,0:T(8,128)(2,1)S(1)} %get-tuple-element.191), channel_id=1, source_target_pairs={{0,2},{1,3},{2,0},{3,1},{4,6},{5,7},{6,4},{7,5},{8,10},{9,11},{10,... | collective-permute-start | bytes 589832 | tf_op jit(solution)/shard_map/ppermute | solution.py:456
  133.8 19.9 %collective-permute-start.21 = (bf16[384,256]{1,0:T(8,128)(2,1)S(1)}, bf16[384,256]{1,0:T(8,128)(2,1)S(1)}, u32[]{:S(2)}, u32[]{:S(2)}) collective-permute-start(bf16[384,256]{1,0:T(8,128)(2,1)S(1)} %get-tuple-element.190), channel_id=1, source_target_pairs={{0,3},{1,2},{2,1},{3,0},{4,7},{5,6},{6,5},{7,4},{8,11},{9,10},{10,... | collective-permute-start | bytes 589832 | tf_op jit(solution)/shard_map/ppermute | solution.py:456
  142.5 11.2 %collective-permute-start.17 = (bf16[272,256]{1,0:T(8,128)(2,1)}, bf16[272,256]{1,0:T(8,128)(2,1)S(1)}, u32[]{:S(2)}, u32[]{:S(2)}) collective-permute-start(bf16[272,256]{1,0:T(8,128)(2,1)} %get-tuple-element.128), channel_id=1, source_target_pairs={{0,4},{4,8},{8,12},{12,16},{16,20},{20,24},{24,28},{28,32},{32,36}... | collective-permute-start | bytes 417800 | tf_op jit(solution)/shard_map/ppermute | solution.py:475
  145.2 10.4 %collective-permute-start.18 = (bf16[272,256]{1,0:T(8,128)(2,1)}, bf16[272,256]{1,0:T(8,128)(2,1)S(1)}, u32[]{:S(2)}, u32[]{:S(2)}) collective-permute-start(bf16[272,256]{1,0:T(8,128)(2,1)} %get-tuple-element.129), channel_id=1, source_target_pairs={{4,0},{8,4},{12,8},{16,12},{20,16},{24,20},{28,24},{32,28},{36,32}... | collective-permute-start | bytes 417800 | tf_op jit(solution)/shard_map/ppermute | solution.py:475
  153.6 10.1 %copy-start.17 = (bf16[384,256]{1,0:T(8,128)(2,1)}, bf16[384,256]{1,0:T(8,128)(2,1)S(1)}, u32[]{:S(2)}) copy-start(bf16[384,256]{1,0:T(8,128)(2,1)S(1)} %collective-permute-done.19.a) | copy-start | bytes 589828
  153.6 10.1 %copy-start.18 = (bf16[384,256]{1,0:T(8,128)(2,1)}, bf16[384,256]{1,0:T(8,128)(2,1)S(1)}, u32[]{:S(2)}) copy-start(bf16[384,256]{1,0:T(8,128)(2,1)S(1)} %collective-permute-done.20.b) | copy-start | bytes 589828
  153.7 10.1 %copy-start.19 = (bf16[384,256]{1,0:T(8,128)(2,1)}, bf16[384,256]{1,0:T(8,128)(2,1)S(1)}, u32[]{:S(2)}) copy-start(bf16[384,256]{1,0:T(8,128)(2,1)S(1)} %collective-permute-done.21.c) | copy-start | bytes 589828
  163.8 2.7 %collective-permute-start.22 = (bf16[2,384,256]{2,1,0:T(8,128)(2,1)}, bf16[2,384,256]{2,1,0:T(8,128)(2,1)S(1)}, u32[]{:S(2)}, u32[]{:S(2)}) collective-permute-start(bf16[2,384,256]{2,1,0:T(8,128)(2,1)} %get-tuple-element.135), channel_id=1, source_target_pairs={{1,0},{0,1},{3,2},{2,3},{5,4},{4,5},{7,6},{6,7},{9,8},{8,9},{11,10... | collective-permute-start | bytes 1179656 | tf_op jit(solution)/shard_map/ppermute | solution.py:39
  164.3 13.7 %collective-permute-start.24 = (f32[8,1408]{1,0:T(8,128)}, f32[8,1408]{1,0:T(8,128)S(1)}, u32[]{:S(2)}, u32[]{:S(2)}) collective-permute-start(f32[8,1408]{1,0:T(8,128)} %get-tuple-element.143.p0), channel_id=1, source_target_pairs={{0,1},{1,0},{2,3},{3,2},{4,5},{5,4},{6,7},{7,6},{8,9},{9,8},{10,11... | collective-permute-start | bytes 135176 | tf_op jit(solution)/shard_map/ppermute | solution.py:456
  164.4 13.6 %collective-permute-start.25 = (f32[8,1408]{1,0:T(8,128)}, f32[8,1408]{1,0:T(8,128)S(1)}, u32[]{:S(2)}, u32[]{:S(2)}) collective-permute-start(f32[8,1408]{1,0:T(8,128)} %get-tuple-element.143.p0), channel_id=1, source_target_pairs={{0,2},{1,3},{2,0},{3,1},{4,6},{5,7},{6,4},{7,5},{8,10},{9,11},{10,... | collective-permute-start | bytes 135176 | tf_op jit(solution)/shard_map/ppermute | solution.py:456
  164.6 13.5 %collective-permute-start.26 = (f32[8,1408]{1,0:T(8,128)}, f32[8,1408]{1,0:T(8,128)S(1)}, u32[]{:S(2)}, u32[]{:S(2)}) collective-permute-start(f32[8,1408]{1,0:T(8,128)} %get-tuple-element.143.p0), channel_id=1, source_target_pairs={{0,3},{1,2},{2,1},{3,0},{4,7},{5,6},{6,5},{7,4},{8,11},{9,10},{10,... | collective-permute-start | bytes 135176 | tf_op jit(solution)/shard_map/ppermute | solution.py:456
  167.5 4.1 %copy-start.1 = (bf16[2,384,256]{2,1,0:T(8,128)(2,1)}, bf16[2,384,256]{2,1,0:T(8,128)(2,1)S(1)}, u32[]{:S(2)}) copy-start(bf16[2,384,256]{2,1,0:T(8,128)(2,1)S(1)} %add_convert_fusion.own) | copy-start | bytes 1179652
  167.6 10.5 %collective-permute-start.23 = (bf16[384,256]{1,0:T(8,128)(2,1)S(1)}, bf16[384,256]{1,0:T(8,128)(2,1)S(1)}, u32[]{:S(2)}, u32[]{:S(2)}) collective-permute-start(bf16[384,256]{1,0:T(8,128)(2,1)S(1)} %slice_bitcast_fusion), channel_id=1, source_target_pairs={{2,0},{0,2},{3,1},{1,3},{6,4},{4,6},{7,5},{5,7},{10,8},{8,10},{11,... | collective-permute-start | bytes 589832 | tf_op jit(solution)/shard_map/ppermute | solution.py:39
  178.0 5.5 %copy-start.6 = (f32[8,1408]{1,0:T(8,128)}, f32[8,1408]{1,0:T(8,128)S(1)}, u32[]{:S(2)}) copy-start(f32[8,1408]{1,0:T(8,128)S(1)} %collective-permute-done.24.p1) | copy-start | bytes 135172
  178.0 5.5 %copy-start.7 = (f32[8,1408]{1,0:T(8,128)}, f32[8,1408]{1,0:T(8,128)S(1)}, u32[]{:S(2)}) copy-start(f32[8,1408]{1,0:T(8,128)S(1)} %collective-permute-done.25.p2) | copy-start | bytes 135172
  178.1 5.5 %copy-start.8 = (f32[8,1408]{1,0:T(8,128)}, f32[8,1408]{1,0:T(8,128)S(1)}, u32[]{:S(2)}) copy-start(f32[8,1408]{1,0:T(8,128)S(1)} %collective-permute-done.26.p3) | copy-start | bytes 135172
  178.8 17.5 %collective-permute-start.27 = (bf16[64,2048]{1,0:T(8,128)(2,1)S(1)}, bf16[64,2048]{1,0:T(8,128)(2,1)S(1)}, u32[]{:S(2)}, u32[]{:S(2)}) collective-permute-start(bf16[64,2048]{1,0:T(8,128)(2,1)S(1)} %get-tuple-element.162), channel_id=1, source_target_pairs={{0,8},{8,16},{16,24},{24,0},{1,9},{9,17},{17,25},{25,1},{2,10},{10... | collective-permute-start | bytes 786440 | tf_op jit(solution)/shard_map/ppermute | solution.py:50
  180.0 16.3 %collective-permute-start.28 = (bf16[64,2048]{1,0:T(8,128)(2,1)S(1)}, bf16[64,2048]{1,0:T(8,128)(2,1)S(1)}, u32[]{:S(2)}, u32[]{:S(2)}) collective-permute-start(bf16[64,2048]{1,0:T(8,128)(2,1)S(1)} %get-tuple-element.163), channel_id=1, source_target_pairs={{0,16},{8,24},{16,0},{24,8},{1,17},{9,25},{17,1},{25,9},{2,18},{10... | collective-permute-start | bytes 786440 | tf_op jit(solution)/shard_map/ppermute | solution.py:50
  182.4 13.9 %collective-permute-start.29 = (bf16[64,2048]{1,0:T(8,128)(2,1)S(1)}, bf16[64,2048]{1,0:T(8,128)(2,1)S(1)}, u32[]{:S(2)}, u32[]{:S(2)}) collective-permute-start(bf16[64,2048]{1,0:T(8,128)(2,1)S(1)} %get-tuple-element.164), channel_id=1, source_target_pairs={{0,24},{8,0},{16,8},{24,16},{1,25},{9,1},{17,9},{25,17},{2,26},{10... | collective-permute-start | bytes 786440 | tf_op jit(solution)/shard_map/ppermute | solution.py:50
  185.3 40.5 %all-to-all-start.1 = ((bf16[32,32,1152]{2,1,0:T(8,128)(2,1)}), bf16[32,32,1152]{2,1,0:T(8,128)(2,1)}, u32[]{:S(2)}, u32[]{:S(2)}) async-start(bf16[32,32,1152]{2,1,0:T(8,128)(2,1)} %bitcast.44), calls=%async_computation.2 | async-start | bytes 4718592 | tf_op jit(solution)/shard_map/all_to_all | solution.py:596
  196.5 24.6 %collective-permute-start.30 = (bf16[32,2048]{1,0:T(8,128)(2,1)S(1)}, bf16[32,2048]{1,0:T(8,128)(2,1)S(1)}, u32[]{:S(2)}, u32[]{:S(2)}) collective-permute-start(bf16[32,2048]{1,0:T(8,128)(2,1)S(1)} %broadcast_select_fusion.2), channel_id=1, source_target_pairs={{4,0},{0,4},{5,1},{1,5},{6,2},{2,6},{7,3},{3,7},{12,8},{8,12},{13,... | collective-permute-start | bytes 393224 | tf_op jit(solution)/shard_map/ppermute | solution.py:39
  (12 other events, 17.9 us)
Sparse Core Ops, SparseCore 0:
  33.5 71.2 all-gather.1
  131.9 44.7 reduce-scatter.1
